TPU v7x, 32 devices: a whole 2x2x4 slice. The times are simulated.
32 devices in a mesh: shard: 8 (over z, y), replica: 4 (over x, core).
Axes of the slice: x: 2, y: 2, z: 4, core: 2. Of those that a mesh axis runs over, the one named last changes fastest.
Arguments:
- tokens: bfloat16 [4096, 2304], P(('shard', 'replica')), may hold values from -6 to 6
- attn_gain: bfloat16 [2304], P('shard'), may hold values from 0.5 to 1.5
- w_query: bfloat16 [2304, 2304], P('shard'), may hold values from -0.125 to 0.125
- w_key: bfloat16 [2304, 2304], P('shard'), may hold values from -0.125 to 0.125
- w_value: bfloat16 [2304, 2304], P('shard'), may hold values from -0.125 to 0.125
- w_out: bfloat16 [2304, 2304], P('shard'), may hold values from -3 to 3
- ffn_gain: bfloat16 [2304], P('shard'), may hold values from 0.5 to 1.5
- w_gate: bfloat16 [2304, 5760], P('shard'), may hold values from -0.125 to 0.125
- w_up: bfloat16 [2304, 5760], P('shard'), may hold values from -0.125 to 0.125
- w_down: bfloat16 [5760, 2304], P('shard'), may hold values from -0.3125 to 0.3125
- seq_ids: int32 [4096], P('shard'), may hold values from 0 to 15, as said below
- block_ids: int32 [4096], P('shard'), may hold values from 0 to 4095, as said below
- cotangent: bfloat16 [4096, 2304], P(('shard', 'replica')), may hold values from -6 to 6
Outputs:
- result: bfloat16 [4096, 2304], P(('shard', 'replica'))
- grad_tokens: bfloat16 [4096, 2304], P(('shard', 'replica'))
- grad_attn_gain: float32 [2304], P('shard')
- grad_query: float32 [2304, 2304], P('shard')
- grad_key: float32 [2304, 2304], P('shard')
- grad_value: float32 [2304, 2304], P('shard')
- grad_out: float32 [2304, 2304], P('shard')
- grad_ffn_gain: float32 [2304], P('shard')
- grad_gate: float32 [2304, 5760], P('shard')
- grad_up: float32 [2304, 5760], P('shard')
- grad_down: float32 [5760, 2304], P('shard')
Inputs may be any that keep to these rules, and one draw needn't show every extreme that they name: `seq_ids`: within each aligned block of 512 tokens held by one index of shard lie two whole documents with ids rising by one: the first begins at the run's first token and ends inside the run's last 128 tokens, the second fills the rest; no id is shared by two runs. `block_ids`: block ids never fall along the tokens and are equal exactly within one block; a block lies in one document, a new block begins at every document's first token, and no block holds more than 256 tokens.
All inputs are finite; a program needn't handle non-finite values.
Results may differ from a plain program's by a relative error of at most 0.022.
Values may be sent and summed in bfloat16 or wider, within the bound.
A program may use at most 512 MiB of HBM per device.

v0:
```python
import math

import jax
import jax.numpy as jnp
from jax import lax
from jax.sharding import PartitionSpec as P

H = 36


branch_scale = 1.4 / math.sqrt(40.0)
norm_eps = 1e-05
rope_base = 10000.0
masked_score = -1e30


def product(left_side, right_side):
    return jnp.dot(left_side, right_side, preferred_element_type=jnp.float32)


def against(left_side, right_side):
    return lax.dot_general(
        left_side, right_side, (((1,), (1,)), ((), ())), preferred_element_type=jnp.float32
    )


def rms_norm(values, gain_vec):
    factor = lax.rsqrt(jnp.mean(values * values, axis=-1, keepdims=True) + norm_eps)
    return (factor, (values * factor * gain_vec.astype(jnp.float32)).astype(jnp.bfloat16))


def norm_back(values, factor, gain_vec, upstream):
    scaled = upstream * gain_vec.astype(jnp.float32)
    inner_mean = jnp.mean(scaled * values, axis=-1, keepdims=True)
    return (
        factor * scaled - values * (factor * factor * factor) * inner_mean,
        jnp.sum(upstream * values * factor, axis=0),
    )


def angle_tables(places, head_dim):
    halves = head_dim // 2
    frequency = jnp.exp(
        jnp.arange(halves).astype(jnp.float32) * (-2.0 * math.log(rope_base) / head_dim)
    )
    angles = places.astype(jnp.float32)[:, None] * frequency[None, :]
    return (jnp.cos(angles)[:, None, :], jnp.sin(angles)[:, None, :])


def rotate(values, cosine, sine_table):
    halves = values.shape[-1] // 2
    former = values[..., :halves]
    latter = values[..., halves:]
    return jnp.concatenate(
        [former * cosine - latter * sine_table, latter * cosine + former * sine_table], axis=-1
    )


def attn_params(attn_gain, w_query, w_key, w_value, w_out):
    return (
        lax.all_gather(attn_gain, "shard", axis=0, tiled=True),
        lax.all_gather(w_query, "shard", axis=0, tiled=True),
        lax.all_gather(w_key, "shard", axis=0, tiled=True),
        lax.all_gather(w_value, "shard", axis=0, tiled=True),
        lax.all_gather(w_out, "shard", axis=0, tiled=True),
    )


def ffn_params(ffn_gain, w_gate, w_up, w_down):
    return (
        lax.all_gather(ffn_gain, "shard", axis=0, tiled=True),
        lax.all_gather(w_gate, "shard", axis=0, tiled=True),
        lax.all_gather(w_up, "shard", axis=0, tiled=True),
        lax.all_gather(w_down, "shard", axis=0, tiled=True),
    )


def forward(inputs, attn_set, ffn_set, cosine, sine_table, allowed, head_count):
    gain_one, query_w, key_w, value_w, out_w = attn_set
    gain_two, gate_w, up_w, down_w = ffn_set
    row_count, model_width = inputs.shape
    head_dim = model_width // head_count
    factor_one, normed = rms_norm(inputs, gain_one)
    queries = rotate(
        product(normed, query_w).reshape(row_count, head_count, head_dim), cosine, sine_table
    ).astype(jnp.bfloat16)
    key_local = rotate(
        product(normed, key_w).reshape(row_count, head_count, head_dim), cosine, sine_table
    ).astype(jnp.bfloat16)
    value_local = (
        product(normed, value_w).astype(jnp.bfloat16).reshape(row_count, head_count, head_dim)
    )
    key_rows, value_rows = (
        lax.all_gather(key_local, "replica", axis=0, tiled=True),
        lax.all_gather(value_local, "replica", axis=0, tiled=True),
    )
    score_scale = 1.0 / math.sqrt(head_dim)
    scores = (
        jnp.einsum("thd,khd->htk", queries, key_rows, preferred_element_type=jnp.float32)
        * score_scale
    )
    scores = jnp.where(allowed[None], scores, masked_score)
    softmax_probs = jax.nn.softmax(scores, axis=-1)
    probs_low = softmax_probs.astype(jnp.bfloat16)
    attn_mixed = (
        jnp.einsum("htk,khd->thd", probs_low, value_rows, preferred_element_type=jnp.float32)
        .reshape(row_count, model_width)
        .astype(jnp.bfloat16)
    )
    after_attn = inputs + branch_scale * product(attn_mixed, out_w)
    factor_two, normed_two = rms_norm(after_attn, gain_two)
    gate_pre = product(normed_two, gate_w)
    up_proj = product(normed_two, up_w)
    hidden = (jax.nn.silu(gate_pre) * up_proj).astype(jnp.bfloat16)
    result = after_attn + branch_scale * product(hidden, down_w)
    stored = (
        factor_one,
        normed,
        queries,
        key_rows,
        value_rows,
        softmax_probs,
        probs_low,
        attn_mixed,
        after_attn,
        factor_two,
        normed_two,
        gate_pre,
        up_proj,
        hidden,
    )
    return (result, stored)


def shard_rows(left_side, right_side):
    return lax.psum_scatter(
        lax.dot_general(
            left_side, right_side, (((0,), (0,)), ((), ())), preferred_element_type=jnp.float32
        ).astype(jnp.bfloat16),
        "shard",
        scatter_dimension=0,
        tiled=True,
    ).astype(jnp.float32)


def body(
    tokens,
    attn_gain,
    w_query,
    w_key,
    w_value,
    w_out,
    ffn_gain,
    w_gate,
    w_up,
    w_down,
    seq_ids,
    block_ids,
    cotangent,
):
    row_count, model_width = tokens.shape
    head_count = H
    head_dim = model_width // head_count
    replica_at = lax.axis_index("replica")
    own_seq = lax.dynamic_slice_in_dim(seq_ids, replica_at * row_count, row_count)
    own_block = lax.dynamic_slice_in_dim(block_ids, replica_at * row_count, row_count)
    earlier = jnp.sum((seq_ids[None, :] < own_seq[:, None]).astype(jnp.int32), axis=1)
    places = replica_at * row_count + jnp.arange(row_count, dtype=jnp.int32) - earlier
    cosine, sine_table = angle_tables(places, head_dim)
    allowed = (seq_ids[None, :] == own_seq[:, None]) & (block_ids[None, :] <= own_block[:, None])
    inputs = tokens.astype(jnp.float32)
    attn_set = attn_params(attn_gain, w_query, w_key, w_value, w_out)
    ffn_set = ffn_params(ffn_gain, w_gate, w_up, w_down)
    result, stored = forward(inputs, attn_set, ffn_set, cosine, sine_table, allowed, head_count)
    attn_set = attn_params(attn_gain, w_query, w_key, w_value, w_out)
    ffn_set = ffn_params(ffn_gain, w_gate, w_up, w_down)
    redone, stored = forward(inputs, attn_set, ffn_set, cosine, sine_table, allowed, head_count)
    (
        factor_one,
        normed,
        queries,
        key_rows,
        value_rows,
        softmax_probs,
        probs_low,
        attn_mixed,
        after_attn,
        factor_two,
        normed_two,
        gate_pre,
        up_proj,
        hidden,
    ) = stored
    gain_one, query_w, key_w, value_w, out_w = attn_set
    gain_two, gate_w, up_w, down_w = ffn_set
    upstream = cotangent.astype(jnp.float32)
    d_down = (branch_scale * upstream).astype(jnp.bfloat16)
    d_hidden = against(d_down, down_w)
    sigmoid_gate = jax.nn.sigmoid(gate_pre)
    d_gate = (d_hidden * up_proj * sigmoid_gate * (1.0 + gate_pre * (1.0 - sigmoid_gate))).astype(
        jnp.bfloat16
    )
    d_up = (d_hidden * gate_pre * sigmoid_gate).astype(jnp.bfloat16)
    d_normed_two = against(d_gate, gate_w) + against(d_up, up_w)
    d_norm_two, gain_two_part = norm_back(after_attn, factor_two, gain_two, d_normed_two)
    d_after = upstream + d_norm_two
    d_proj = (branch_scale * d_after).astype(jnp.bfloat16)
    d_mixed = against(d_proj, out_w).astype(jnp.bfloat16).reshape(row_count, head_count, head_dim)
    score_scale = 1.0 / math.sqrt(head_dim)
    d_probs = jnp.einsum("thd,khd->htk", d_mixed, value_rows, preferred_element_type=jnp.float32)
    d_scores = (
        softmax_probs * (d_probs - jnp.sum(d_probs * softmax_probs, axis=-1, keepdims=True))
    ).astype(jnp.bfloat16)
    d_queries = (
        jnp.einsum("htk,khd->thd", d_scores, key_rows, preferred_element_type=jnp.float32)
        * score_scale
    )
    amount = row_count * lax.axis_size("replica")
    d_key_part = (
        jnp.einsum("htk,thd->khd", d_scores, queries, preferred_element_type=jnp.float32)
        * score_scale
    )
    d_value_part = jnp.einsum(
        "htk,thd->khd", probs_low, d_mixed, preferred_element_type=jnp.float32
    )
    key_sums = lax.psum_scatter(
        jnp.concatenate(
            [d_key_part.reshape(amount, model_width), d_value_part.reshape(amount, model_width)],
            axis=1,
        ).astype(jnp.bfloat16),
        "replica",
        scatter_dimension=0,
        tiled=True,
    ).astype(jnp.float32)
    d_query_raw = (
        rotate(d_queries, cosine, -sine_table).reshape(row_count, model_width).astype(jnp.bfloat16)
    )
    d_key_raw = (
        rotate(
            key_sums[:, :model_width].reshape(row_count, head_count, head_dim), cosine, -sine_table
        )
        .reshape(row_count, model_width)
        .astype(jnp.bfloat16)
    )
    d_value_raw = key_sums[:, model_width:].astype(jnp.bfloat16)
    d_normed = (
        against(d_query_raw, query_w) + against(d_key_raw, key_w) + against(d_value_raw, value_w)
    )
    d_norm_one, gain_one_part = norm_back(inputs, factor_one, gain_one, d_normed)
    grad_tokens = (d_after + d_norm_one).astype(jnp.bfloat16)
    grad_pairs = (
        (normed, d_query_raw),
        (normed, d_key_raw),
        (normed, d_value_raw),
        (attn_mixed, d_proj),
        (normed_two, d_gate),
        (normed_two, d_up),
        (hidden, d_down),
    )
    row_sums = [shard_rows(left_side, right_side) for left_side, right_side in grad_pairs]
    gain_sums = (
        lax.psum_scatter(gain_one_part, "shard", scatter_dimension=0, tiled=True),
        lax.psum_scatter(gain_two_part, "shard", scatter_dimension=0, tiled=True),
    )
    summed = (
        lax.psum(gain_sums[0].astype(jnp.bfloat16), "replica").astype(jnp.float32),
        lax.psum(row_sums[0].astype(jnp.bfloat16), "replica").astype(jnp.float32),
        lax.psum(row_sums[1].astype(jnp.bfloat16), "replica").astype(jnp.float32),
        lax.psum(row_sums[2].astype(jnp.bfloat16), "replica").astype(jnp.float32),
        lax.psum(row_sums[3].astype(jnp.bfloat16), "replica").astype(jnp.float32),
        lax.psum(gain_sums[1].astype(jnp.bfloat16), "replica").astype(jnp.float32),
        lax.psum(row_sums[4].astype(jnp.bfloat16), "replica").astype(jnp.float32),
        lax.psum(row_sums[5].astype(jnp.bfloat16), "replica").astype(jnp.float32),
        lax.psum(row_sums[6].astype(jnp.bfloat16), "replica").astype(jnp.float32),
    )
    return (
        result.astype(jnp.bfloat16),
        grad_tokens,
        summed[0],
        summed[1],
        summed[2],
        summed[3],
        summed[4],
        summed[5],
        summed[6],
        summed[7],
        summed[8],
    )


def solution(mesh):
    in_specs = (
        P(("shard", "replica"), None),
        P("shard"),
        P("shard", None),
        P("shard", None),
        P("shard", None),
        P("shard", None),
        P("shard"),
        P("shard", None),
        P("shard", None),
        P("shard", None),
        P("shard"),
        P("shard"),
        P(("shard", "replica"), None),
    )
    out_specs = (
        P(("shard", "replica"), None),
        P(("shard", "replica"), None),
        P("shard"),
        P("shard", None),
        P("shard", None),
        P("shard", None),
        P("shard", None),
        P("shard"),
        P("shard", None),
        P("shard", None),
        P("shard", None),
    )
    return jax.shard_map(body, mesh=mesh, in_specs=in_specs, out_specs=out_specs, check_vma=False)
```

profile of v0, /device:TPU:9, one launch (start us, length us, event | category | flops | bytes accessed | tf_op | source)
XLA Modules:
  0.0 4630.8 jit_solution(29973728917010236)
XLA Ops:
  11.3 29.0 all-reduce.5
  42.2 119.8 %all-gather.14.cloned.1.call-done = bf16[2304,2304]{1,0:T(8,128)(2,1)} async-done(((bf16[288,2304]{1,0:T(8,128)(2,1)}), bf16[2304,2304]{1,0:T(8,128)(2,1)}) %all-gather.14.cloned.1.call-update) | async-done | bytes 10616848 | tf_op jit(solution)/shard_map/all_gather | solution.py:62
  161.9 7.0 fusion.55
  168.9 145.9 %all-gather.16.cloned.1.call-done = bf16[2304,2304]{1,0:T(8,128)(2,1)} async-done(((bf16[288,2304]{1,0:T(8,128)(2,1)}), bf16[2304,2304]{1,0:T(8,128)(2,1)}) %all-gather.16.cloned.1.call-update) | async-done | bytes 10616848 | tf_op jit(solution)/shard_map/all_gather | solution.py:63
  314.8 7.0 fusion.53
  323.2 144.4 %all-gather.10.cloned.1.call-done = bf16[2304,2304]{1,0:T(8,128)(2,1)} async-done(((bf16[288,2304]{1,0:T(8,128)(2,1)}), bf16[2304,2304]{1,0:T(8,128)(2,1)}) %all-gather.10.cloned.1.call-update) | async-done | bytes 10616848 | tf_op jit(solution)/shard_map/all_gather | solution.py:64
  467.6 5.6 convolution_convert_fusion.8
  478.2 16.6 all-gather.18.cloned.1.call-done
  494.9 8.6 fusion.59
  503.5 17.7 all-gather.12.cloned.1.call-done
  521.2 6.2 fusion.16
  527.5 145.6 %all-gather.20.cloned.1.call-done = bf16[2304,2304]{1,0:T(8,128)(2,1)} async-done(((bf16[288,2304]{1,0:T(8,128)(2,1)}), bf16[2304,2304]{1,0:T(8,128)(2,1)}) %all-gather.20.cloned.1.call-update) | async-done | bytes 10616848 | tf_op jit(solution)/shard_map/all_gather | solution.py:65
  673.1 5.8 multiply_reduce_fusion.3
  679.6 501.9 %all-gather.24.cloned.1.call-done = bf16[2304,5760]{1,0:T(8,128)(2,1)} async-done(((bf16[288,5760]{1,0:T(8,128)(2,1)}), bf16[2304,5760]{1,0:T(8,128)(2,1)}) %all-gather.24.cloned.1.call-update) | async-done | bytes 26542096 | tf_op jit(solution)/shard_map/all_gather | solution.py:73
  1181.5 14.0 fusion.61
  1195.5 493.8 %all-gather.22.cloned.1.call-done = bf16[2304,5760]{1,0:T(8,128)(2,1)} async-done(((bf16[288,5760]{1,0:T(8,128)(2,1)}), bf16[2304,5760]{1,0:T(8,128)(2,1)}) %all-gather.22.cloned.1.call-update) | async-done | bytes 26542096 | tf_op jit(solution)/shard_map/all_gather | solution.py:72
  1689.3 14.5 fusion.60
  1703.8 493.3 %all-gather.26.cloned.1.call-done = bf16[5760,2304]{1,0:T(8,128)(2,1)} async-done(((bf16[720,2304]{1,0:T(8,128)(2,1)}), bf16[5760,2304]{1,0:T(8,128)(2,1)}) %all-gather.26.cloned.1.call-update) | async-done | bytes 26542096 | tf_op jit(solution)/shard_map/all_gather | solution.py:74
  2197.1 16.1 multiply_convert_fusion.2
  2213.2 12.9 fusion.62
  2226.1 14.5 multiply_reduce_fusion.1
  2243.1 8.8 convolution_convert_fusion.7
  2254.1 4.9 fusion.12
  2270.6 6.6 copy.41
  2278.3 5.8 convolution_convert_fusion.3
  2284.2 40.8 reduce-scatter.25.cloned.1.call-done
  2325.0 6.7 convolution_convert_fusion.4
  2331.8 4.8 fusion.15
  2340.1 5.7 convolution_convert_fusion.5
  2345.9 5.9 convolution_convert_fusion.6
  2353.3 12.0 convolution_convert_fusion.2
  2366.7 12.9 convolution_convert_fusion
  2381.0 12.4 convolution_convert_fusion.1
  2393.7 113.7 %reduce-scatter.17.cloned.1.call-done = bf16[288,2304]{1,0:T(8,128)(2,1)} async-done(((bf16[2304,2304]{1,0:T(8,128)(2,1)}), bf16[288,2304]{1,0:T(8,128)(2,1)}) %reduce-scatter.17.cloned.1.call-update) | async-done | bytes 1327120 | tf_op jit(solution)/shard_map/reduce_scatter | solution.py:136
  2507.4 182.4 %reduce-scatter.15.cloned.1.call-done = bf16[288,2304]{1,0:T(8,128)(2,1)} async-done(((bf16[2304,2304]{1,0:T(8,128)(2,1)}), bf16[288,2304]{1,0:T(8,128)(2,1)}) %reduce-scatter.15.cloned.1.call-update) | async-done | bytes 1327120 | tf_op jit(solution)/shard_map/reduce_scatter | solution.py:136
  2689.8 183.1 %reduce-scatter.13.cloned.1.call-done = bf16[288,2304]{1,0:T(8,128)(2,1)} async-done(((bf16[2304,2304]{1,0:T(8,128)(2,1)}), bf16[288,2304]{1,0:T(8,128)(2,1)}) %reduce-scatter.13.cloned.1.call-update) | async-done | bytes 1327120 | tf_op jit(solution)/shard_map/reduce_scatter | solution.py:136
  2872.9 182.4 %reduce-scatter.11.cloned.1.call-done = bf16[288,2304]{1,0:T(8,128)(2,1)} async-done(((bf16[2304,2304]{1,0:T(8,128)(2,1)}), bf16[288,2304]{1,0:T(8,128)(2,1)}) %reduce-scatter.11.cloned.1.call-update) | async-done | bytes 1327120 | tf_op jit(solution)/shard_map/reduce_scatter | solution.py:136
  3055.3 426.0 %reduce-scatter.23.cloned.1.call-done = bf16[720,2304]{1,0:T(8,128)(2,1)} async-done(((bf16[5760,2304]{1,0:T(8,128)(2,1)}), bf16[720,2304]{1,0:T(8,128)(2,1)}) %reduce-scatter.23.cloned.1.call-update) | async-done | bytes 3317776 | tf_op jit(solution)/shard_map/reduce_scatter | solution.py:136
  3481.2 426.1 %reduce-scatter.21.cloned.1.call-done = bf16[288,5760]{1,0:T(8,128)(2,1)} async-done(((bf16[2304,5760]{1,0:T(8,128)(2,1)}), bf16[288,5760]{1,0:T(8,128)(2,1)}) %reduce-scatter.21.cloned.1.call-update) | async-done | bytes 3317776 | tf_op jit(solution)/shard_map/reduce_scatter | solution.py:136
  3907.3 426.1 %reduce-scatter.19.cloned.1.call-done = bf16[288,5760]{1,0:T(8,128)(2,1)} async-done(((bf16[2304,5760]{1,0:T(8,128)(2,1)}), bf16[288,5760]{1,0:T(8,128)(2,1)}) %reduce-scatter.19.cloned.1.call-update) | async-done | bytes 3317776 | tf_op jit(solution)/shard_map/reduce_scatter | solution.py:136
  4334.2 13.9 fusion.7
  4348.2 4.6 fusion.63
  4352.8 8.0 convolution_add_fusion.1
  4360.9 3.6 fusion.29
  4364.6 28.3 all-reduce.4
  4393.0 12.9 all-reduce.6
  4408.4 195.5 %all-reduce.10.cloned.1.call-done = (bf16[288,2304]{1,0:T(8,128)(2,1)}, bf16[288,2304]{1,0:T(8,128)(2,1)}, bf16[288,2304]{1,0:T(8,128)(2,1)}, bf16[288,2304]{1,0...) async-done(((bf16[288,2304]{1,0:T(8,128)(2,1)}, bf16[288,2304]{1,0:T(8,128)(2,1)}, bf16[288,2304]{1,0:T(8,128)(2,1)}, ...) | async-done | bytes 15261712 | tf_op jit(solution)/shard_map/psum | solution.py:267
  4613.6 3.3 convert_element_type.208
  (189 shorter events, 56.6 us)
Async XLA Ops:
  7.2 154.8 %all-gather.14.cloned.1.call-start = ((), (), s32[]{:S(2)}) async-start(), calls=%async_computation.10 | async-start | bytes 11943936 | tf_op jit(solution)/shard_map/all_gather | solution.py:62
  7.9 32.4 copy-start.35
  8.0 32.6 copy-start
  8.0 306.8 %all-gather.16.cloned.1.call-start = ((), (), s32[]{:S(2)}) async-start(), calls=%async_computation.11 | async-start | bytes 11943936 | tf_op jit(solution)/shard_map/all_gather | solution.py:63
  8.7 458.9 %all-gather.10.cloned.1.call-start = ((), (), s32[]{:S(2)}) async-start(), calls=%async_computation.8 | async-start | bytes 11943936 | tf_op jit(solution)/shard_map/all_gather | solution.py:64
  9.4 485.4 %all-gather.18.cloned.1.call-start = ((), (), s32[]{:S(2)}) async-start(), calls=%async_computation.12 | async-start | bytes 2949120 | tf_op jit(solution)/shard_map/all_gather | solution.py:94
  42.2 279.6 %copy-start.29 = (f32[128,32]{0,1:T(8,128)}, f32[128,32]{0,1:T(8,128)S(1)}, u32[]{:S(2)}) copy-start(f32[128,32]{0,1:T(8,128)S(1)} %get-tuple-element.45) | copy-start | bytes 49156
  322.1 172.8 %copy-start.23 = (bf16[128,36,32]{0,2,1:T(8,128)(2,1)}, bf16[128,36,32]{0,2,1:T(8,128)(2,1)S(1)}, u32[]{:S(2)}) copy-start(bf16[128,36,32]{0,2,1:T(8,128)(2,1)S(1)} %get-tuple-element.35) | copy-start | bytes 884740
  322.1 172.8 %copy-start.25 = (bf16[128,36,32]{0,2,1:T(8,128)(2,1)}, bf16[128,36,32]{0,2,1:T(8,128)(2,1)S(1)}, u32[]{:S(2)}) copy-start(bf16[128,36,32]{0,2,1:T(8,128)(2,1)S(1)} %get-tuple-element.36) | copy-start | bytes 884740
  323.2 198.1 %all-gather.12.cloned.1.call-start = ((), (), s32[]{:S(2)}) async-start(), calls=%async_computation.9 | async-start | bytes 2949120 | tf_op jit(solution)/shard_map/all_gather | solution.py:95
  474.3 198.8 %all-gather.20.cloned.1.call-start = ((), (), s32[]{:S(2)}) async-start(), calls=%async_computation.13 | async-start | bytes 11943936 | tf_op jit(solution)/shard_map/all_gather | solution.py:65
  474.9 706.6 %all-gather.24.cloned.1.call-start = ((), (), s32[]{:S(2)}) async-start(), calls=%async_computation.15 | async-start | bytes 29859840 | tf_op jit(solution)/shard_map/all_gather | solution.py:73
  475.7 1213.6 %all-gather.22.cloned.1.call-start = ((), (), s32[]{:S(2)}) async-start(), calls=%async_computation.14 | async-start | bytes 29859840 | tf_op jit(solution)/shard_map/all_gather | solution.py:72
  476.4 1720.7 %all-gather.26.cloned.1.call-start = ((), (), s32[]{:S(2)}) async-start(), calls=%async_computation.16 | async-start | bytes 29859840 | tf_op jit(solution)/shard_map/all_gather | solution.py:74
  477.2 1847.9 %reduce-scatter.25.cloned.1.call-start = ((), (), s32[]{:S(2)}) async-start(), calls=%async_computation.24 | async-start | bytes 5898240
  503.5 24.0 copy-start.33
  527.5 151.4 %copy-start.12 = (bf16[36,64,128]{2,1,0:T(8,128)(2,1)}, bf16[36,64,128]{2,1,0:T(8,128)(2,1)S(1)}, u32[]{:S(2)}) copy-start(bf16[36,64,128]{2,1,0:T(8,128)(2,1)S(1)} %fusion.16) | copy-start | bytes 1769476
  673.1 6.4 copy-start.28
  678.9 1562.3 %copy-start.2 = (f32[128,2304]{1,0:T(8,128)}, f32[128,2304]{1,0:T(8,128)S(1)}, u32[]{:S(2)}) copy-start(f32[128,2304]{1,0:T(8,128)S(1)} %get-tuple-element.55) | copy-start | bytes 3538948
  679.4 516.0 %copy-start.36 = (f32[128]{0:T(128)}, f32[128]{0:T(128)S(1)}, u32[]{:S(2)}) copy-start(f32[128]{0:T(128)S(1)} %get-tuple-element.51) | copy-start | bytes 1540
  1195.5 1001.6 %copy-start.18 = (bf16[128,2304]{1,0:T(8,128)(2,1)S(1)}, bf16[128,2304]{1,0:T(8,128)(2,1)}, u32[]{:S(2)}) copy-start(bf16[128,2304]{1,0:T(8,128)(2,1)} %param.25) | copy-start | bytes 1769476
  2243.1 34.2 copy-start.3
  2243.1 10.9 copy-start.34
  2243.1 15.9 slice-start.6
  2254.1 5.1 slice-start.7
  2254.1 6.3 slice-start.8
  2254.1 6.4 copy-start.27
  2254.1 7.2 copy-start.42
  2277.2 230.2 %reduce-scatter.17.cloned.1.call-start = ((), (), s32[]{:S(2)}) async-start(), calls=%async_computation.20 | async-start | bytes 11943936 | tf_op jit(solution)/shard_map/reduce_scatter | solution.py:136
  2284.2 405.6 %reduce-scatter.15.cloned.1.call-start = ((), (), s32[]{:S(2)}) async-start(), calls=%async_computation.19 | async-start | bytes 11943936 | tf_op jit(solution)/shard_map/reduce_scatter | solution.py:136
  2331.8 541.1 %reduce-scatter.13.cloned.1.call-start = ((), (), s32[]{:S(2)}) async-start(), calls=%async_computation.18 | async-start | bytes 11943936 | tf_op jit(solution)/shard_map/reduce_scatter | solution.py:136
  2339.3 6.6 copy-start.10
  2345.8 709.4 %reduce-scatter.11.cloned.1.call-start = ((), (), s32[]{:S(2)}) async-start(), calls=%async_computation.17 | async-start | bytes 11943936 | tf_op jit(solution)/shard_map/reduce_scatter | solution.py:136
  2351.8 1129.5 %reduce-scatter.23.cloned.1.call-start = ((), (), s32[]{:S(2)}) async-start(), calls=%async_computation.23 | async-start | bytes 29859840 | tf_op jit(solution)/shard_map/reduce_scatter | solution.py:136
  2365.3 1542.0 %reduce-scatter.21.cloned.1.call-start = ((), (), s32[]{:S(2)}) async-start(), calls=%async_computation.22 | async-start | bytes 29859840 | tf_op jit(solution)/shard_map/reduce_scatter | solution.py:136
  2379.7 1953.7 %reduce-scatter.19.cloned.1.call-start = ((), (), s32[]{:S(2)}) async-start(), calls=%async_computation.21 | async-start | bytes 29859840 | tf_op jit(solution)/shard_map/reduce_scatter | solution.py:136
  2393.4 2210.5 %all-reduce.10.cloned.1.call-start = ((), (), s32[]{:S(2)}) async-start(), calls=%async_computation.25 | async-start | bytes 30523392 | tf_op jit(solution)/shard_map/psum | solution.py:267
  4333.4 14.7 slice-start.3
  4334.2 13.9 slice-start.4
  4334.2 13.9 slice-start.5
  4334.2 13.9 copy-start.11
  4348.2 4.7 copy-start.9
  4348.2 12.7 slice-start
  4348.2 12.7 slice-start.1
  4352.8 8.0 slice-start.2
  4352.8 8.1 copy-start.17
  4360.9 46.2 copy-start.4
  4360.9 46.1 copy-start.41
  (23 other events, 44.3 us)
Sparse Core Ops, SparseCore 0:
  10.2 151.7 all-gather.13
  164.1 150.6 all-gather.15
  317.0 150.6 all-gather.9
  469.6 25.2 all-gather.17
  496.8 24.3 all-gather.11
  523.3 149.7 all-gather.19
  674.6 506.8 all-gather.23
  1183.1 506.1 all-gather.21
  1690.8 506.1 all-gather.25
  2277.4 47.6 reduce-scatter.24
  2329.1 178.3 reduce-scatter.16
  2510.9 178.8 reduce-scatter.14
  2693.8 179.0 reduce-scatter.12
  2876.3 178.8 reduce-scatter.10
  3059.6 421.5 reduce-scatter.22
  3485.6 421.6 reduce-scatter.20
  3911.7 421.6 reduce-scatter.18
  4336.8 267.0 all-reduce.9
where the time goes:
time: 4640 us; the launch traced here: 4630 us
  waiting for transfers between devices  4260 us (92%)
  matrix products  226 us (5%)
  blocking collectives  70.2 us (2%)
    reduce_scatter x7, waiting for transfers between devices, shard_rows(): lax.psum_scatter(lax.dot_general(left_side, right_side, (((0,), (0,)), ((...  1940 us
    all_gather x1, waiting for transfers between devices, ffn_params(): lax.all_gather(w_up, 'shard', axis=0, tiled=True)  502 us
    all_gather x1, waiting for transfers between devices, ffn_params(): lax.all_gather(w_gate, 'shard', axis=0, tiled=True)  494 us
    all_gather x1, waiting for transfers between devices, ffn_params(): lax.all_gather(w_down, 'shard', axis=0, tiled=True)  493 us
    psum x1, waiting for transfers between devices, body(): lax.psum(row_sums[0].astype(jnp.bfloat16), 'replica').astype(jnp.float32)  196 us
    all_gather x1, waiting for transfers between devices, attn_params(): lax.all_gather(w_key, 'shard', axis=0, tiled=True)  146 us
    all_gather x1, waiting for transfers between devices, attn_params(): lax.all_gather(w_out, 'shard', axis=0, tiled=True)  146 us
    all_gather x1, waiting for transfers between devices, attn_params(): lax.all_gather(w_value, 'shard', axis=0, tiled=True)  144 us
  transfers between devices with their start and end apart: 18, of which 18 were waited for; matrix products, arithmetic and copies ran while one was open for 4% of the time, Pallas kernels for 0%

commit v1 on v0

v1 whole, which is shorter than its diff:
```python
import math

import jax
import jax.numpy as jnp
from jax import lax
from jax.sharding import PartitionSpec as P

H = 36
A = 4

branch_scale = 1.4 / math.sqrt(40.0)
norm_eps = 1e-05
rope_base = 10000.0
masked_score = -1e30


def product(left_side, right_side):
    return jnp.dot(left_side, right_side, preferred_element_type=jnp.float32)


def against(left_side, right_side):
    return lax.dot_general(
        left_side, right_side, (((1,), (1,)), ((), ())), preferred_element_type=jnp.float32
    )


def across(left_side, right_side):
    return lax.dot_general(
        left_side, right_side, (((0,), (0,)), ((), ())), preferred_element_type=jnp.float32
    )


def rms_norm(values, gain_vec):
    factor = lax.rsqrt(jnp.mean(values * values, axis=-1, keepdims=True) + norm_eps)
    return (factor, (values * factor * gain_vec).astype(jnp.bfloat16))


def norm_back(values, factor, gain_vec, upstream):
    scaled = upstream * gain_vec
    inner_mean = jnp.mean(scaled * values, axis=-1, keepdims=True)
    return (
        factor * scaled - values * (factor * factor * factor) * inner_mean,
        jnp.sum(upstream * values * factor, axis=0),
    )


def angle_tables(places, head_dim):
    halves = head_dim // 2
    frequency = jnp.exp(
        jnp.arange(halves).astype(jnp.float32) * (-2.0 * math.log(rope_base) / head_dim)
    )
    angles = places.astype(jnp.float32)[:, None] * frequency[None, :]
    return (jnp.cos(angles)[:, None, :], jnp.sin(angles)[:, None, :])


def rotate(values, cosine, sine_table):
    halves = values.shape[-1] // 2
    former = values[..., :halves]
    latter = values[..., halves:]
    return jnp.concatenate(
        [former * cosine - latter * sine_table, latter * cosine + former * sine_table], axis=-1
    )


def body(
    tokens,
    attn_gain,
    w_query,
    w_key,
    w_value,
    w_out,
    ffn_gain,
    w_gate,
    w_up,
    w_down,
    seq_ids,
    block_ids,
    cotangent,
):
    S = lax.axis_size("shard")
    R = lax.axis_size("replica")
    B = S // A
    rows, width = tokens.shape
    group = rows * R
    head_dim = width // H
    heads = H // R
    wcols = width // R
    ff = w_gate.shape[1]
    fcols = ff // (A * R)
    wrows = width // S
    shard_at = lax.axis_index("shard")
    r = lax.axis_index("replica")
    a, b = shard_at // B, shard_at % B
    a_groups = [[i * B + j for i in range(A)] for j in range(B)]
    b_groups = [[i * B + j for j in range(B)] for i in range(A)]
    bf = jnp.bfloat16
    score_scale = 1.0 / math.sqrt(head_dim)

    earlier = jnp.sum((seq_ids[None, :] < seq_ids[:, None]).astype(jnp.int32), axis=1)
    places = jnp.arange(group, dtype=jnp.int32) - earlier
    cosine, sine_table = angle_tables(places, head_dim)
    allowed = (seq_ids[None, :] == seq_ids[:, None]) & (block_ids[None, :] <= block_ids[:, None])

    gains = lax.all_gather(jnp.stack([attn_gain, ffn_gain]), "shard", axis=1, tiled=True)
    gain_one, gain_two = gains[0].astype(jnp.float32), gains[1].astype(jnp.float32)
    own_cols = lambda w: lax.dynamic_slice_in_dim(w, r * wcols, wcols, 1)
    w4 = jnp.concatenate([own_cols(w) for w in (w_query, w_key, w_value, w_out)], axis=1)
    w4 = lax.all_gather(w4, "shard", axis=0, tiled=True)
    wqkv, wo = w4[:, : 3 * wcols], w4[:, 3 * wcols :]
    tokens_group = lax.all_gather(tokens, "replica", axis=0, tiled=True)

    def spread(w):
        w = w.reshape(wrows, A, R, fcols)
        w = lax.dynamic_index_in_dim(w, r, 2, keepdims=False).transpose(1, 0, 2)
        w = lax.all_to_all(w, "shard", 0, 0, axis_index_groups=a_groups, tiled=True)
        w = lax.all_gather(w, "shard", axis=1, axis_index_groups=b_groups, tiled=True)
        return w.reshape(width, fcols)

    gate_w, up_w = spread(w_gate), spread(w_up)
    down_a = lax.all_gather(w_down, "shard", axis=0, axis_index_groups=b_groups, tiled=True)
    down_w = lax.dynamic_slice_in_dim(down_a, r * fcols, fcols, 0)

    def widen(v):
        v = lax.all_gather(v, "shard", axis=0, axis_index_groups=a_groups, tiled=True)
        return lax.all_gather(v, "replica", axis=0, tiled=True)

    def shrink(v):
        v = lax.psum_scatter(v, "replica", scatter_dimension=0, tiled=True)
        return lax.psum_scatter(
            v, "shard", scatter_dimension=0, axis_index_groups=a_groups, tiled=True
        )

    upstream = cotangent.astype(jnp.float32)
    d_down = widen((branch_scale * upstream).astype(bf))

    inputs = tokens.astype(jnp.float32)
    _, normed = rms_norm(tokens_group.astype(jnp.float32), gain_one)
    qkv = product(normed, wqkv)
    heads_of = lambda v: v.reshape(group, heads, head_dim)
    queries = rotate(heads_of(qkv[:, :wcols]), cosine, sine_table).astype(bf)
    keys = rotate(heads_of(qkv[:, wcols : 2 * wcols]), cosine, sine_table).astype(bf)
    values = heads_of(qkv[:, 2 * wcols :].astype(bf))
    scores = (
        jnp.einsum("thd,khd->htk", queries, keys, preferred_element_type=jnp.float32)
        * score_scale
    )
    scores = jnp.where(allowed[None], scores, masked_score)
    probs = jax.nn.softmax(scores, axis=-1)
    probs_low = probs.astype(bf)
    mixed = (
        jnp.einsum("htk,khd->thd", probs_low, values, preferred_element_type=jnp.float32)
        .reshape(group, wcols)
        .astype(bf)
    )
    mixed_all = lax.all_gather(mixed, "replica", axis=1, tiled=True)
    proj = product(mixed_all, wo).astype(bf)
    proj = lax.all_to_all(proj, "replica", 0, 1, tiled=True)
    after_attn = inputs + branch_scale * proj.astype(jnp.float32)
    factor_two, normed_two = rms_norm(after_attn, gain_two)

    n2 = widen(normed_two)
    gate_pre = product(n2, gate_w)
    up_proj = product(n2, up_w)
    sig = jax.nn.sigmoid(gate_pre)
    hidden = (gate_pre * sig * up_proj).astype(bf)
    d_hidden = against(d_down, down_w)
    d_gate = (d_hidden * up_proj * sig * (1.0 + gate_pre * (1.0 - sig))).astype(bf)
    d_up = (d_hidden * gate_pre * sig).astype(bf)
    d_n2 = shrink((against(d_gate, gate_w) + against(d_up, up_w)).astype(bf))
    ffn_out = shrink(product(hidden, down_w).astype(bf))
    result = after_attn + branch_scale * ffn_out.astype(jnp.float32)

    d_norm_two, gain_two_part = norm_back(
        after_attn, factor_two, gain_two, d_n2.astype(jnp.float32)
    )
    d_after = upstream + d_norm_two
    d_proj = (branch_scale * d_after).astype(bf)
    d_proj = lax.all_to_all(d_proj, "replica", 1, 0, tiled=True)
    d_mixed = lax.psum_scatter(
        against(d_proj, wo).astype(bf), "replica", scatter_dimension=1, tiled=True
    )
    d_mixed = heads_of(d_mixed)

    d_probs = jnp.einsum("thd,khd->htk", d_mixed, values, preferred_element_type=jnp.float32)
    d_scores = (
        probs * (d_probs - jnp.sum(d_probs * probs, axis=-1, keepdims=True))
    ).astype(bf)
    d_queries = (
        jnp.einsum("htk,khd->thd", d_scores, keys, preferred_element_type=jnp.float32)
        * score_scale
    )
    d_keys = (
        jnp.einsum("htk,thd->khd", d_scores, queries, preferred_element_type=jnp.float32)
        * score_scale
    )
    d_values = jnp.einsum("htk,thd->khd", probs_low, d_mixed, preferred_element_type=jnp.float32)
    d_qkv = jnp.concatenate(
        [
            rotate(d_queries, cosine, -sine_table).reshape(group, wcols).astype(bf),
            rotate(d_keys, cosine, -sine_table).reshape(group, wcols).astype(bf),
            d_values.reshape(group, wcols).astype(bf),
        ],
        axis=1,
    )
    d_normed = lax.psum_scatter(
        against(d_qkv, wqkv).astype(bf), "replica", scatter_dimension=0, tiled=True
    )
    factor_one, _ = rms_norm(inputs, gain_one)
    d_norm_one, gain_one_part = norm_back(
        inputs, factor_one, gain_one, d_normed.astype(jnp.float32)
    )
    grad_tokens = (d_after + d_norm_one).astype(bf)

    g4 = jnp.concatenate([across(normed, d_qkv), across(mixed_all, d_proj)], axis=1).astype(bf)
    g4 = lax.psum_scatter(g4, "shard", scatter_dimension=0, tiled=True)
    g4 = lax.all_gather(g4.reshape(wrows, 4, wcols), "replica", axis=2, tiled=True)
    g4 = g4.astype(jnp.float32)

    def collect(g):
        g = g.reshape(A, B, wrows, fcols)
        g = lax.psum_scatter(
            g, "shard", scatter_dimension=1, axis_index_groups=b_groups, tiled=True
        ).reshape(A, wrows, fcols)
        g = lax.all_to_all(g, "shard", 0, 0, axis_index_groups=a_groups, tiled=True)
        g = lax.all_gather(g, "replica", axis=0)
        return g.transpose(2, 1, 0, 3).reshape(wrows, ff).astype(jnp.float32)

    grad_gate = collect(across(n2, d_gate).astype(bf))
    grad_up = collect(across(n2, d_up).astype(bf))
    g_down = lax.all_gather(across(hidden, d_down).astype(bf), "replica", axis=0, tiled=True)
    grad_down = lax.psum_scatter(
        g_down, "shard", scatter_dimension=0, axis_index_groups=b_groups, tiled=True
    ).astype(jnp.float32)

    gain_grads = lax.psum(jnp.stack([gain_one_part, gain_two_part]), ("shard", "replica"))
    gain_grads = lax.dynamic_slice_in_dim(gain_grads, shard_at * wrows, wrows, 1)
    return (
        result.astype(bf),
        grad_tokens,
        gain_grads[0],
        g4[:, 0],
        g4[:, 1],
        g4[:, 2],
        g4[:, 3],
        gain_grads[1],
        grad_gate,
        grad_up,
        grad_down,
    )


def solution(mesh):
    split = P(("shard", "replica"), None)
    vec, mat = P("shard"), P("shard", None)
    in_specs = (split, vec, mat, mat, mat, mat, vec, mat, mat, mat, vec, vec, split)
    out_specs = (split, split, vec, mat, mat, mat, mat, vec, mat, mat, mat)
    return jax.shard_map(body, mesh=mesh, in_specs=in_specs, out_specs=out_specs, check_vma=False)
```

time: 4640 us -> 1630 us (0.35)
  waiting for transfers between devices: 4260 us -> 1030 us
  blocking collectives: 70.2 us -> 236 us
  local copies, waits for them, and re-layouts: 24.5 us -> 124 us
  matrix products: 226 us -> 154 us
    reduce_scatter x7, waiting for transfers between devices: 1940 us -> 292 us  [the longest x2 146 us: shrink(): v = lax.psum_scatter(v, 'replica', scatter_dimension=0, tiled=True)]
    all_gather x9 -> x14, waiting for transfers between devices: 2080 us -> 540 us  [the longest x1 150 us: body(): w4 = lax.all_gather(w4, 'shard', axis=0, tiled=True)]
    psum x1 -> x0, waiting for transfers between devices: 196 us -> none  [body(): lax.psum(row_sums[0].astype(jnp.bfloat16), 'replica').astype(jnp.float32)]
    all_to_all x0 -> x6, blocking collectives: none -> 173 us  [the longest x2 98.1 us: spread(): w = lax.all_to_all(w, 'shard', 0, 0, axis_index_groups=a_groups, tiled=True)]
    unnamed x19 -> x25, waiting for transfers between devices: 45.7 us -> 199 us
    unnamed x2 -> x0, blocking collectives: 57.3 us -> none
  transfers between devices with their start and end apart: 18 -> 23, of which waited for: 18 -> 20; matrix products, arithmetic and copies ran while one was open for 4% -> 15% of each run, Pallas kernels for 0% -> 0%
where the time goes in v1:
time: 1630 us; the launch traced here: 1620 us
  waiting for transfers between devices  1030 us (63%)
  blocking collectives  236 us (14%)
  matrix products  154 us (9%)
  local copies, waits for them, and re-layouts  124 us (8%)
  other arithmetic  55.4 us (3%)
    unnamed x25, waiting for transfers between devices  199 us
    all_gather x1, waiting for transfers between devices, body(): w4 = lax.all_gather(w4, 'shard', axis=0, tiled=True)  150 us
    reduce_scatter x2, waiting for transfers between devices, shrink(): v = lax.psum_scatter(v, 'replica', scatter_dimension=0, tiled=True)  146 us
    all_gather x2, waiting for transfers between devices, widen(): return lax.all_gather(v, 'replica', axis=0, tiled=True)  132 us
    all_to_all x2, blocking collectives, spread(): w = lax.all_to_all(w, 'shard', 0, 0, axis_index_groups=a_groups, tiled=True)  98.1 us
    all_gather x1, waiting for transfers between devices, body(): lax.all_gather(w_down, 'shard', axis=0, axis_index_groups=b_groups, tiled...  76.4 us
    reduce_scatter x1, waiting for transfers between devices, body(): lax.psum_scatter(g_down, 'shard', scatter_dimension=0, axis_index_groups=...  62.5 us
    all_gather x2, waiting for transfers between devices, spread(): lax.all_gather(w, 'shard', axis=1, axis_index_groups=b_groups, tiled=True)  53.9 us
  transfers between devices with their start and end apart: 23, of which 20 were waited for; matrix products, arithmetic and copies ran while one was open for 15% of the time, Pallas kernels for 0%

profile of v1, /device:TPU:9, one launch (start us, length us, event | category | flops | bytes accessed | tf_op | source)
XLA Modules:
  0.0 1617.1 jit_solution(6948980309731413471)
XLA Ops:
  13.2 20.2 %all-gather.2 = bf16[8,288,2]{1,2,0:T(2,128)(2,1)S(1)} all-gather(bf16[1,288,2]{1,2,0:T(2,128)(2,1)S(1)} %maximum_bitcast_fusion), channel_id=1, replica_groups=mesh['shard'=8,'replica'=4] {'shard'}, dimensions={0}, use_global_device_ids=true | all-gather | bytes 10368 | tf_op jit(solution)/shard_map/all_gather | solution.py:104
  38.1 149.7 %all-gather.20.cloned.1.call-done = bf16[2304,2304]{1,0:T(8,128)(2,1)} async-done(((bf16[288,2304]{1,0:T(8,128)(2,1)}), bf16[2304,2304]{1,0:T(8,128)(2,1)}) %all-gather.20.cloned.1.call-update) | async-done | bytes 10616848 | tf_op jit(solution)/shard_map/all_gather | solution.py:108
  187.8 7.1 fusion.3
  207.7 25.0 %all-gather.22.cloned.1.call-done = bf16[512,2304]{0,1:T(8,128)(2,1)} async-done(((bf16[512,576]{0,1:T(8,128)(2,1)}), bf16[512,2304]{0,1:T(8,128)(2,1)}) %all-gather.22.cloned.1.call-update) | async-done | bytes 2359312 | tf_op jit(solution)/shard_map/all_gather | solution.py:155
  238.2 11.9 all_to_all.52
  254.0 8.8 reshape.275
  266.8 47.1 %all_to_all.53 = bf16[4,288,360]{2,1,0:T(8,128)(2,1)} all-to-all(bf16[4,288,360]{2,1,0:T(8,128)(2,1)S(1)} %bitcast.120), channel_id=1, replica_groups={{0,8,16,24},{4,12,20,28},{1,9,17,25},{5,13,21,29},{2,10,18,26},{6,14,22..., dimensions={0} | all-to-all | bytes 1658880 | tf_op jit(solution)/shard_map/all_to_all | solution.py:115
  318.9 8.8 reshape.273
  331.7 51.0 %all_to_all.54 = bf16[4,288,360]{2,1,0:T(8,128)(2,1)} all-to-all(bf16[4,288,360]{2,1,0:T(8,128)(2,1)S(1)} %bitcast.121), channel_id=1, replica_groups={{0,8,16,24},{4,12,20,28},{1,9,17,25},{5,13,21,29},{2,10,18,26},{6,14,22..., dimensions={0} | all-to-all | bytes 1658880 | tf_op jit(solution)/shard_map/all_to_all | solution.py:115
  388.8 32.8 %all-gather.30.cloned.1.call-done = bf16[4,576,360]{2,1,0:T(8,128)(2,1)} async-done(((bf16[4,288,360]{2,1,0:T(8,128)(2,1)}), bf16[4,576,360]{2,1,0:T(8,128)(2,1)}) %all-gather.30.cloned.1.call-update) | async-done | bytes 1658896 | tf_op jit(solution)/shard_map/all_gather | solution.py:116
  421.6 66.3 %all-gather.26.cloned.1.call-done = bf16[2048,2304]{1,0:T(8,128)(2,1)} async-done(((bf16[512,2304]{1,0:T(8,128)(2,1)}), bf16[2048,2304]{1,0:T(8,128)(2,1)}) %all-gather.26.cloned.1.call-update) | async-done | bytes 9437200 | tf_op jit(solution)/shard_map/all_gather | solution.py:125
  487.8 9.4 fusion.83
  497.2 21.2 %all-gather.28.cloned.1.call-done = bf16[4,576,360]{2,1,0:T(8,128)(2,1)} async-done(((bf16[4,288,360]{2,1,0:T(8,128)(2,1)}), bf16[4,576,360]{2,1,0:T(8,128)(2,1)}) %all-gather.28.cloned.1.call-update) | async-done | bytes 1658896 | tf_op jit(solution)/shard_map/all_gather | solution.py:116
  518.4 9.4 fusion.82
  527.8 76.4 %all-gather.32.cloned.1.call-done = bf16[1440,2304]{1,0:T(8,128)(2,1)} async-done(((bf16[720,2304]{1,0:T(8,128)(2,1)}), bf16[1440,2304]{1,0:T(8,128)(2,1)}) %all-gather.32.cloned.1.call-update) | async-done | bytes 6635536 | tf_op jit(solution)/shard_map/all_gather | solution.py:120
  604.3 66.1 %all-gather.36.cloned.1.call-done = bf16[2048,2304]{1,0:T(8,128)(2,1)} async-done(((bf16[512,2304]{1,0:T(8,128)(2,1)}), bf16[2048,2304]{1,0:T(8,128)(2,1)}) %all-gather.36.cloned.1.call-update) | async-done | bytes 9437200 | tf_op jit(solution)/shard_map/all_gather | solution.py:125
  670.4 11.5 multiply_convert_fusion.1
  681.8 11.5 fusion.84
  693.3 11.3 add_convert_fusion
  704.6 78.1 %reduce-scatter.17.cloned.1.call-done = bf16[512,2304]{1,0:T(8,128)(2,1)} async-done(((bf16[2048,2304]{1,0:T(8,128)(2,1)}), bf16[512,2304]{1,0:T(8,128)(2,1)}) %reduce-scatter.17.cloned.1.call-update) | async-done | bytes 2359312 | tf_op jit(solution)/shard_map/reduce_scatter | solution.py:128
  782.8 47.8 %reduce-scatter.19.cloned.1.call-done = bf16[128,2304]{1,0:T(8,128)(2,1)} async-done(((bf16[512,2304]{1,0:T(8,128)(2,1)}), bf16[128,2304]{1,0:T(8,128)(2,1)}) %reduce-scatter.19.cloned.1.call-update) | async-done | bytes 589840 | tf_op jit(solution)/shard_map/reduce_scatter | solution.py:129
  837.2 14.2 all_to_all.55
  857.6 8.8 convolution_convert_fusion.6
  870.6 8.4 convolution_convert_fusion.5
  884.2 8.5 convolution_convert_fusion.4
  892.8 8.9 convolution_convert_fusion.1
  907.6 7.2 multiply_reduce_fusion
  914.8 11.4 multiply_convert_fusion
  937.7 6.5 convolution_convert_fusion
  944.2 12.3 pad_maximum_fusion
  956.5 15.2 copy.100
  972.9 15.1 all-reduce.5.cloned.1.call-done
  989.9 24.4 %all_to_all.56 = bf16[4,288,360]{2,1,0:T(8,128)(2,1)} all-to-all(bf16[4,288,360]{2,1,0:T(8,128)(2,1)S(1)} %dynamic-slice_bitcast_fusion.1), channel_id=1, replica_groups={{0,8,16,24},{4,12,20,28},{1,9,17,25},{5,13,21,29},{2,10,18,26},{6,14,22..., dimensions={0} | all-to-all | bytes 1658880 | tf_op jit(solution)/shard_map/all_to_all | solution.py:224
  1016.3 24.3 %all_to_all.57 = bf16[4,288,360]{2,1,0:T(8,128)(2,1)} all-to-all(bf16[4,288,360]{2,1,0:T(8,128)(2,1)S(1)} %dynamic-slice_bitcast_fusion), channel_id=1, replica_groups={{0,8,16,24},{4,12,20,28},{1,9,17,25},{5,13,21,29},{2,10,18,26},{6,14,22..., dimensions={0} | all-to-all | bytes 1658880 | tf_op jit(solution)/shard_map/all_to_all | solution.py:224
  1041.8 9.1 fusion.12
  1051.1 68.2 %reduce-scatter.13.cloned.1.call-done = bf16[512,2304]{1,0:T(8,128)(2,1)} async-done(((bf16[2048,2304]{1,0:T(8,128)(2,1)}), bf16[512,2304]{1,0:T(8,128)(2,1)}) %reduce-scatter.13.cloned.1.call-update) | async-done | bytes 2359312 | tf_op jit(solution)/shard_map/reduce_scatter | solution.py:128
  1119.3 181.7 %reduce-scatter.27.cloned.1.call-done = bf16[288,2304]{1,0:T(8,128)(2,1)} async-done(((bf16[2304,2304]{1,0:T(8,128)(2,1)}), bf16[288,2304]{1,0:T(8,128)(2,1)}) %reduce-scatter.27.cloned.1.call-update) | async-done | bytes 1327120
  1306.2 28.3 %all-gather.42.cloned.1.call-done = bf16[16,288,360]{2,1,0:T(8,128)(2,1)} async-done(((bf16[4,288,360]{2,1,0:T(8,128)(2,1)}), bf16[16,288,360]{2,1,0:T(8,128)(2,1)}) %all-gather.42.cloned.1.call-update) | async-done | bytes 3317776 | tf_op jit(solution)/shard_map/all_gather | solution.py:225
  1337.2 7.8 copy.93
  1345.0 9.9 reshape.285
  1354.9 12.0 all-gather.44.cloned.1.call-done
  1369.7 8.0 copy.95
  1377.7 9.4 reshape.286
  1387.1 62.5 %reduce-scatter.25.cloned.1.call-done = bf16[720,2304]{1,0:T(8,128)(2,1)} async-done(((bf16[1440,2304]{1,0:T(8,128)(2,1)}), bf16[720,2304]{1,0:T(8,128)(2,1)}) %reduce-scatter.25.cloned.1.call-update) | async-done | bytes 3317776 | tf_op jit(solution)/shard_map/reduce_scatter | solution.py:231
  1454.9 31.0 %reduce-scatter.23.cloned.1.call-done = bf16[128,2304]{1,0:T(8,128)(2,1)} async-done(((bf16[512,2304]{1,0:T(8,128)(2,1)}), bf16[128,2304]{1,0:T(8,128)(2,1)}) %reduce-scatter.23.cloned.1.call-update) | async-done | bytes 589840 | tf_op jit(solution)/shard_map/reduce_scatter | solution.py:205
  1487.3 42.6 %psum.7 = f32[2,2304]{1,0:T(2,128)S(1)} all-reduce(f32[2,2304]{1,0:T(2,128)S(1)} %pad_maximum_fusion.20), channel_id=1, replica_groups=mesh['shard'=8,'replica'=4] {'shard','replica'}, use_global_device_ids=true, to_apply=%region_17.18 | all-reduce | flops 4608 | bytes 36864 | tf_op jit(solution)/shard_map/psum | solution.py:235
  1538.0 52.2 %all-gather.38.cloned.1.call-done = bf16[288,4,2304]{0,1,2:T(4,128)(2,1)} async-done(((bf16[288,4,576]{0,1,2:T(4,128)(2,1)}), bf16[288,4,2304]{0,1,2:T(4,128)(2,1)}) %all-gather.38.cloned.1.call-update) | async-done | bytes 5308432 | tf_op jit(solution)/shard_map/all_gather | solution.py:216
  1590.2 12.3 copy.91
  (213 shorter events, 130.3 us)
Async XLA Ops:
  7.2 28.6 %all-gather.18.cloned.1.call-start = ((), (), s32[]{:S(2)}) async-start(), calls=%async_computation.14 | async-start | bytes 2949120 | tf_op jit(solution)/shard_map/all_gather | solution.py:110
  7.9 179.9 %all-gather.20.cloned.1.call-start = ((), (), s32[]{:S(2)}) async-start(), calls=%async_computation.15 | async-start | bytes 11943936 | tf_op jit(solution)/shard_map/all_gather | solution.py:108
  11.0 22.6 %copy-start.33 = (s32[512]{0:T(512)S(1)}, s32[512]{0:T(512)}, u32[]{:S(2)}) copy-start(s32[512]{0:T(512)} %param.23) | copy-start | bytes 6148
  11.0 23.8 %copy-start.34 = (s32[512]{0:T(512)S(1)}, s32[512]{0:T(512)}, u32[]{:S(2)}) copy-start(s32[512]{0:T(512)} %param.24) | copy-start | bytes 6148
  13.1 219.7 %all-gather.22.cloned.1.call-start = ((), (), s32[]{:S(2)}) async-start(), calls=%async_computation.16 | async-start | bytes 2949120 | tf_op jit(solution)/shard_map/all_gather | solution.py:155
  33.6 161.3 %copy-start.27 = (f32[2304]{0:T(1024)}, f32[2304]{0:T(1024)S(1)}, u32[]{:S(2)}) copy-start(f32[2304]{0:T(1024)S(1)} %get-tuple-element.29) | copy-start | bytes 27652
  35.7 152.1 %copy-start.7 = (bf16[512,2304]{1,0:T(8,128)(2,1)S(1)}, bf16[512,2304]{1,0:T(8,128)(2,1)}, u32[]{:S(2)}) copy-start(bf16[512,2304]{1,0:T(8,128)(2,1)} %all-gather.18.cloned.1.call-done) | copy-start | bytes 7077892
  38.1 156.8 %copy-start.35 = (f32[512]{0:T(512)}, f32[512]{0:T(512)S(1)}, u32[]{:S(2)}) copy-start(f32[512]{0:T(512)S(1)} %add_rsqrt_fusion) | copy-start | bytes 6148
  195.0 7.2 copy-start.20
  196.4 5.8 copy-start.10
  196.4 5.8 copy-start.12
  196.5 5.7 copy-start.14
  207.7 111.2 %all-gather.24.cloned.1.call-start = ((), (), s32[]{:S(2)}) async-start(), calls=%async_computation.17 | async-start | bytes 2949120 | tf_op jit(solution)/shard_map/all_gather | solution.py:124
  252.0 580.7 %copy-start.37 = (f32[128]{0:T(128)}, f32[128]{0:T(128)S(1)}, u32[]{:S(2)}) copy-start(f32[128]{0:T(128)S(1)} %get-tuple-element.63) | copy-start | bytes 1540
  253.0 135.6 %all-gather.34.cloned.1.call-start = ((), (), s32[]{:S(2)}) async-start(), calls=%async_computation.24 | async-start | bytes 2949120 | tf_op jit(solution)/shard_map/all_gather | solution.py:124
  254.0 167.6 %all-gather.30.cloned.1.call-start = ((), (), s32[]{:S(2)}) async-start(), calls=%async_computation.20 | async-start | bytes 2654208 | tf_op jit(solution)/shard_map/all_gather | solution.py:116
  314.0 173.9 %all-gather.26.cloned.1.call-start = ((), (), s32[]{:S(2)}) async-start(), calls=%async_computation.18 | async-start | bytes 11796480 | tf_op jit(solution)/shard_map/all_gather | solution.py:125
  318.9 199.5 %all-gather.28.cloned.1.call-start = ((), (), s32[]{:S(2)}) async-start(), calls=%async_computation.19 | async-start | bytes 2654208 | tf_op jit(solution)/shard_map/all_gather | solution.py:116
  382.7 221.6 %all-gather.32.cloned.1.call-start = ((), (), s32[]{:S(2)}) async-start(), calls=%async_computation.21 | async-start | bytes 9953280 | tf_op jit(solution)/shard_map/all_gather | solution.py:120
  383.4 286.9 %all-gather.36.cloned.1.call-start = ((), (), s32[]{:S(2)}) async-start(), calls=%async_computation.25 | async-start | bytes 11796480 | tf_op jit(solution)/shard_map/all_gather | solution.py:125
  388.6 394.1 %reduce-scatter.17.cloned.1.call-start = ((), (), s32[]{:S(2)}) async-start(), calls=%async_computation.26 | async-start | bytes 11796480 | tf_op jit(solution)/shard_map/reduce_scatter | solution.py:128
  681.8 11.5 copy-start.6
  681.8 11.5 copy-start.9
  704.6 126.0 %reduce-scatter.19.cloned.1.call-start = ((), (), s32[]{:S(2)}) async-start(), calls=%async_computation.27 | async-start | bytes 2949120 | tf_op jit(solution)/shard_map/reduce_scatter | solution.py:129
  782.8 124.8 %reduce-scatter.21.cloned.1.call-start = ((), (), s32[]{:S(2)}) async-start(), calls=%async_computation.28 | async-start | bytes 2949120 | tf_op jit(solution)/shard_map/reduce_scatter | solution.py:179
  832.6 18.8 %copy-start.39 = (f32[128]{0:T(128)}, f32[128]{0:T(128)S(1)}, u32[]{:S(2)}) copy-start(f32[128]{0:T(128)S(1)} %broadcast_multiply_fusion.1) | copy-start | bytes 1540
  857.5 130.5 %all-reduce.5.cloned.1.call-start = ((), (), s32[]{:S(2)}) async-start(), calls=%async_computation.36 | async-start | bytes 7077888
  882.9 157.9 %all-gather.40.cloned.1.call-start = ((), (), s32[]{:S(2)}) async-start(), calls=%async_computation.31 | async-start | bytes 8294400 | tf_op jit(solution)/shard_map/all_gather | solution.py:230
  892.8 226.5 %reduce-scatter.13.cloned.1.call-start = ((), (), s32[]{:S(2)}) async-start(), calls=%async_computation.22 | async-start | bytes 11796480 | tf_op jit(solution)/shard_map/reduce_scatter | solution.py:128
  901.8 5.8 copy-start.21
  901.8 5.8 copy-start.32
  901.8 399.2 %reduce-scatter.27.cloned.1.call-start = ((), (), s32[]{:S(2)}) async-start(), calls=%async_computation.35 | async-start | bytes 11943936
  914.8 11.4 copy-start.15
  914.8 11.4 copy-start.17
  937.6 6.6 copy-start.44
  937.6 6.5 copy-start.5
  971.7 362.8 %all-gather.42.cloned.1.call-start = ((), (), s32[]{:S(2)}) async-start(), calls=%async_computation.33 | async-start | bytes 4423680 | tf_op jit(solution)/shard_map/all_gather | solution.py:225
  1014.4 352.6 %all-gather.44.cloned.1.call-start = ((), (), s32[]{:S(2)}) async-start(), calls=%async_computation.34 | async-start | bytes 4423680 | tf_op jit(solution)/shard_map/all_gather | solution.py:225
  1040.7 408.9 %reduce-scatter.25.cloned.1.call-start = ((), (), s32[]{:S(2)}) async-start(), calls=%async_computation.32 | async-start | bytes 9953280 | tf_op jit(solution)/shard_map/reduce_scatter | solution.py:231
  1041.3 444.5 %reduce-scatter.23.cloned.1.call-start = ((), (), s32[]{:S(2)}) async-start(), calls=%async_computation.29 | async-start | bytes 2949120 | tf_op jit(solution)/shard_map/reduce_scatter | solution.py:205
  1051.0 484.0 %reduce-scatter.15.cloned.1.call-start = ((), (), s32[]{:S(2)}) async-start(), calls=%async_computation.23 | async-start | bytes 2949120 | tf_op jit(solution)/shard_map/reduce_scatter | solution.py:129
  1119.3 470.9 %all-gather.38.cloned.1.call-start = ((), (), s32[]{:S(2)}) async-start(), calls=%async_computation.30 | async-start | bytes 8847360 | tf_op jit(solution)/shard_map/all_gather | solution.py:216
  1387.1 67.8 %copy-start.30 = (f32[2304]{0:T(1024)S(1)}, f32[2304]{0:T(1024)}, u32[]{:S(2)}) copy-start(f32[2304]{0:T(1024)} %get-tuple-element.22) | copy-start | bytes 27652
  1387.1 98.7 %copy-start.2 = (bf16[128,2304]{1,0:T(8,128)(2,1)S(1)}, bf16[128,2304]{1,0:T(8,128)(2,1)}, u32[]{:S(2)}) copy-start(bf16[128,2304]{1,0:T(8,128)(2,1)} %param.13) | copy-start | bytes 1769476
  1387.1 98.7 %copy-start.29 = (f32[2304]{0:T(1024)S(1)}, f32[2304]{0:T(1024)}, u32[]{:S(2)}) copy-start(f32[2304]{0:T(1024)} %copy-done.27) | copy-start | bytes 27652
  1387.1 148.0 %copy-start.3 = (bf16[128,2304]{1,0:T(8,128)(2,1)S(1)}, bf16[128,2304]{1,0:T(8,128)(2,1)}, u32[]{:S(2)}) copy-start(bf16[128,2304]{1,0:T(8,128)(2,1)} %reduce-scatter.19.cloned.1.call-done) | copy-start | bytes 1769476
  1387.1 148.0 %copy-start.38 = (f32[128]{0:T(128)S(1)}, f32[128]{0:T(128)}, u32[]{:S(2)}) copy-start(f32[128]{0:T(128)} %copy-done.37) | copy-start | bytes 1540
  1387.1 147.9 %copy-start.40 = (f32[128]{0:T(128)S(1)}, f32[128]{0:T(128)}, u32[]{:S(2)}) copy-start(f32[128]{0:T(128)} %copy-done.39) | copy-start | bytes 1540
  (23 other events, 57.8 us)
Sparse Core Ops, SparseCore 0:
  9.6 25.6 all-gather.17
  38.0 149.7 all-gather.19
  207.8 24.9 all-gather.21
  253.1 65.7 all-gather.23
  320.9 67.6 all-gather.33
  390.0 31.5 all-gather.29
  423.1 64.6 all-gather.25
  489.4 28.9 all-gather.27
  520.0 84.2 all-gather.31
  605.7 64.6 all-gather.35
  704.7 77.9 reduce-scatter.16
  784.9 45.6 reduce-scatter.18
  857.6 32.8 reduce-scatter.20
  893.4 94.5 all-reduce.4
  990.0 48.7 all-gather.39
  1041.2 77.9 reduce-scatter.12
  1122.7 178.2 reduce-scatter.26
  1302.5 31.9 all-gather.41
  1336.1 30.7 all-gather.43
  1369.2 80.3 reduce-scatter.24
  1452.7 33.0 reduce-scatter.22
  1488.2 46.7 reduce-scatter.14
  1537.3 52.8 all-gather.37

commit v2 on v1

v2 whole, which is shorter than its diff:
```python
import functools
import math

import jax
import jax.numpy as jnp
from jax import lax
from jax.experimental import pallas as pl
from jax.experimental.pallas import tpu as pltpu
from jax.sharding import PartitionSpec as P

H = 36
A = 4
X = 2

branch_scale = 1.4 / math.sqrt(40.0)
norm_eps = 1e-05
rope_base = 10000.0
masked_score = -1e30
MESH = pl.DeviceIdType.MESH
bf = jnp.bfloat16
f32 = jnp.float32
DMA = pltpu.SemaphoreType.DMA


class Place:
    def __init__(self, B):
        self.B = B
        s, r = lax.axis_index("shard"), lax.axis_index("replica")
        self.s, self.r = s, r
        self.a, self.b = s // B, s % B
        self.x, self.c = r // X, r % X
        self.rx = (1 - self.x) * X + self.c
        self.rc = self.x * X + 1 - self.c

    def line(self, a):
        return (a * self.B + self.b, self.r)

    def side(self, b):
        return (self.a * self.B + b, self.r)

    @property
    def over_x(self):
        return (self.s, self.rx)

    @property
    def over_core(self):
        return (self.s, self.rc)


def greet(place, a_peers=True, b_peers=False, r_peers=True, everyone=None):
    barrier = pltpu.get_barrier_semaphore()

    def signal(device):
        pl.semaphore_signal(barrier, inc=1, device_id=device, device_id_type=MESH)

    if everyone is not None:
        S, R = everyone

        def one(k, carry):
            signal((lax.rem(place.s + k // R, S), lax.rem(place.r + k % R, R)))
            return carry

        lax.fori_loop(1, S * R, one, 0)
        pl.semaphore_wait(barrier, S * R - 1)
        return
    count = 0
    if a_peers:
        for k in range(1, A):
            signal(place.line((place.a + k) % A))
            count += 1
    if b_peers:
        for k in range(1, place.B):
            signal(place.side((place.b + k) % place.B))
            count += 1
    if r_peers:
        signal(place.over_x)
        signal(place.over_core)
        count += 2
    pl.semaphore_wait(barrier, count)


def remote(src, dst, send, recv, device):
    return pltpu.make_async_remote_copy(
        src_ref=src, dst_ref=dst, send_sem=send, recv_sem=recv, device_id=device,
        device_id_type=MESH,
    )


def add_into(dst, first, second, tile=32):
    rows = dst.shape[0]
    tile = math.gcd(rows, tile) if math.gcd(rows, tile) >= 16 else rows

    def step(i, carry):
        at = pl.ds(pl.multiple_of(i * tile, tile), tile)
        dst[at, :] = (first[at, :].astype(f32) + second[at, :].astype(f32)).astype(dst.dtype)
        return carry

    lax.fori_loop(0, rows // tile, step, 0)


def run_flows(flows):
    flows = list(flows)
    while flows:
        for flow in list(flows):
            try:
                next(flow)
            except StopIteration:
                flows.remove(flow)


def widen_sems():
    return [DMA((A,)), DMA((X,)), DMA((A, 2)), DMA((A, 2)), DMA((X, A, 2)), DMA((1,))]


def widen_flow(place, own, out, sems):
    line_recv, _, line_send, over_x, over_core, local = sems
    a, r = place.a, place.r
    keep = pltpu.make_async_copy(own, out.at[r, a], local.at[0])
    keep.start()

    def to_line(src, block, way):
        at = 0 if way > 0 else 1
        return remote(
            src, out.at[r, block], line_send.at[block, at], line_recv.at[block],
            place.line(a + way),
        )

    def to_x(src, block):
        return remote(
            src, out.at[r, block], over_x.at[block, 0], over_x.at[block, 1], place.over_x
        )

    def to_core(src, x, block):
        return remote(
            src, out.at[x * X + place.c, block], over_core.at[x, block, 0],
            over_core.at[x, block, 1], place.over_core,
        )

    @pl.when(a < A - 1)
    def _():
        to_line(own, a, 1).start()

    @pl.when(a > 0)
    def _():
        to_line(own, a, -1).start()

    to_x(own, a).start()
    to_core(own, place.x, a).start()

    def pass_x(k):
        for ok, block in ((a - k >= 0, a - k), (a + k < A, a + k)) if k else ((None, a),):
            def go():
                src = out.at[place.rx, block]
                to_x(src, block).wait_recv()
                to_core(src, 1 - place.x, block).start()

            go() if ok is None else pl.when(ok)(go)

    for k in range(1, A):
        yield
        for way in (1, -1):
            block = a - way * k

            @pl.when((block >= 0) & (block < A))
            def _():
                src = out.at[r, block]
                to_line(src, block, way).wait_recv()

                @pl.when((a + way >= 0) & (a + way < A))
                def _():
                    to_line(src, block, way).start()

                to_x(src, block).start()
                to_core(src, place.x, block).start()

        yield
        pass_x(k - 1)
    yield
    pass_x(A - 1)
    yield
    keep.wait()
    for block in range(A):
        src = out.at[r, block]

        @pl.when((a < A - 1) & (block <= a))
        def _():
            to_line(src, block, 1).wait_send()

        @pl.when((a > 0) & (block >= a))
        def _():
            to_line(src, block, -1).wait_send()

        to_x(src, block).wait_send()
        for x in range(X):
            to_core(src, x, block).wait()


def shrink_scratch(rows, width):
    block = (rows, width)
    return [
        pltpu.VMEM((X, A) + block, bf),
        pltpu.VMEM((X, A) + block, bf),
        pltpu.VMEM((A,) + block, bf),
        pltpu.VMEM((2, A) + block, bf),
        DMA((X, A)), DMA((X, A, 2)), DMA((A, 2)), DMA((2, A, 2)),
    ]


shrink_order = (3, 0, 2, 1)


def line_reduce(place, sums, landed, sems, ready, final):
    a = place.a

    def hop(d, way):
        at = 0 if way > 0 else 1
        return remote(
            sums.at[d], landed.at[at, d], sems.at[at, d, 0], sems.at[at, d, 1],
            place.line(a + way),
        )

    for d in shrink_order:
        yield
        ready(d)
        for way in (1, -1):
            @pl.when((d - a) * way > 0)
            def _():
                @pl.when((a - way >= 0) & (a - way < A))
                def _():
                    hop(d, way).wait_recv()
                    add_into(sums.at[d], sums.at[d], landed.at[0 if way > 0 else 1, d])

                hop(d, way).start()

    yield
    for d in range(A):
        @pl.when(d == a)
        def _():
            for way in (1, -1):
                @pl.when((a - way >= 0) & (a - way < A))
                def _():
                    hop(d, way).wait_recv()
                    add_into(sums.at[d], sums.at[d], landed.at[0 if way > 0 else 1, d])

            final(sums.at[d])

        for way in (1, -1):
            @pl.when((d - a) * way > 0)
            def _():
                hop(d, way).wait_send()


def shrink_flow(place, part, out, scratch):
    half, from_core, from_x, landed, load_sem, core_sem, x_sem, line_sem = scratch
    x, c = place.x, place.c

    def load(i, d):
        return pltpu.make_async_copy(part.at[i * X + c, d], half.at[i, d], load_sem.at[i, d])

    def to_core(i, d):
        return remote(
            part.at[i * X + 1 - c, d], from_core.at[i, d], core_sem.at[i, d, 0],
            core_sem.at[i, d, 1], place.over_core,
        )

    def to_x(d):
        return remote(
            half.at[1 - x, d], from_x.at[d], x_sem.at[d, 0], x_sem.at[d, 1], place.over_x
        )

    for j in range(X):
        for d in shrink_order:
            i = 1 - x if j == 0 else x
            load(i, d).start()
            to_core(i, d).start()
    for d in shrink_order:
        yield
        load(1 - x, d).wait()
        to_core(1 - x, d).wait_recv()
        add_into(half.at[1 - x, d], half.at[1 - x, d], from_core.at[1 - x, d])
        to_x(d).start()

    def ready(d):
        load(x, d).wait()
        to_core(x, d).wait_recv()
        add_into(half.at[x, d], half.at[x, d], from_core.at[x, d])
        to_x(d).wait_recv()
        add_into(half.at[x, d], half.at[x, d], from_x.at[d])

    def final(ref):
        out[...] = ref[...]

    yield from line_reduce(place, half.at[x], landed, line_sem, ready, final)
    for d in range(A):
        to_x(d).wait_send()
        for i in range(X):
            to_core(i, d).wait_send()


def fold_scratch(rows, width):
    block = (rows, width)
    return [
        pltpu.VMEM((X,) + block, bf), pltpu.VMEM((X,) + block, bf), pltpu.VMEM(block, bf),
        DMA((X,)), DMA((X, 2)), DMA((2,)),
    ]


def fold_flow(place, part, out, scratch):
    half, from_core, from_x, load_sem, core_sem, x_sem = scratch
    x, c = place.x, place.c

    def load(i):
        return pltpu.make_async_copy(part.at[i * X + c], half.at[i], load_sem.at[i])

    def to_core(i):
        return remote(
            part.at[i * X + 1 - c], from_core.at[i], core_sem.at[i, 0], core_sem.at[i, 1],
            place.over_core,
        )

    to_x = remote(half.at[1 - x], from_x, x_sem.at[0], x_sem.at[1], place.over_x)
    for i in (1 - x, x):
        load(i).start()
        to_core(i).start()
    yield
    for i in (1 - x, x):
        load(i).wait()
        to_core(i).wait_recv()
        add_into(half.at[i], half.at[i], from_core.at[i])
        if i is not x:
            to_x.start()
    yield
    to_x.wait_recv()
    add_into(out, half.at[x], from_x)
    yield
    to_x.wait_send()
    for i in range(X):
        to_core(i).wait_send()


def share_sems():
    return [DMA((2,)), DMA((X, 2)), DMA((1,))]


def share_flow(place, own, out, sems, ready=None):
    x_sem, core_sem, local = sems
    r, x, c = place.r, place.x, place.c
    if ready is not None:
        yield
        ready()
    keep = pltpu.make_async_copy(own, out.at[r], local.at[0])
    to_x = remote(own, out.at[r], x_sem.at[0], x_sem.at[1], place.over_x)
    near = remote(own, out.at[r], core_sem.at[x, 0], core_sem.at[x, 1], place.over_core)
    far = remote(
        out.at[place.rx], out.at[place.rx], core_sem.at[1 - x, 0], core_sem.at[1 - x, 1],
        place.over_core,
    )
    to_x.start()
    near.start()
    keep.start()
    yield
    to_x.wait_recv()
    far.start()
    yield
    keep.wait()
    to_x.wait_send()
    near.wait()
    far.wait()


def exchange_sems():
    return [DMA((4, 2)), DMA((1,))]


def exchange_flow(place, part, out, sems):
    sem, local = sems
    r = place.r
    keep = pltpu.make_async_copy(part.at[r], out.at[r], local.at[0])
    keep.start()
    copies = []
    for k in (2, 3, 1):
        to = (r + k) % 4
        copies.append(
            remote(part.at[to], out.at[r], sem.at[k, 0], sem.at[k, 1], (place.s, to))
        )
        copies[-1].start()
    yield
    keep.wait()
    for copy in copies:
        copy.wait()


def greet_replicas(place):
    barrier = pltpu.get_barrier_semaphore()
    for k in range(1, 4):
        pl.semaphore_signal(
            barrier, inc=1, device_id=(place.s, (place.r + k) % 4), device_id_type=MESH
        )
    pl.semaphore_wait(barrier, 3)


def spread_sems(B):
    return [DMA((A,)), DMA((A, 2)), DMA((B, A, 2)), DMA((1,))]


def spread_flow(place, own, out, sems):
    line_recv, line_send, side, local = sems
    a, b, B = place.a, place.b, place.B
    keep = pltpu.make_async_copy(own, out.at[a, b], local.at[0])
    keep.start()

    def to_line(src, block, way):
        return remote(
            src, out.at[block, b], line_send.at[block, 0 if way > 0 else 1],
            line_recv.at[block], place.line(a + way),
        )

    def to_side(src, block, k):
        return remote(
            src, out.at[block, b], side.at[k, block, 0], side.at[k, block, 1],
            place.side((b + k) % B),
        )

    @pl.when(a < A - 1)
    def _():
        to_line(own, a, 1).start()

    @pl.when(a > 0)
    def _():
        to_line(own, a, -1).start()

    for k in range(1, B):
        to_side(own, a, k).start()
    for step in range(1, A):
        yield
        for way in (1, -1):
            block = a - way * step

            @pl.when((block >= 0) & (block < A))
            def _():
                src = out.at[block, b]
                to_line(src, block, way).wait_recv()

                @pl.when((a + way >= 0) & (a + way < A))
                def _():
                    to_line(src, block, way).start()

                for k in range(1, B):
                    to_side(src, block, k).start()

    yield
    keep.wait()
    for block in range(A):
        src = out.at[block, b]

        @pl.when((a < A - 1) & (block <= a))
        def _():
            to_line(src, block, 1).wait_send()

        @pl.when((a > 0) & (block >= a))
        def _():
            to_line(src, block, -1).wait_send()

        for k in range(1, B):
            to_side(src, block, k).wait()


def columns_sems(B):
    return [DMA((A, 2)), DMA((B, A, 2)), DMA((1,))]


def columns_flow(place, own, out, sems):
    line, side, local = sems
    a, b, B = place.a, place.b, place.B
    keep = pltpu.make_async_copy(own.at[a], out.at[a, b], local.at[0])
    keep.start()

    def to_line(k):
        to = (a + k) % A
        return remote(own.at[to], out.at[a, b], line.at[k, 0], line.at[k, 1], place.line(to))

    def to_side(src, block, k):
        return remote(
            src, out.at[block, b], side.at[k, block, 0], side.at[k, block, 1],
            place.side((b + k) % B),
        )

    for k in range(1, A):
        to_line(k).start()
    for k in range(1, B):
        to_side(own.at[a], a, k).start()
    for k in (1, 3, 2):
        yield
        to_line(k).wait_recv()
        block = (a + A - k) % A
        for j in range(1, B):
            to_side(out.at[block, b], block, j).start()
    yield
    keep.wait()
    for k in range(1, A):
        to_line(k).wait_send()
    for block in range(A):
        for k in range(1, B):
            to_side(out.at[block, b], block, k).wait()


def sides_sems(B):
    return [DMA((B, 2)), DMA((1,))]


def sides_flow(place, own, out, sems):
    side, local = sems
    b, B = place.b, place.B
    keep = pltpu.make_async_copy(own, out.at[b], local.at[0])
    keep.start()
    copies = [
        remote(own, out.at[b], side.at[k, 0], side.at[k, 1], place.side((b + k) % B))
        for k in range(1, B)
    ]
    for copy in copies:
        copy.start()
    yield
    keep.wait()
    for copy in copies:
        copy.wait()


def gather_scratch(B, rows, width):
    block = (rows, width)
    return [
        pltpu.VMEM((A,) + block, bf),
        pltpu.VMEM((B - 1, A) + block, bf),
        pltpu.VMEM((2, A) + block, bf),
        DMA((A,)), DMA((B, A, 2)), DMA((2, A, 2)),
    ]


def gather_flow(place, part, keep_at, scratch):
    sums, from_side, landed, load_sem, side_sem, line_sem = scratch
    b, B = place.b, place.B

    def load(d):
        return pltpu.make_async_copy(part.at[d, b], sums.at[d], load_sem.at[d])

    def to_side(k, d):
        to = (b + k) % B
        return remote(
            part.at[d, to], from_side.at[k - 1, d], side_sem.at[k, d, 0], side_sem.at[k, d, 1],
            place.side(to),
        )

    for d in shrink_order:
        load(d).start()
        for k in range(1, B):
            to_side(k, d).start()

    def ready(d):
        load(d).wait()
        for k in range(1, B):
            to_side(k, d).wait_recv()
            add_into(sums.at[d], sums.at[d], from_side.at[k - 1, d])

    yield from line_reduce(place, sums, landed, line_sem, ready, keep_at)
    for d in range(A):
        for k in range(1, B):
            to_side(k, d).wait_send()


def owners_scratch(B, rows, width):
    block = (rows, width)
    return [
        pltpu.VMEM((A,) + block, bf), pltpu.VMEM((B - 1, A) + block, bf),
        DMA((A,)), DMA((B, A, 2)), DMA((A, 2)), DMA((1,)),
    ]


def owners_flow(place, part, out, scratch):
    sums, from_side, load_sem, side_sem, line_sem, local = scratch
    a, b, B = place.a, place.b, place.B

    def load(d):
        return pltpu.make_async_copy(part.at[d, b], sums.at[d], load_sem.at[d])

    def to_side(k, d):
        to = (b + k) % B
        return remote(
            part.at[d, to], from_side.at[k - 1, d], side_sem.at[k, d, 0], side_sem.at[k, d, 1],
            place.side(to),
        )

    def to_line(k):
        to = (a + k) % A
        return remote(sums.at[to], out.at[a], line_sem.at[k, 0], line_sem.at[k, 1], place.line(to))

    for k in (1, 3, 2, 0):
        d = (a + k) % A
        load(d).start()
        for j in range(1, B):
            to_side(j, d).start()
    for k in (1, 3, 2, 0):
        yield
        d = (a + k) % A
        load(d).wait()
        for j in range(1, B):
            to_side(j, d).wait_recv()
            add_into(sums.at[d], sums.at[d], from_side.at[j - 1, d])
        if k:
            to_line(k).start()
    keep = pltpu.make_async_copy(sums.at[a], out.at[a], local.at[0])
    keep.start()
    yield
    keep.wait()
    for k in range(1, A):
        to_line(k).wait()
    for d in range(A):
        for j in range(1, B):
            to_side(j, d).wait_send()


ANY = pl.BlockSpec(memory_space=pl.ANY)
VMEM = pl.BlockSpec(memory_space=pltpu.VMEM)


def call(kernel, name, collective_id, outs, out_specs, scratch, args, in_specs):
    return pl.pallas_call(
        kernel,
        out_shape=outs,
        in_specs=in_specs,
        out_specs=out_specs,
        scratch_shapes=scratch,
        name=name,
        compiler_params=pltpu.CompilerParams(
            collective_id=collective_id, has_side_effects=True, vmem_limit_bytes=60 * 2**20
        ),
    )(*args)


def shape(*dims, dtype=bf):
    return jax.ShapeDtypeStruct(dims, dtype)


def split_refs(refs, *sizes):
    found, at = [], 0
    for size in sizes:
        found.append(refs[at : at + size])
        at += size
    return found


def first_gather(B, w4, tokens, d_down):
    def kernel(w4_in, tok_in, d_in, w4_out, tok_out, d_out, *refs):
        place = Place(B)
        s1, s2, s3 = split_refs(refs, 4, 3, 6)
        greet(place, True, True, True)
        run_flows(
            [
                share_flow(place, tok_in, tok_out, s2),
                spread_flow(place, w4_in, w4_out, s1),
                widen_flow(place, d_in, d_out, s3),
            ]
        )

    return call(
        kernel, "first_gather", 1,
        [
            shape(A, B, *w4.shape), shape(4, *tokens.shape), shape(4, A, *d_down.shape),
        ],
        [ANY] * 3,
        spread_sems(B) + share_sems() + widen_sems(),
        [w4, tokens, d_down],
        [ANY] * 3,
    )


def ffn_gather(B, normed_two, gate_up, down):
    def kernel(n_in, g_in, w_in, n_out, g_out, w_out, *refs):
        place = Place(B)
        s1, s2, s3 = split_refs(refs, 6, 3, 2)
        greet(place, True, True, True)
        run_flows(
            [
                widen_flow(place, n_in, n_out, s1),
                columns_flow(place, g_in, g_out, s2),
                sides_flow(place, w_in, w_out, s3),
            ]
        )

    return call(
        kernel, "ffn_gather", 2,
        [
            shape(4, A, *normed_two.shape), shape(A, B, *gate_up.shape[1:]),
            shape(B, *down.shape),
        ],
        [ANY] * 3,
        widen_sems() + columns_sems(B) + sides_sems(B),
        [normed_two, gate_up, down],
        [ANY] * 3,
    )


def share(name, collective_id, own):
    def kernel(own_in, out, *sems):
        place = Place(1)
        place.s = lax.axis_index("shard")
        greet(place, False, False, True)
        run_flows([share_flow(place, own_in, out, sems)])

    return call(
        kernel, name, collective_id, shape(4, *own.shape), ANY, share_sems(), [own], [ANY]
    )


def exchange(name, collective_id, part):
    def kernel(part_in, out, *sems):
        place = Place(1)
        greet_replicas(place)
        run_flows([exchange_flow(place, part_in, out, sems)])

    return call(
        kernel, name, collective_id, shape(*part.shape), ANY, exchange_sems(), [part], [ANY]
    )


def fold(name, collective_id, part):
    def kernel(part_in, out, *refs):
        place = Place(1)
        greet(place, False, False, True)
        run_flows([fold_flow(place, part_in, out, refs)])

    return call(
        kernel, name, collective_id, shape(*part.shape[1:]), VMEM,
        fold_scratch(*part.shape[1:]), [part], [ANY],
    )


def ffn_reduce(B, d_n2, g_gate_up, g_down):
    rows, width = d_n2.shape[2:]
    gu_rows, gu_cols = g_gate_up.shape[2:]
    d_rows = g_down.shape[1]

    def kernel(d_in, gu_in, gd_in, d_out, gu_out, gd_out, *refs):
        place = Place(B)
        s1, s2, s3 = split_refs(refs, 8, 6, 6)
        greet(place, True, True, True)
        run_flows(
            [
                shrink_flow(place, d_in, d_out, s1),
                owners_flow(place, gu_in, gu_out, s2),
                side_sum_flow(place, gd_in, gd_out, s3),
            ]
        )

    return call(
        kernel, "ffn_reduce", 3,
        [shape(rows, width), shape(A, gu_rows, gu_cols), shape(4, d_rows, width)],
        [VMEM, ANY, ANY],
        shrink_scratch(rows, width) + owners_scratch(B, gu_rows, gu_cols)
        + side_sum_scratch(B, d_rows, width),
        [d_n2, g_gate_up, g_down],
        [ANY] * 3,
    )


def side_sum_scratch(B, rows, width):
    return [
        pltpu.VMEM((rows, width), bf), pltpu.VMEM((B - 1, rows, width), bf),
        DMA((1,)), DMA((B, 2)), share_sems_pack(), DMA((1,)),
    ]


def share_sems_pack():
    return DMA((X + 1, 2))


def side_sum_flow(place, part, out, scratch):
    sums, from_side, load_sem, side_sem, share_sem, local = scratch
    b, B = place.b, place.B
    load = pltpu.make_async_copy(part.at[b], sums, load_sem.at[0])
    load.start()

    def to_side(k):
        to = (b + k) % B
        return remote(
            part.at[to], from_side.at[k - 1], side_sem.at[k, 0], side_sem.at[k, 1], place.side(to)
        )

    for k in range(1, B):
        to_side(k).start()
    yield
    yield
    load.wait()
    for k in range(1, B):
        to_side(k).wait_recv()
        add_into(sums, sums, from_side.at[k - 1])
    yield from share_flow(
        place, sums, out, [share_sem.at[X], share_sem, local]
    )
    for k in range(1, B):
        to_side(k).wait_send()


def last_reduce(B, S, g4, d_normed, ffn_out, g_gate_up, gains):
    g_rows, width = g4.shape[2:]
    rows = d_normed.shape[1]

    def kernel(g4_in, dn_in, f_in, gu_in, gain_in, g4_out, dn_out, f_out, gu_out, gain_out, *refs):
        place = Place(B)
        s1, s2, s3, s4, s5, s6 = split_refs(refs, 6, 6, 8, 3, 3, 2)
        own = s1[0]
        greet(place, everyone=(S, 4))

        def total():
            yield from gather_flow(place, g4_in, lambda ref: None, s1)
            yield from share_flow(place, own.at[place.a], g4_out, s4)

        run_flows(
            [
                total(),
                gains_flow(place, S, gain_in, gain_out, s6),
                fold_flow(place, dn_in, dn_out, s2),
                share_flow(place, gu_in, gu_out, s5),
                shrink_flow(place, f_in, f_out, s3),
            ]
        )

    return call(
        kernel, "last_reduce", 4,
        [
            shape(4, g_rows, width), shape(rows, width), shape(rows, width),
            shape(4, *g_gate_up.shape), shape(4 * S, *gains.shape[1:], dtype=f32),
        ],
        [ANY, VMEM, VMEM, ANY, ANY],
        gather_scratch(B, g_rows, width) + fold_scratch(rows, width)
        + shrink_scratch(rows, width) + share_sems() + share_sems() + gains_sems(S),
        [g4, d_normed, ffn_out, g_gate_up, gains],
        [ANY] * 5,
    )


def gains_sems(S):
    return [DMA((4 * S, 2)), DMA((1,))]


def gains_flow(place, S, part, out, sems):
    sem, local = sems
    keep = pltpu.make_async_copy(part.at[place.s], out.at[0], local.at[0])
    keep.start()

    def copy(k):
        to = lax.rem(place.s + k // 4, S)
        return remote(
            part.at[to], out.at[k], sem.at[k, 0], sem.at[k, 1], (to, lax.rem(place.r + k % 4, 4))
        )

    def begin(k, carry):
        copy(k).start()
        return carry

    def end(k, carry):
        copy(k).wait()
        return carry

    lax.fori_loop(1, 4 * S, begin, 0)
    yield
    yield
    yield
    yield
    keep.wait()
    lax.fori_loop(1, 4 * S, end, 0)


def product(left_side, right_side):
    return jnp.dot(left_side, right_side, preferred_element_type=f32)


def against(left_side, right_side):
    return lax.dot_general(
        left_side, right_side, (((1,), (1,)), ((), ())), preferred_element_type=f32
    )


def across(left_side, right_side):
    return lax.dot_general(
        left_side, right_side, (((0,), (0,)), ((), ())), preferred_element_type=f32
    )


def rms_norm(values, gain_vec):
    factor = lax.rsqrt(jnp.mean(values * values, axis=-1, keepdims=True) + norm_eps)
    return (factor, (values * factor * gain_vec).astype(bf))


def norm_back(values, factor, gain_vec, upstream):
    scaled = upstream * gain_vec
    inner_mean = jnp.mean(scaled * values, axis=-1, keepdims=True)
    return factor * scaled - values * (factor * factor * factor) * inner_mean


def angle_tables(places, head_dim):
    halves = head_dim // 2
    frequency = jnp.exp(
        jnp.arange(halves).astype(f32) * (-2.0 * math.log(rope_base) / head_dim)
    )
    angles = frequency[:, None] * places.astype(f32)[None, :]
    return (jnp.cos(angles)[None], jnp.sin(angles)[None])


def rotate(values, cosine, sine_table):
    halves = values.shape[1] // 2
    former = values[:, :halves]
    latter = values[:, halves:]
    return jnp.concatenate(
        [former * cosine - latter * sine_table, latter * cosine + former * sine_table], axis=1
    )


def body(
    tokens,
    attn_gain,
    w_query,
    w_key,
    w_value,
    w_out,
    ffn_gain,
    w_gate,
    w_up,
    w_down,
    seq_ids,
    block_ids,
    cotangent,
):
    S = lax.axis_size("shard")
    R = lax.axis_size("replica")
    B = S // A
    rows, width = tokens.shape
    group = rows * R
    head_dim = width // H
    heads = H // R
    wcols = width // R
    ff = w_gate.shape[1]
    sub = ff // (S * R)
    pad = -(-sub // 16) * 16
    fcols = B * pad
    wrows = width // S
    r = lax.axis_index("replica")
    score_scale = 1.0 / math.sqrt(head_dim)

    earlier = jnp.sum((seq_ids[None, :] < seq_ids[:, None]).astype(jnp.int32), axis=1)
    places = jnp.arange(group, dtype=jnp.int32) - earlier
    cosine, sine_table = angle_tables(places, head_dim)
    allowed = (seq_ids[None, :] == seq_ids[:, None]) & (block_ids[None, :] <= block_ids[:, None])

    gains = lax.all_gather(jnp.stack([attn_gain, ffn_gain]), "shard", axis=1, tiled=True)
    gain_one, gain_two = gains[0].astype(f32), gains[1].astype(f32)
    own_cols = lambda w: lax.dynamic_slice_in_dim(w, r * wcols, wcols, 1)
    w4 = jnp.concatenate([own_cols(w) for w in (w_query, w_key, w_value, w_out)], axis=1)
    upstream = cotangent.astype(f32)
    w4, tokens_group, d_down = first_gather(
        B, w4, tokens, (branch_scale * upstream).astype(bf)
    )
    w4 = w4.reshape(width, 4 * wcols)
    wqkv, wo = w4[:, : 3 * wcols], w4[:, 3 * wcols :]
    tokens_group = tokens_group.reshape(group, width).astype(f32)
    d_down = d_down.reshape(R * A * rows, width)

    def own_hidden(w):
        w = w.reshape(wrows, A, B, R, sub)
        w = lax.dynamic_index_in_dim(w, r, 3, keepdims=False)
        w = jnp.pad(w, ((0, 0), (0, 0), (0, 0), (0, pad - sub)))
        return w.transpose(1, 0, 2, 3).reshape(A, wrows, fcols)

    gate_up = jnp.concatenate([own_hidden(w_gate), own_hidden(w_up)], axis=1)
    down = lax.dynamic_index_in_dim(w_down.reshape(R, sub, width), r, 0, keepdims=False)
    down = jnp.pad(down, ((0, pad - sub), (0, 0)))

    inputs = tokens.astype(f32)
    factor_group, normed = rms_norm(tokens_group, gain_one)
    qkv = lax.dot_general(wqkv, normed, (((0,), (1,)), ((), ())), preferred_element_type=f32)
    heads_of = lambda v: v.reshape(heads, head_dim, group)
    queries = rotate(heads_of(qkv[:wcols]), cosine, sine_table).astype(bf)
    keys = rotate(heads_of(qkv[wcols : 2 * wcols]), cosine, sine_table).astype(bf)
    values = heads_of(qkv[2 * wcols :].astype(bf))
    scores = (
        jnp.einsum("hdt,hdk->htk", queries, keys, preferred_element_type=f32) * score_scale
    )
    scores = jnp.where(allowed[None], scores, masked_score)
    probs = jax.nn.softmax(scores, axis=-1)
    probs_low = probs.astype(bf)
    mixed = (
        jnp.einsum("htk,hdk->hdt", probs_low, values, preferred_element_type=f32)
        .reshape(wcols, group)
        .astype(bf)
    )
    mixed_all = share("mixed_share", 5, mixed).reshape(width, group)
    proj = across(mixed_all, wo).astype(bf)
    proj = exchange("proj_exchange", 6, proj.reshape(R, rows, wcols))
    proj = proj.transpose(1, 0, 2).reshape(rows, width)
    after_attn = inputs + branch_scale * proj.astype(f32)
    factor_two, normed_two = rms_norm(after_attn, gain_two)

    n2, gate_up, down_w = ffn_gather(B, normed_two, gate_up, down)
    n2 = n2.reshape(R * A * rows, width)
    gate_up = gate_up.reshape(S, 2, wrows, fcols)
    gate_w = gate_up[:, 0].reshape(width, fcols)
    up_w = gate_up[:, 1].reshape(width, fcols)
    down_w = down_w.reshape(fcols, width)
    gate_pre = product(n2, gate_w)
    up_proj = product(n2, up_w)
    sig = jax.nn.sigmoid(gate_pre)
    hidden = (gate_pre * sig * up_proj).astype(bf)
    d_hidden = against(d_down, down_w)
    d_gate = (d_hidden * up_proj * sig * (1.0 + gate_pre * (1.0 - sig))).astype(bf)
    d_up = (d_hidden * gate_pre * sig).astype(bf)
    d_n2 = (against(d_gate, gate_w) + against(d_up, up_w)).astype(bf)
    g_gate = across(n2, d_gate).astype(bf).reshape(A, B, wrows, fcols)
    g_up = across(n2, d_up).astype(bf).reshape(A, B, wrows, fcols)
    g_down = across(hidden, d_down).astype(bf).reshape(B, pad, width)
    d_n2, g_gate_up, g_down = ffn_reduce(
        B, d_n2.reshape(R, A, rows, width), jnp.concatenate([g_gate, g_up], axis=2), g_down
    )
    grad_down = g_down[:, :sub].astype(f32).reshape(R * sub, width)
    ffn_out = product(hidden, down_w).astype(bf).reshape(R, A, rows, width)

    d_n2 = d_n2.astype(f32)
    gain_two_part = jnp.sum(d_n2 * after_attn * factor_two, axis=0)
    d_after = upstream + norm_back(after_attn, factor_two, gain_two, d_n2)
    d_proj = (branch_scale * d_after).astype(bf)
    d_proj = exchange(
        "d_proj_exchange", 7, d_proj.reshape(rows, R, wcols).transpose(1, 0, 2)
    ).reshape(group, wcols)
    d_mixed = against(wo, d_proj).astype(bf).reshape(R, wcols, group)
    d_mixed = heads_of(fold("d_mixed_fold", 8, d_mixed))

    d_probs = jnp.einsum("hdt,hdk->htk", d_mixed, values, preferred_element_type=f32)
    d_scores = (
        probs * (d_probs - jnp.sum(d_probs * probs, axis=-1, keepdims=True))
    ).astype(bf)
    d_queries = (
        jnp.einsum("htk,hdk->hdt", d_scores, keys, preferred_element_type=f32) * score_scale
    )
    d_keys = (
        jnp.einsum("htk,hdt->hdk", d_scores, queries, preferred_element_type=f32) * score_scale
    )
    d_values = jnp.einsum("htk,hdt->hdk", probs_low, d_mixed, preferred_element_type=f32)
    d_qkv = jnp.concatenate(
        [
            rotate(d_queries, cosine, -sine_table).reshape(wcols, group).astype(bf),
            rotate(d_keys, cosine, -sine_table).reshape(wcols, group).astype(bf),
            d_values.reshape(wcols, group).astype(bf),
        ],
        axis=0,
    )
    d_normed = lax.dot_general(
        d_qkv, wqkv, (((0,), (1,)), ((), ())), preferred_element_type=f32
    )
    gain_one_part = jnp.sum(d_normed * tokens_group * factor_group, axis=0)
    g_qkv = lax.dot_general(
        normed, d_qkv, (((0,), (1,)), ((), ())), preferred_element_type=f32
    )
    g4 = jnp.concatenate([g_qkv, product(mixed_all, d_proj)], axis=1).astype(bf)
    gain_parts = jnp.stack(
        [gain_one_part.reshape(S, wrows), gain_two_part.reshape(S, wrows)], axis=1
    )
    g4, d_normed, ffn_out, g_gate_up, gain_sums = last_reduce(
        B, S, g4.reshape(A, B, wrows, 4 * wcols), d_normed.astype(bf).reshape(R, rows, width),
        ffn_out, g_gate_up, gain_parts,
    )
    result = after_attn + branch_scale * ffn_out.astype(f32)
    factor_one, _ = rms_norm(inputs, gain_one)
    grad_tokens = d_after + norm_back(inputs, factor_one, gain_one, d_normed.astype(f32))
    g4 = g4.reshape(R, wrows, 4, wcols).transpose(2, 1, 0, 3).reshape(4, wrows, width)
    g4 = g4.astype(f32)
    g_gate_up = g_gate_up.reshape(R, A, 2, wrows, B, pad)[..., :sub]
    g_gate_up = g_gate_up.transpose(2, 3, 1, 4, 0, 5).reshape(2, wrows, ff).astype(f32)
    gain_sums = jnp.sum(gain_sums, axis=0)
    return (
        result.astype(bf),
        grad_tokens.astype(bf),
        gain_sums[0],
        g4[0],
        g4[1],
        g4[2],
        g4[3],
        gain_sums[1],
        g_gate_up[0],
        g_gate_up[1],
        grad_down,
    )


def solution(mesh):
    split = P(("shard", "replica"), None)
    vec, mat = P("shard"), P("shard", None)
    in_specs = (split, vec, mat, mat, mat, mat, vec, mat, mat, mat, vec, vec, split)
    out_specs = (split, split, vec, mat, mat, mat, mat, vec, mat, mat, mat)
    return jax.shard_map(body, mesh=mesh, in_specs=in_specs, out_specs=out_specs, check_vma=False)
```

time: 1630 us -> 1150 us (0.71)
  waiting for transfers between devices: 1030 us -> 0 us
  Pallas kernels: 0 us -> 696 us
  blocking collectives: 236 us -> 19.7 us
  local copies, waits for them, and re-layouts: 124 us -> 203 us
    pallas_call x0 -> x8, Pallas kernels: none -> 696 us  [call(): pl.pallas_call(kernel, out_shape=outs, in_specs=in_specs, out_specs=out_s...]
    all_gather x14 -> x0, waiting for transfers between devices: 540 us -> none  [the longest x1 150 us: body(): w4 = lax.all_gather(w4, 'shard', axis=0, tiled=True)]
    reduce_scatter x7 -> x0, waiting for transfers between devices: 292 us -> none  [the longest x2 146 us: shrink(): v = lax.psum_scatter(v, 'replica', scatter_dimension=0, tiled=True)]
    unnamed x25 -> x0, waiting for transfers between devices: 199 us -> none
    all_to_all x6 -> x0, blocking collectives: 173 us -> none  [the longest x2 98.1 us: spread(): w = lax.all_to_all(w, 'shard', 0, 0, axis_index_groups=a_groups, tiled=True)]
    slice x3 -> x10, local copies, waits for them, and re-layouts: 0.96 us -> 49.7 us  [the longest x2 24.5 us: body(): g4[3]]
    psum x1 -> x0, blocking collectives: 42.6 us -> none  [body(): lax.psum(jnp.stack([gain_one_part, gain_two_part]), ('shard', 'replica'))]
    reshape x5 -> x8, local copies, waits for them, and re-layouts: 24 us -> 63.7 us  [the longest x2 32.2 us: own_hidden(): w = w.reshape(wrows, A, B, R, sub)]
  transfers between devices with their start and end apart: 23 -> 0, of which waited for: 20 -> 0; matrix products, arithmetic and copies ran while one was open for 15% -> 0% of each run, Pallas kernels for 0% -> 0%
where the time goes in v2:
time: 1150 us; the launch traced here: 1130 us
  Pallas kernels  696 us (61%)
  local copies, waits for them, and re-layouts  203 us (18%)
  matrix products  138 us (12%)
  other arithmetic  68.7 us (6%)
  blocking collectives  19.7 us (2%)
    pallas_call x8, Pallas kernels, call(): pl.pallas_call(kernel, out_shape=outs, in_specs=in_specs, out_specs=out_s...  696 us
    dot_general x4, matrix products, against(): lax.dot_general(left_side, right_side, (((1,), (1,)), ((), ())), preferre...  35.1 us
    reshape x2, local copies, waits for them, and re-layouts, own_hidden(): w = w.reshape(wrows, A, B, R, sub)  32.2 us
    dot_general x4, matrix products, product(): return jnp.dot(left_side, right_side, preferred_element_type=f32)  28.2 us
    slice x2, local copies, waits for them, and re-layouts, body(): g4[3]  24.5 us

profile of v2, /device:TPU:9, one launch (start us, length us, event | category | flops | bytes accessed | tf_op | source)
XLA Modules:
  0.0 1127.3 jit_solution(3223667425862640703)
XLA Ops:
  3.0 19.7 %all-gather = bf16[8,288,2]{1,2,0:T(2,128)(2,1)S(1)} all-gather(bf16[1,288,2]{1,2,0:T(2,128)(2,1)S(1)} %maximum_bitcast_fusion), channel_id=1, replica_groups=mesh['shard'=8,'replica'=4] {'shard'}, dimensions={0}, use_global_device_ids=true | all-gather | bytes 10368 | tf_op jit(solution)/shard_map/all_gather | solution.py:953
  36.5 17.2 %reshape.360 = bf16[288,4,2,4,180]{4,3,2,1,0:T(4,128)(2,1)} reshape(bf16[288,5760]{1,0:T(8,128)(2,1)} %param.20) | data formatting | bytes 6635520 | tf_op jit(solution)/shard_map/reshape | solution.py:967
  53.8 15.0 %reshape.362 = bf16[288,4,2,4,180]{4,3,2,1,0:T(4,128)(2,1)} reshape(bf16[288,5760]{1,0:T(8,128)(2,1)S(1)} %copy-done.9) | data formatting | bytes 6635520 | tf_op jit(solution)/shard_map/reshape | solution.py:967
  68.7 10.1 constant_dynamic-slice_fusion
  78.9 6.0 copy.86
  92.4 128.6 %first_gather.1 = (bf16[4,2,288,2304]{3,2,1,0:T(8,128)(2,1)}, bf16[4,128,2304]{2,1,0:T(8,128)(2,1)}, bf16[4,4,128,2304]{3,2,1,0:T(8,128)(2,1)}) custom-call(bf16[288,2304]{1,0:T(8,128)(2,1)} %concatenate.33.w4_in, bf16[128,2304]{1,0:T(8,128)(2,1)} %tok_in.1, bf16[128,2304]{1,0:T(8,128)(2,1)} %fusion.35.d_in), custom_call_target="tpu_custom_call" | custom-call | tf_op jit(solution)/shard_map/first_gather/pallas_call | solution.py:625
  226.5 6.9 fusion.3
  235.0 5.6 fusion.64
  240.7 5.4 fusion.24
  246.1 21.5 %mixed_share.1 = bf16[4,576,512]{2,1,0:T(8,128)(2,1)} custom-call(bf16[576,512]{1,0:T(8,128)(2,1)} %bitcast.144), custom_call_target="tpu_custom_call" | custom-call | tf_op jit(solution)/shard_map/mixed_share/pallas_call | solution.py:625
  267.6 5.3 fusion.30
  274.0 11.2 proj_exchange.1
  288.7 113.3 %ffn_gather.1 = (bf16[4,4,128,2304]{3,2,1,0:T(8,128)(2,1)}, bf16[4,2,576,384]{3,2,1,0:T(8,128)(2,1)}, bf16[2,192,2304]{2,1,0:T(8,128)(2,1)}) custom-call(bf16[128,2304]{1,0:T(8,128)(2,1)} %multiply_convert_fusion.5.n_in, bf16[4,576,384]{2,1,0:T(8,128)(2,1)} %pad_maximum_fusion.2.g_in, bf16[192,2304]{1,0:T(8,128)(2,1)} %pad.13.w_in), custom_call_target="tpu_custom_call" | custom-call | tf_op jit(solution)/shard_map/ffn_gather/pallas_call | solution.py:625
  402.0 9.4 fusion.65
  411.9 6.9 fusion.66
  418.7 8.5 multiply_convert_fusion.1
  427.3 5.3 convolution_convert_fusion.3
  432.6 5.2 convolution_convert_fusion.5
  437.8 5.5 convolution_convert_fusion.4
  446.5 7.4 convolution_convert_fusion
  453.9 9.1 fusion.67
  463.0 11.3 %add_convert_fusion = bf16[2048,2304]{1,0:T(8,128)(2,1)} fusion(f32[2048,2304]{1,0:T(8,128)} %fusion.67, bf16[2048,384]{1,0:T(8,128)(2,1)S(1)} %get-tuple-element.57, bf16[2304,384]{1,0:T(8,128)(2,1)S(1)} %bitcast.112), kind=kOutput, calls=%fused_computation.2 | convolution fusion | flops 3633315840 | bytes 31653888 | tf_op jit(solution)/shard_map/dot_general | solution.py:877
  474.3 156.9 %ffn_reduce.1 = (bf16[128,2304]{1,0:T(8,128)(2,1)}, bf16[4,576,384]{2,1,0:T(8,128)(2,1)}, bf16[4,192,2304]{2,1,0:T(8,128)(2,1)}) custom-call(bf16[4,4,128,2304]{3,2,1,0:T(8,128)(2,1)} %bitcast.106, bf16[4,2,576,384]{3,2,1,0:T(8,128)(2,1)} %pad_maximum_fusion.1.gu_in, bf16[2,192,2304]{2,1,0:T(8,128)(2,1)} %bitcast.133), custom_call_target="tpu_custom_call" | custom-call | tf_op jit(solution)/shard_map/ffn_reduce/pallas_call | solution.py:625
  636.4 11.6 %d_proj_exchange.1 = bf16[4,128,576]{2,1,0:T(8,128)(2,1)} custom-call(bf16[4,128,576]{2,1,0:T(8,128)(2,1)} %bitcast.124), custom_call_target="tpu_custom_call" | custom-call | tf_op jit(solution)/shard_map/d_proj_exchange/pallas_call | solution.py:625
  648.0 5.5 convolution_convert_fusion.6
  653.4 5.3 convolution_convert_fusion.2
  658.7 18.7 %d_mixed_fold.1 = bf16[576,512]{1,0:T(8,128)(2,1)} custom-call(bf16[4,576,512]{2,1,0:T(8,128)(2,1)} %bitcast.129), custom_call_target="tpu_custom_call" | custom-call | tf_op jit(solution)/shard_map/d_mixed_fold/pallas_call | solution.py:625
  677.4 6.4 fusion.27
  687.1 5.2 reshape.385
  692.3 7.8 multiply_reduce_fusion
  700.1 11.3 multiply_convert_fusion
  718.1 9.9 fusion.10
  728.8 6.8 convolution_convert_fusion.1
  735.6 7.0 pad_maximum_fusion.g4_in
  742.7 234.0 %last_reduce.1 = (bf16[4,288,2304]{2,1,0:T(8,128)(2,1)}, bf16[128,2304]{1,0:T(8,128)(2,1)}, bf16[128,2304]{1,0:T(8,128)(2,1)}, bf16[4,4,576,384]{3,2,1,0:T(8,128)(2,1)}, f32[32,2,288]{2,1,0:T(2,128)}) custom-call(bf16[4,2,288,2304]{3,2,1,0:T(8,128)(2,1)} %pad_maximum_fusion.g4_in, bf16[4,128,2304]{2,1,0:T(8,128)(2,1)} %bitcast.125, ...), custom_call_target="tpu_custom_call" | custom-call | tf_op jit(solution)/shard_map/last_reduce/pallas_call | solution.py:625
  981.8 20.6 %reshape.378 = bf16[4,4,2,288,2,192]{5,4,3,2,1,0:T(2,128)(2,1)} reshape(bf16[4,4,576,384]{3,2,1,0:T(8,128)(2,1)} %get-tuple-element.37) | data formatting | bytes 14155776 | tf_op jit(solution)/shard_map/reshape | solution.py:1073
  1002.3 22.8 %convert_bitcast_fusion = f32[2,288,4,2,4,180]{5,4,3,2,1,0:T(4,128)S(1)} fusion(bf16[4,4,2,288,2,180]{5,4,3,2,1,0:T(2,128)(2,1)} %bitcast.108), kind=kLoop, calls=%fused_computation.1 | loop fusion | flops 3317760 | bytes 19906560 | tf_op jit(solution)/shard_map/convert_element_type | solution.py:1074
  1025.1 9.8 fusion.60
  1034.9 11.0 squeeze.47
  1045.9 11.0 squeeze.46
  1056.9 13.5 %reshape.386 = f32[4,288,4,576]{3,2,1,0:T(4,128)} reshape(bf16[4,288,2304]{2,1,0:T(8,128)(2,1)} %get-tuple-element.36) | data formatting | bytes 15925248 | tf_op jit(solution)/shard_map/convert_element_type | solution.py:1072
  1070.4 21.0 %fusion.61 = (f32[1,288,4,576]{3,0,1,2:T(1,128)S(1)}, f32[1,288,4,576]{3,0,1,2:T(1,128)}, f32[1,288,4,576]{3,0,1,2:T(1,128)}, f32[1,288,4,576]{3,0,1,2:T(1,128)S(1)}) fusion(f32[4,288,4,576]{3,0,1,2:T(4,128)} %bitcast.107), kind=kLoop, calls=%fused_computation.133 | loop fusion | bytes 21233664 | tf_op jit(solution)/shard_map/slice | solution.py:1083
  1094.9 4.5 squeeze.44
  1099.4 5.3 copy.96
  1104.7 4.5 squeeze.43
  1109.3 5.3 copy.95
  1114.6 4.5 squeeze.42
  1122.6 4.5 squeeze.41
  (159 shorter events, 66.6 us)
Async XLA Ops:
  36.5 17.3 %copy-start.9 = (bf16[288,5760]{1,0:T(8,128)(2,1)S(1)}, bf16[288,5760]{1,0:T(8,128)(2,1)}, u32[]{:S(2)}) copy-start(bf16[288,5760]{1,0:T(8,128)(2,1)} %param.21) | copy-start | bytes 9953284
  89.8 1.2 copy-start.7
  92.4 131.0 %copy-start.29 = (f32[2304]{0:T(1024)S(1)}, f32[2304]{0:T(1024)}, u32[]{:S(2)}) copy-start(f32[2304]{0:T(1024)} %get-tuple-element.44) | copy-start | bytes 27652
  221.0 2.4 copy-start.1
  223.4 0.6 copy-start.34
  233.5 7.1 copy-start.23
  233.5 0.9 copy-start.21
  233.5 1.0 copy-start.27
  233.8 1.2 copy-start.28
  235.0 5.7 copy-start.12
  235.0 5.7 copy-start.14
  235.0 5.7 copy-start.16
  235.0 5.7 copy-start.18
  240.7 451.7 %copy-start.33 = (f32[9,512]{1,0:T(8,128)}, f32[9,512]{1,0:T(8,128)S(1)}, u32[]{:S(2)}) copy-start(f32[9,512]{1,0:T(8,128)S(1)} %get-tuple-element.85) | copy-start | bytes 55300
  286.4 1.1 copy-start.3
  287.7 345.6 %copy-start.36 = (f32[128]{0:T(128)}, f32[128]{0:T(128)S(1)}, u32[]{:S(2)}) copy-start(f32[128]{0:T(128)S(1)} %get-tuple-element.83) | copy-start | bytes 1540
  402.0 9.5 copy-start.8
  402.0 9.8 copy-start.40
  411.8 15.4 %slice-start = ((s8[9437184]{0:T(1024)(128)(4,1)}), s8[4194304]{0:T(1024)(128)(4,1)S(1)}, s32[]{:S(2)}) async-start(s8[9437184]{0:T(1024)(128)(4,1)} %bitcast.151), calls=%async_computation | async-start | bytes 8388608
  411.9 15.4 %slice-start.1 = ((s8[9437184]{0:T(1024)(128)(4,1)}), s8[4194304]{0:T(1024)(128)(4,1)S(1)}, s32[]{:S(2)}) async-start(s8[9437184]{0:T(1024)(128)(4,1)} %bitcast.151), calls=%async_computation.1 | async-start | bytes 8388608
  418.7 8.5 slice-start.2
  427.2 5.3 copy-start.43
  443.3 2.2 copy-start.41
  443.3 3.2 copy-start.44
  474.3 159.1 %copy-start.6 = (bf16[128,2304]{1,0:T(8,128)(2,1)S(1)}, bf16[128,2304]{1,0:T(8,128)(2,1)}, u32[]{:S(2)}) copy-start(bf16[128,2304]{1,0:T(8,128)(2,1)} %param.25) | copy-start | bytes 1769476
  633.4 3.0 copy-start.38
  648.0 5.5 copy-start.20
  677.4 6.4 copy-start.10
  687.1 5.2 copy-start.24
  687.1 5.2 copy-start.25
  700.1 11.3 copy-start.17
  700.1 11.3 copy-start.19
  711.4 4.0 copy-start
  711.4 4.0 copy-start.13
  711.4 4.0 copy-start.15
  715.4 0.9 copy-start.22
  715.4 0.9 copy-start.26
  716.3 1.7 copy-start.2
  716.3 1.7 copy-start.35
  716.4 1.8 copy-start.42
  718.1 10.0 copy-start.32
  728.8 6.8 copy-start.11
  742.6 234.0 %copy-start.4 = (bf16[128,2304]{1,0:T(8,128)(2,1)S(1)}, bf16[128,2304]{1,0:T(8,128)(2,1)}, u32[]{:S(2)}) copy-start(bf16[128,2304]{1,0:T(8,128)(2,1)} %tok_in.1) | copy-start | bytes 1769476
  742.6 234.0 %copy-start.30 = (f32[2304]{0:T(1024)S(1)}, f32[2304]{0:T(1024)}, u32[]{:S(2)}) copy-start(f32[2304]{0:T(1024)} %get-tuple-element.44) | copy-start | bytes 27652
  742.6 235.5 %copy-start.5 = (bf16[128,2304]{1,0:T(8,128)(2,1)S(1)}, bf16[128,2304]{1,0:T(8,128)(2,1)}, u32[]{:S(2)}) copy-start(bf16[128,2304]{1,0:T(8,128)(2,1)} %get-tuple-element.31) | copy-start | bytes 1769476
  742.6 235.5 %copy-start.37 = (f32[128]{0:T(128)S(1)}, f32[128]{0:T(128)}, u32[]{:S(2)}) copy-start(f32[128]{0:T(128)} %copy-done.36) | copy-start | bytes 1540
  742.6 235.5 %copy-start.39 = (f32[128]{0:T(128)S(1)}, f32[128]{0:T(128)}, u32[]{:S(2)}) copy-start(f32[128]{0:T(128)} %copy-done.38) | copy-start | bytes 1540
  978.1 3.0 copy-start.31

commit v3 on v2

--- a/solution.py
+++ b/solution.py
@@ -98,14 +98,33 @@
     lax.fori_loop(0, rows // tile, step, 0)
 
 
-def run_flows(flows):
-    flows = list(flows)
-    while flows:
-        for flow in list(flows):
+def run_flows(flows, turns=()):
+    ended = set()
+
+    def step(at):
+        if at not in ended:
             try:
-                next(flow)
+                next(flows[at])
             except StopIteration:
-                flows.remove(flow)
+                ended.add(at)
+
+    for at in turns:
+        step(at)
+    while len(ended) < len(flows):
+        for at in range(len(flows)):
+            step(at)
+
+
+def halves(rows):
+    return 2 if rows % 32 == 0 else 1
+
+
+def piece(ref, at, h, parts):
+    if parts == 1:
+        return ref.at[at]
+    rows = ref.shape[-2] // parts
+    index = at if isinstance(at, tuple) else (at,)
+    return ref.at[index + (pl.ds(h * rows, rows),)]
 
 
 def widen_sems():
@@ -197,104 +216,124 @@
 
 def shrink_scratch(rows, width):
     block = (rows, width)
+    P_ = halves(rows)
     return [
         pltpu.VMEM((X, A) + block, bf),
         pltpu.VMEM((X, A) + block, bf),
         pltpu.VMEM((A,) + block, bf),
-        pltpu.VMEM((2, A) + block, bf),
-        DMA((X, A)), DMA((X, A, 2)), DMA((A, 2)), DMA((2, A, 2)),
+        pltpu.VMEM((A + 1,) + block, bf),
+        DMA((X, A, P_)), DMA((X, A, P_, 2)), DMA((A, P_, 2)), DMA((2, A, P_, 2)),
     ]
 
 
 shrink_order = (3, 0, 2, 1)
 
 
-def line_reduce(place, sums, landed, sems, ready, final):
+def line_reduce(place, sums, landed, sems, parts, ready, final):
     a = place.a
 
-    def hop(d, way):
+    def hop(d, h, way):
         at = 0 if way > 0 else 1
         return remote(
-            sums.at[d], landed.at[at, d], sems.at[at, d, 0], sems.at[at, d, 1],
-            place.line(a + way),
-        )
-
-    for d in shrink_order:
-        yield
-        ready(d)
-        for way in (1, -1):
-            @pl.when((d - a) * way > 0)
-            def _():
-                @pl.when((a - way >= 0) & (a - way < A))
-                def _():
-                    hop(d, way).wait_recv()
-                    add_into(sums.at[d], sums.at[d], landed.at[0 if way > 0 else 1, d])
-
-                hop(d, way).start()
-
-    yield
-    for d in range(A):
+            piece(sums, d, h, parts), piece(landed, d + 1 - at, h, parts), sems.at[at, d, h, 0],
+            sems.at[at, d, h, 1], place.line(a + way),
+        )
+
+    def take(d, h, way):
+        @pl.when((a - way >= 0) & (a - way < A))
+        def _():
+            hop(d, h, way).wait_recv()
+            here = piece(sums, d, h, parts)
+            add_into(here, here, piece(landed, d + (way > 0), h, parts))
+
+    def finish(d):
         @pl.when(d == a)
         def _():
+            for h in range(parts):
+                take(d, h, 1)
+                take(d, h, -1)
+                final(d, h)
+
+    for i, d in enumerate(shrink_order):
+        for h in range(parts):
+            yield
+            ready(d, h)
             for way in (1, -1):
-                @pl.when((a - way >= 0) & (a - way < A))
+                @pl.when((d - a) * way > 0)
                 def _():
-                    hop(d, way).wait_recv()
-                    add_into(sums.at[d], sums.at[d], landed.at[0 if way > 0 else 1, d])
-
-            final(sums.at[d])
-
-        for way in (1, -1):
-            @pl.when((d - a) * way > 0)
-            def _():
-                hop(d, way).wait_send()
+                    take(d, h, way)
+                    hop(d, h, way).start()
+
+        if i:
+            yield
+            finish(shrink_order[i - 1])
+    yield
+    finish(shrink_order[-1])
+    yield
+    for d in range(A):
+        for h in range(parts):
+            for way in (1, -1):
+                @pl.when((d - a) * way > 0)
+                def _():
+                    hop(d, h, way).wait_send()
 
 
 def shrink_flow(place, part, out, scratch):
     half, from_core, from_x, landed, load_sem, core_sem, x_sem, line_sem = scratch
     x, c = place.x, place.c
-
-    def load(i, d):
-        return pltpu.make_async_copy(part.at[i * X + c, d], half.at[i, d], load_sem.at[i, d])
-
-    def to_core(i, d):
-        return remote(
-            part.at[i * X + 1 - c, d], from_core.at[i, d], core_sem.at[i, d, 0],
-            core_sem.at[i, d, 1], place.over_core,
-        )
-
-    def to_x(d):
-        return remote(
-            half.at[1 - x, d], from_x.at[d], x_sem.at[d, 0], x_sem.at[d, 1], place.over_x
-        )
-
-    for j in range(X):
-        for d in shrink_order:
-            i = 1 - x if j == 0 else x
-            load(i, d).start()
-            to_core(i, d).start()
-    for d in shrink_order:
+    parts = halves(out.shape[0])
+
+    def load(i, d, h):
+        return pltpu.make_async_copy(
+            piece(part, (i * X + c, d), h, parts), piece(half, (i, d), h, parts),
+            load_sem.at[i, d, h],
+        )
+
+    def to_core(i, d, h):
+        return remote(
+            piece(part, (i * X + 1 - c, d), h, parts), piece(from_core, (i, d), h, parts),
+            core_sem.at[i, d, h, 0], core_sem.at[i, d, h, 1], place.over_core,
+        )
+
+    def to_x(d, h):
+        return remote(
+            piece(half, (1 - x, d), h, parts), piece(from_x, d, h, parts), x_sem.at[d, h, 0],
+            x_sem.at[d, h, 1], place.over_x,
+        )
+
+    def merge(i, d, h):
+        load(i, d, h).wait()
+        to_core(i, d, h).wait_recv()
+        here = piece(half, (i, d), h, parts)
+        add_into(here, here, piece(from_core, (i, d), h, parts))
+
+    every = [(d, h) for d in shrink_order for h in range(parts)]
+    for i in (1 - x, x):
+        for d, h in every:
+            load(i, d, h).start()
+            to_core(i, d, h).start()
+    for d, h in every:
         yield
-        load(1 - x, d).wait()
-        to_core(1 - x, d).wait_recv()
-        add_into(half.at[1 - x, d], half.at[1 - x, d], from_core.at[1 - x, d])
-        to_x(d).start()
-
-    def ready(d):
-        load(x, d).wait()
-        to_core(x, d).wait_recv()
-        add_into(half.at[x, d], half.at[x, d], from_core.at[x, d])
-        to_x(d).wait_recv()
-        add_into(half.at[x, d], half.at[x, d], from_x.at[d])
-
-    def final(ref):
-        out[...] = ref[...]
-
-    yield from line_reduce(place, half.at[x], landed, line_sem, ready, final)
-    for d in range(A):
-        to_x(d).wait_send()
+        merge(1 - x, d, h)
+        to_x(d, h).start()
+
+    def ready(d, h):
+        merge(x, d, h)
+        to_x(d, h).wait_recv()
+        here = piece(half, (x, d), h, parts)
+        add_into(here, here, piece(from_x, d, h, parts))
+
+    rows = out.shape[0] // parts
+
+    def final(d, h):
+        at = pl.ds(h * rows, rows)
+        out[at, :] = half[x, d, at, :]
+
+    yield from line_reduce(place, half.at[x], landed, line_sem, parts, ready, final)
+    for d, h in every:
+        to_x(d, h).wait_send()
         for i in range(X):
-            to_core(i, d).wait_send()
+            to_core(i, d, h).wait_send()
 
 
 def fold_scratch(rows, width):
@@ -527,43 +566,88 @@
 
 def gather_scratch(B, rows, width):
     block = (rows, width)
+    P_ = halves(rows)
     return [
         pltpu.VMEM((A,) + block, bf),
         pltpu.VMEM((B - 1, A) + block, bf),
-        pltpu.VMEM((2, A) + block, bf),
-        DMA((A,)), DMA((B, A, 2)), DMA((2, A, 2)),
+        pltpu.VMEM((A + 1,) + block, bf),
+        DMA((A, P_)), DMA((B, A, P_, 2)), DMA((2, A, P_, 2)),
+        DMA((P_, 2)), DMA((X, P_, 2)), DMA((P_,)),
     ]
 
 
-def gather_flow(place, part, keep_at, scratch):
-    sums, from_side, landed, load_sem, side_sem, line_sem = scratch
-    b, B = place.b, place.B
-
-    def load(d):
-        return pltpu.make_async_copy(part.at[d, b], sums.at[d], load_sem.at[d])
-
-    def to_side(k, d):
+def gather_flow(place, part, out, scratch):
+    sums, from_side, landed, load_sem, side_sem, line_sem, x_sem, core_sem, local = scratch
+    b, B, r, x = place.b, place.B, place.r, place.x
+    parts = halves(out.shape[1])
+
+    def load(d, h):
+        return pltpu.make_async_copy(
+            piece(part, (d, b), h, parts), piece(sums, d, h, parts), load_sem.at[d, h]
+        )
+
+    def to_side(k, d, h):
         to = (b + k) % B
         return remote(
-            part.at[d, to], from_side.at[k - 1, d], side_sem.at[k, d, 0], side_sem.at[k, d, 1],
-            place.side(to),
+            piece(part, (d, to), h, parts), piece(from_side, (k - 1, d), h, parts),
+            side_sem.at[k, d, h, 0], side_sem.at[k, d, h, 1], place.side(to),
         )
 
     for d in shrink_order:
-        load(d).start()
+        for h in range(parts):
+            load(d, h).start()
+            for k in range(1, B):
+                to_side(k, d, h).start()
+
+    def ready(d, h):
+        load(d, h).wait()
         for k in range(1, B):
-            to_side(k, d).start()
-
-    def ready(d):
-        load(d).wait()
-        for k in range(1, B):
-            to_side(k, d).wait_recv()
-            add_into(sums.at[d], sums.at[d], from_side.at[k - 1, d])
-
-    yield from line_reduce(place, sums, landed, line_sem, ready, keep_at)
-    for d in range(A):
-        for k in range(1, B):
-            to_side(k, d).wait_send()
+            to_side(k, d, h).wait_recv()
+            here = piece(sums, d, h, parts)
+            add_into(here, here, piece(from_side, (k - 1, d), h, parts))
+
+    def keep(src, h):
+        return pltpu.make_async_copy(src, piece(out, r, h, parts), local.at[h])
+
+    def to_x(src, h):
+        return remote(src, piece(out, r, h, parts), x_sem.at[h, 0], x_sem.at[h, 1], place.over_x)
+
+    def near(src, h):
+        return remote(
+            src, piece(out, r, h, parts), core_sem.at[x, h, 0], core_sem.at[x, h, 1],
+            place.over_core,
+        )
+
+    def far(h):
+        src = piece(out, place.rx, h, parts)
+        return remote(
+            src, src, core_sem.at[1 - x, h, 0], core_sem.at[1 - x, h, 1], place.over_core
+        )
+
+    def final(d, h):
+        src = piece(sums, d, h, parts)
+        to_x(src, h).start()
+        near(src, h).start()
+        keep(src, h).start()
+
+    yield from line_reduce(place, sums, landed, line_sem, parts, ready, final)
+    yield
+    for h in range(parts):
+        src = piece(out, r, h, parts)
+        to_x(src, h).wait_recv()
+        far(h).start()
+    yield
+    for h in range(parts):
+        src = piece(out, r, h, parts)
+        keep(src, h).wait()
+        to_x(src, h).wait_send()
+        near(src, h).wait()
+    for d in shrink_order:
+        for h in range(parts):
+            for k in range(1, B):
+                to_side(k, d, h).wait_send()
+    for h in range(parts):
+        far(h).wait()
 
 
 def owners_scratch(B, rows, width):
@@ -647,28 +731,124 @@
     return found
 
 
-def first_gather(B, w4, tokens, d_down):
-    def kernel(w4_in, tok_in, d_in, w4_out, tok_out, d_out, *refs):
+def select(rows, cols, shift, at, width):
+    row = lax.broadcasted_iota(jnp.int32, (rows, cols), 0)
+    col = lax.broadcasted_iota(jnp.int32, (rows, cols), 1)
+    j = col - at
+    return jnp.where((row - shift == j) & (j >= 0) & (j < width), 1.0, 0.0).astype(bf)
+
+
+def first_gather(B, weights, gates, w_down, gains, tokens, d_down):
+    wrows, width = weights[0].shape
+    ff = gates[0].shape[1]
+    wcols = width // 4
+    sub = ff // (A * B * 4)
+    pad = -(-sub // 16) * 16
+    fcols = B * pad
+    wide = 384
+    span = -(-wcols // 128) * 128
+    pair = 2 * wcols
+
+    def kernel(*refs):
+        w_in, g_in, (wd_in, gain_in, tok_in, d_in), outs, scratch, refs = split_refs(
+            refs, 4, 2, 4, 6, 7, 100
+        )
+        w4_out, gain_out, tok_out, d_out, gu_out, dn_out = outs
+        w_all, g_all, wd_all, own4, gu_own, dn_own, load = scratch
+        s1, s2, s3, s4 = split_refs(refs, 4, 4, 3, 6)
         place = Place(B)
-        s1, s2, s3 = split_refs(refs, 4, 3, 6)
+        r = place.r
+        loads = [pltpu.make_async_copy(w, w_all.at[i], load.at[i]) for i, w in enumerate(w_in)]
+        loads += [
+            pltpu.make_async_copy(w, g_all.at[i], load.at[4 + i]) for i, w in enumerate(g_in)
+        ]
+        loads.append(pltpu.make_async_copy(wd_in, wd_all, load.at[6]))
+        for copy in loads:
+            copy.start()
+        start = pl.multiple_of(r * wcols // 128 * 128, 128)
+        shift = r * wcols - start
+        for i in range(2):
+            total = jnp.zeros((wrows, pair), f32)
+            for j in range(2):
+                loads[2 * i + j].wait()
+                total += jnp.dot(
+                    w_all[2 * i + j, :, pl.ds(start, span)],
+                    select(span, pair, shift, j * wcols, wcols), preferred_element_type=f32,
+                )
+            own4[:, i * pair : (i + 1) * pair] = total.astype(bf)
         greet(place, True, True, True)
+
+        def pack():
+            for i in range(2):
+                loads[4 + i].wait()
+            loads[6].wait()
+            yield
+
+            def one(n, carry):
+                i, block = n // A, n % A
+                total = jnp.zeros((wrows, fcols), f32)
+                for j in range(B):
+                    first = ((block * B + j) * 4 + r) * sub
+                    at = pl.multiple_of(jnp.minimum(first // 128 * 128, ff - wide), 128)
+                    total += jnp.dot(
+                        g_all[i, :, pl.ds(at, wide)],
+                        select(wide, fcols, first - at, j * pad, sub),
+                        preferred_element_type=f32,
+                    )
+                gu_own[block, i] = total.astype(bf)
+                return carry
+
+            lax.fori_loop(0, 2 * A, one, 0)
+            row = lax.broadcasted_iota(jnp.int32, (pad, ff // (A * B)), 0)
+            col = lax.broadcasted_iota(jnp.int32, (pad, ff // (A * B)), 1)
+            pick = jnp.where((col - r * sub == row) & (row < sub), 1.0, 0.0).astype(bf)
+            tile = 768
+
+            def down(n, carry):
+                at = pl.ds(pl.multiple_of(n * tile, tile), tile)
+                dn_own[:, at] = jnp.dot(
+                    pick, wd_all[:, at], preferred_element_type=f32
+                ).astype(bf)
+                return carry
+
+            lax.fori_loop(0, width // tile, down, 0)
+            out = [
+                pltpu.make_async_copy(gu_own, gu_out, load.at[0]),
+                pltpu.make_async_copy(dn_own, dn_out, load.at[1]),
+            ]
+            for copy in out:
+                copy.start()
+            yield
+            for copy in out:
+                copy.wait()
+
         run_flows(
             [
-                share_flow(place, tok_in, tok_out, s2),
-                spread_flow(place, w4_in, w4_out, s1),
-                widen_flow(place, d_in, d_out, s3),
-            ]
+                spread_flow(place, own4, w4_out, s1),
+                share_flow(place, tok_in, tok_out, s3),
+                spread_flow(place, gain_in, gain_out, s2),
+                widen_flow(place, d_in, d_out, s4),
+                pack(),
+            ],
+            (0, 1, 2, 3, 4, 1, 4),
         )
 
     return call(
         kernel, "first_gather", 1,
         [
-            shape(A, B, *w4.shape), shape(4, *tokens.shape), shape(4, A, *d_down.shape),
+            shape(A, B, wrows, 4 * wcols), shape(A, B, *gains.shape, dtype=f32),
+            shape(4, *tokens.shape), shape(4, A, *d_down.shape),
+            shape(A, 2, wrows, fcols), shape(pad, width),
         ],
-        [ANY] * 3,
-        spread_sems(B) + share_sems() + widen_sems(),
-        [w4, tokens, d_down],
-        [ANY] * 3,
+        [ANY] * 6,
+        [
+            pltpu.VMEM((4, wrows, width), bf), pltpu.VMEM((2, wrows, ff), bf),
+            pltpu.VMEM(w_down.shape, bf), pltpu.VMEM((wrows, 4 * wcols), bf),
+            pltpu.VMEM((A, 2, wrows, fcols), bf), pltpu.VMEM((pad, width), bf), DMA((7,)),
+        ]
+        + spread_sems(B) + spread_sems(B) + share_sems() + widen_sems(),
+        [*weights, *gates, w_down, gains, tokens, d_down],
+        [ANY] * 10,
     )
 
 
@@ -747,7 +927,8 @@
                 shrink_flow(place, d_in, d_out, s1),
                 owners_flow(place, gu_in, gu_out, s2),
                 side_sum_flow(place, gd_in, gd_out, s3),
-            ]
+            ],
+            (0, 1, 2) + (0,) * 8 + (0, 0, 1, 0, 0, 0, 1, 0, 0, 0, 1, 0, 0, 0, 1, 2, 2, 0, 1, 2),
         )
 
     return call(
@@ -799,40 +980,144 @@
         to_side(k).wait_send()
 
 
-def last_reduce(B, S, g4, d_normed, ffn_out, g_gate_up, gains):
-    g_rows, width = g4.shape[2:]
+def last_reduce(B, S, g4, d_normed, g_gate_up, g_down, gains, ff):
+    wrows, width = g4.shape[2], g4.shape[3]
     rows = d_normed.shape[1]
-
-    def kernel(g4_in, dn_in, f_in, gu_in, gain_in, g4_out, dn_out, f_out, gu_out, gain_out, *refs):
+    wcols = width // 4
+    sub = ff // (S * 4)
+    pad = -(-sub // 16) * 16
+    fcols = B * pad
+    wide = 384
+    span = -(-wcols // 128) * 128
+    pair = 2 * wcols
+    drows = ff // S
+
+    def kernel(*refs):
+        ins, outs, own, refs = split_refs(refs, 5, 9, 6, 100)
+        g4_in, dn_in, gu_in, gd_in, gain_in = ins
+        dn_out, gain_out = outs[:2]
+        g4_outs, gu_outs, gd_out = outs[2:6], outs[6:8], outs[8]
+        g4_all, gu_all, gd_all, stage, stage_down, sem = own
+        s1, s2, s3, s4 = split_refs(refs, 9, 6, 3, 2)
         place = Place(B)
-        s1, s2, s3, s4, s5, s6 = split_refs(refs, 6, 6, 8, 3, 3, 2)
-        own = s1[0]
         greet(place, everyone=(S, 4))
 
-        def total():
-            yield from gather_flow(place, g4_in, lambda ref: None, s1)
-            yield from share_flow(place, own.at[place.a], g4_out, s4)
+        def lay_down():
+            load = pltpu.make_async_copy(gd_in, gd_all, sem.at[0])
+            load.start()
+            yield
+            load.wait()
+            row = lax.broadcasted_iota(jnp.int32, (drows, 4 * pad), 0)
+            col = lax.broadcasted_iota(jnp.int32, (drows, 4 * pad), 1)
+            pick = (col % pad < sub) & (col // pad * sub + col % pad == row)
+            pick = jnp.where(pick, 1.0, 0.0).astype(bf)
+
+            def copy(n):
+                at = pl.ds(pl.multiple_of(n * wide, 128), wide)
+                return pltpu.make_async_copy(
+                    stage_down.at[n % 2], gd_out.at[:, at], sem.at[1 + n % 2]
+                )
+
+            def one(n, carry):
+                @pl.when(n >= 2)
+                def _():
+                    copy(n - 2).wait()
+
+                at = pl.ds(pl.multiple_of(n * wide, 128), wide)
+                stage_down[n % 2] = jnp.dot(pick, gd_all[:, at], preferred_element_type=f32)
+                copy(n).start()
+                return carry
+
+            count = width // wide
+            lax.fori_loop(0, count, one, 0)
+            yield
+            for n in range(count - 2, count):
+                copy(n).wait()
+
+        def lay_gate_up():
+            def one(n, carry):
+                i, block = n % 2, n // 2
+                total = jnp.zeros((wrows, wide), f32)
+                for t in range(-(-wide // sub) + 1):
+                    m = block * wide // sub + t
+                    inside = jnp.where(m < 4 * S, sub, 0)
+                    m = jnp.minimum(m, 4 * S - 1)
+                    s = m // 4
+                    total += jnp.dot(
+                        gu_all[m % 4, s // B, i],
+                        select(fcols, wide, s % B * pad, m * sub - block * wide, inside),
+                        preferred_element_type=f32,
+                    )
+                stage[i, :, pl.ds(pl.multiple_of(block * wide, 128), wide)] = total
+                return carry
+
+            count = 2 * (ff // wide)
+            cuts = [count * k // 5 for k in range(6)]
+            for k in range(5):
+                lax.fori_loop(cuts[k], cuts[k + 1], one, 0)
+                yield
+            copies = [
+                pltpu.make_async_copy(stage.at[i], gu_outs[i], sem.at[3 + i]) for i in range(2)
+            ]
+            for copy in copies:
+                copy.start()
+            yield
+            for copy in copies:
+                copy.wait()
 
         run_flows(
             [
-                total(),
-                gains_flow(place, S, gain_in, gain_out, s6),
+                gather_flow(place, g4_in, g4_all, s1),
+                gains_flow(place, S, gain_in, gain_out, s4),
                 fold_flow(place, dn_in, dn_out, s2),
-                share_flow(place, gu_in, gu_out, s5),
-                shrink_flow(place, f_in, f_out, s3),
-            ]
-        )
+                share_flow(place, gu_in, gu_all, s3),
+                lay_down(),
+                lay_gate_up(),
+            ],
+            (0, 1, 2, 3, 4, 2, 4, 0, 2, 0, 0, 0, 0, 3, 3, 3, 5, 0, 5, 0, 5, 0, 5, 0, 5, 0, 5, 0)
+            + (0,) * 10,
+        )
+
+        def lay(n, carry):
+            i, side = n % 4, n // 4
+            at = pl.multiple_of(i * wcols // 128 * 128, 128)
+            total = jnp.zeros((wrows, pair), f32)
+            for c in range(2):
+                total += jnp.dot(
+                    g4_all[side * 2 + c, :, pl.ds(at, span)],
+                    select(span, pair, i * wcols - at, c * wcols, wcols),
+                    preferred_element_type=f32,
+                )
+            to = pl.multiple_of(i % 2 * width + side * pair, 128)
+            stage[i // 2, :, pl.ds(to, pair)] = total
+            return carry
+
+        lax.fori_loop(0, 8, lay, 0)
+        copies = [
+            pltpu.make_async_copy(
+                stage.at[i // 2, :, pl.ds(i % 2 * width, width)], g4_outs[i], sem.at[3 + i]
+            )
+            for i in range(4)
+        ]
+        for copy in copies:
+            copy.start()
+        for copy in copies:
+            copy.wait()
 
     return call(
         kernel, "last_reduce", 4,
+        [shape(rows, width), shape(4 * S, *gains.shape[1:], dtype=f32)]
+        + [shape(wrows, width, dtype=f32)] * 4 + [shape(wrows, ff, dtype=f32)] * 2
+        + [shape(drows, width, dtype=f32)],
+        [VMEM] + [ANY] * 8,
         [
-            shape(4, g_rows, width), shape(rows, width), shape(rows, width),
-            shape(4, *g_gate_up.shape), shape(4 * S, *gains.shape[1:], dtype=f32),
-        ],
-        [ANY, VMEM, VMEM, ANY, ANY],
-        gather_scratch(B, g_rows, width) + fold_scratch(rows, width)
-        + shrink_scratch(rows, width) + share_sems() + share_sems() + gains_sems(S),
-        [g4, d_normed, ffn_out, g_gate_up, gains],
+            pltpu.VMEM((4, wrows, width), bf), pltpu.VMEM((4, A, 2, wrows, fcols), bf),
+            pltpu.VMEM((4 * pad, width), bf), pltpu.VMEM((2, wrows, ff), f32),
+            pltpu.VMEM((2, drows, wide), f32), DMA((7,)),
+        ]
+        + gather_scratch(B, wrows, width) + fold_scratch(rows, width) + share_sems()
+        + gains_sems(S),
+        [g4, d_normed, g_gate_up, g_down, gains],
         [ANY] * 5,
     )
 
@@ -950,28 +1235,18 @@
     cosine, sine_table = angle_tables(places, head_dim)
     allowed = (seq_ids[None, :] == seq_ids[:, None]) & (block_ids[None, :] <= block_ids[:, None])
 
-    gains = lax.all_gather(jnp.stack([attn_gain, ffn_gain]), "shard", axis=1, tiled=True)
-    gain_one, gain_two = gains[0].astype(f32), gains[1].astype(f32)
-    own_cols = lambda w: lax.dynamic_slice_in_dim(w, r * wcols, wcols, 1)
-    w4 = jnp.concatenate([own_cols(w) for w in (w_query, w_key, w_value, w_out)], axis=1)
     upstream = cotangent.astype(f32)
-    w4, tokens_group, d_down = first_gather(
-        B, w4, tokens, (branch_scale * upstream).astype(bf)
-    )
+    w4, gains, tokens_group, d_down, gate_up, down = first_gather(
+        B, [w_query, w_key, w_value, w_out], [w_gate, w_up], w_down,
+        jnp.stack([attn_gain, ffn_gain]).astype(f32), tokens, (branch_scale * upstream).astype(bf),
+    )
+    gains = gains.reshape(S, 2, wrows)
+    gain_one, gain_two = gains[:, 0].reshape(width), gains[:, 1].reshape(width)
     w4 = w4.reshape(width, 4 * wcols)
     wqkv, wo = w4[:, : 3 * wcols], w4[:, 3 * wcols :]
     tokens_group = tokens_group.reshape(group, width).astype(f32)
     d_down = d_down.reshape(R * A * rows, width)
-
-    def own_hidden(w):
-        w = w.reshape(wrows, A, B, R, sub)
-        w = lax.dynamic_index_in_dim(w, r, 3, keepdims=False)
-        w = jnp.pad(w, ((0, 0), (0, 0), (0, 0), (0, pad - sub)))
-        return w.transpose(1, 0, 2, 3).reshape(A, wrows, fcols)
-
-    gate_up = jnp.concatenate([own_hidden(w_gate), own_hidden(w_up)], axis=1)
-    down = lax.dynamic_index_in_dim(w_down.reshape(R, sub, width), r, 0, keepdims=False)
-    down = jnp.pad(down, ((0, pad - sub), (0, 0)))
+    gate_up = gate_up.reshape(A, 2 * wrows, fcols)
 
     inputs = tokens.astype(f32)
     factor_group, normed = rms_norm(tokens_group, gain_one)
@@ -1018,8 +1293,12 @@
     d_n2, g_gate_up, g_down = ffn_reduce(
         B, d_n2.reshape(R, A, rows, width), jnp.concatenate([g_gate, g_up], axis=2), g_down
     )
-    grad_down = g_down[:, :sub].astype(f32).reshape(R * sub, width)
-    ffn_out = product(hidden, down_w).astype(bf).reshape(R, A, rows, width)
+    ffn_out = product(hidden, down_w).astype(bf)
+    ffn_out = lax.psum_scatter(ffn_out, "replica", scatter_dimension=0, tiled=True)
+    ffn_out = lax.psum_scatter(
+        ffn_out, "shard", scatter_dimension=0, tiled=True,
+        axis_index_groups=[[i * B + j for i in range(A)] for j in range(B)],
+    )
 
     d_n2 = d_n2.astype(f32)
     gain_two_part = jnp.sum(d_n2 * after_attn * factor_two, axis=0)
@@ -1061,29 +1340,22 @@
     gain_parts = jnp.stack(
         [gain_one_part.reshape(S, wrows), gain_two_part.reshape(S, wrows)], axis=1
     )
-    g4, d_normed, ffn_out, g_gate_up, gain_sums = last_reduce(
+    d_normed, gain_sums, *g_attn, grad_gate, grad_up, grad_down = last_reduce(
         B, S, g4.reshape(A, B, wrows, 4 * wcols), d_normed.astype(bf).reshape(R, rows, width),
-        ffn_out, g_gate_up, gain_parts,
+        g_gate_up.reshape(A, 2, wrows, fcols), g_down.reshape(R * pad, width), gain_parts, ff,
     )
     result = after_attn + branch_scale * ffn_out.astype(f32)
     factor_one, _ = rms_norm(inputs, gain_one)
     grad_tokens = d_after + norm_back(inputs, factor_one, gain_one, d_normed.astype(f32))
-    g4 = g4.reshape(R, wrows, 4, wcols).transpose(2, 1, 0, 3).reshape(4, wrows, width)
-    g4 = g4.astype(f32)
-    g_gate_up = g_gate_up.reshape(R, A, 2, wrows, B, pad)[..., :sub]
-    g_gate_up = g_gate_up.transpose(2, 3, 1, 4, 0, 5).reshape(2, wrows, ff).astype(f32)
     gain_sums = jnp.sum(gain_sums, axis=0)
     return (
         result.astype(bf),
         grad_tokens.astype(bf),
         gain_sums[0],
-        g4[0],
-        g4[1],
-        g4[2],
-        g4[3],
+        *g_attn,
         gain_sums[1],
-        g_gate_up[0],
-        g_gate_up[1],
+        grad_gate,
+        grad_up,
         grad_down,
     )
 

time: 1150 us -> 924 us (0.80); the launches traced: 1130 us -> 918 us
  local copies, waits for them, and re-layouts: 203 us -> 40.6 us
  Pallas kernels: 696 us -> 669 us
  blocking collectives: 19.7 us -> 0 us
  other arithmetic: 68.7 us -> 49.3 us
  between operations: 1.65 us -> 15.2 us
    reshape x7 -> x0, local copies, waits for them, and re-layouts: 62.6 us -> none  [the longest x2 32.2 us: own_hidden(): w = w.reshape(wrows, A, B, R, sub)]
    slice x7 -> x2, local copies, waits for them, and re-layouts: 48.8 us -> 4 us  [the longest x1 2.52 us: body(): gate_w = gate_up[:, 0].reshape(width, fcols)]
    squeeze x7 -> x0, local copies, waits for them, and re-layouts: 40.1 us -> none  [the longest x1 11 us: body(): g_gate_up[1]]
    pallas_call x8, Pallas kernels: 696 us -> 669 us  [call(): pl.pallas_call(kernel, out_shape=outs, in_specs=in_specs, out_specs=out_s...]
    convert_element_type x1, other arithmetic: 22.8 us -> 0.58 us  [body(): jnp.stack([attn_gain, ffn_gain]).astype(f32)]
    dynamic_slice x5 -> x0, local copies, waits for them, and re-layouts: 21.3 us -> none  [the longest x3 18.3 us: own_hidden(): w = lax.dynamic_index_in_dim(w, r, 3, keepdims=False)]
    all_gather x1 -> x0, blocking collectives: 19.7 us -> none  [body(): lax.all_gather(jnp.stack([attn_gain, ffn_gain]), 'shard', axis=1, tiled=T...]
    unnamed x97 -> x133, local copies, waits for them, and re-layouts: 3.61 us -> 22.5 us
  transfers between devices with their start and end apart: 0 -> 2, of which waited for: 0 -> 0; matrix products, arithmetic and copies ran while one was open for 0% -> 13% of each run, Pallas kernels for 0% -> 42%
where the time goes in v3:
time: 924 us; the launch traced here: 918 us
  Pallas kernels  669 us (72%)
  matrix products  143 us (15%)
  other arithmetic  49.3 us (5%)
  local copies, waits for them, and re-layouts  40.6 us (4%)
  between operations  15.2 us (2%)
    pallas_call x8, Pallas kernels, call(): pl.pallas_call(kernel, out_shape=outs, in_specs=in_specs, out_specs=out_s...  669 us
    dot_general x4, matrix products, against(): lax.dot_general(left_side, right_side, (((1,), (1,)), ((), ())), preferre...  35.7 us
    dot_general x4, matrix products, product(): return jnp.dot(left_side, right_side, preferred_element_type=f32)  27.4 us
    dot_general x4, matrix products, across(): lax.dot_general(left_side, right_side, (((0,), (0,)), ((), ())), preferre...  27 us
    unnamed x133, local copies, waits for them, and re-layouts  22.5 us
  transfers between devices with their start and end apart: 2, of which 0 were waited for; matrix products, arithmetic and copies ran while one was open for 13% of the time, Pallas kernels for 42%

profile of v3, /device:TPU:9, one launch (start us, length us, event | category | flops | bytes accessed | tf_op | source)
XLA Modules:
  0.0 917.8 jit_solution(2456868146370524158)
XLA Ops:
  9.1 2.0 fusion.35.refs_9_
  11.7 130.5 %first_gather.1 = (bf16[4,2,288,2304]{3,2,1,0:T(8,128)(2,1)}, f32[4,2,2,288]{3,2,1,0:T(2,128)}, bf16[4,128,2304]{2,1,0:T(8,128)(2,1)}, bf16[4,4,128,2304]{3,2,1,...) custom-call(bf16[288,2304]{1,0:T(8,128)(2,1)} %refs_0_.1, bf16[288,2304]{1,0:T(8,128)(2,1)} %refs_1_.1, ...), custom_call_target="tpu_custom_call" | custom-call | tf_op jit(solution)/shard_map/first_gather/pallas_call | solution.py:709
  143.7 2.2 fusion.6
  146.0 2.3 fusion.8
  148.3 7.1 fusion.3
  159.4 1.6 fusion.47
  161.0 2.7 subtract_convert_fusion.3
  163.7 8.5 fusion.60
  172.2 5.4 fusion.24
  177.6 20.6 %mixed_share.1 = bf16[4,576,512]{2,1,0:T(8,128)(2,1)} custom-call(bf16[576,512]{1,0:T(8,128)(2,1)} %bitcast.126), custom_call_target="tpu_custom_call" | custom-call | tf_op jit(solution)/shard_map/mixed_share/pallas_call | solution.py:709
  198.2 5.3 fusion.30
  204.5 11.2 %proj_exchange.1 = bf16[4,128,576]{2,1,0:T(8,128)(2,1)} custom-call(bf16[4,128,576]{2,1,0:T(8,128)(2,1)} %bitcast.103), custom_call_target="tpu_custom_call" | custom-call | tf_op jit(solution)/shard_map/proj_exchange/pallas_call | solution.py:709
  215.8 2.3 multiply_bitcast_fusion
  218.0 1.7 copy.35
  221.1 1.7 multiply_reduce_fusion.1
  224.3 116.8 %ffn_gather.1 = (bf16[4,4,128,2304]{3,2,1,0:T(8,128)(2,1)}, bf16[4,2,576,384]{3,2,1,0:T(8,128)(2,1)}, bf16[2,192,2304]{2,1,0:T(8,128)(2,1)}) custom-call(bf16[128,2304]{1,0:T(8,128)(2,1)} %multiply_convert_fusion.5.n_in, bf16[4,576,384]{2,1,0:T(8,128)(2,1)} %bitcast.114, bf16[192,2304]{1,0:T(8,128)(2,1)} %get-tuple-element.36.w_in), custom_call_target="tpu_custom_call" | custom-call | tf_op jit(solution)/shard_map/ffn_gather/pallas_call | solution.py:709
  341.1 2.5 fusion.58
  343.7 9.0 fusion.62
  352.9 6.8 fusion.61
  359.7 8.9 multiply_convert_fusion.1
  369.8 7.4 convolution_convert_fusion
  377.3 2.9 copy.37
  380.1 8.3 convolution_convert_fusion.4
  388.5 8.0 convolution_convert_fusion.5
  396.5 2.2 pad_maximum_fusion.1.gu_in
  398.8 5.5 convolution_convert_fusion.3
  404.2 9.1 fusion.63
  413.4 12.2 %add_convert_fusion = bf16[2048,2304]{1,0:T(8,128)(2,1)} fusion(f32[2048,2304]{1,0:T(8,128)} %fusion.63, bf16[2048,384]{1,0:T(8,128)(2,1)S(1)} %copy-done.9, bf16[2304,384]{1,0:T(8,128)(2,1)S(1)} %bitcast.89), kind=kOutput, calls=%fused_computation.1 | convolution fusion | flops 3633315840 | bytes 31653888 | tf_op jit(solution)/shard_map/dot_general | solution.py:1162
  425.6 131.9 %ffn_reduce.1 = (bf16[128,2304]{1,0:T(8,128)(2,1)}, bf16[4,576,384]{2,1,0:T(8,128)(2,1)}, bf16[4,192,2304]{2,1,0:T(8,128)(2,1)}) custom-call(bf16[4,4,128,2304]{3,2,1,0:T(8,128)(2,1)} %bitcast.86, bf16[4,2,576,384]{3,2,1,0:T(8,128)(2,1)} %pad_maximum_fusion.1.gu_in, bf16[2,192,2304]{2,1,0:T(8,128)(2,1)} %bitcast.115), custom_call_target="tpu_custom_call" | custom-call | tf_op jit(solution)/shard_map/ffn_reduce/pallas_call | solution.py:709
  559.6 1.6 multiply_convert_fusion.4
  562.7 9.9 %d_proj_exchange.1 = bf16[4,128,576]{2,1,0:T(8,128)(2,1)} custom-call(bf16[4,128,576]{2,1,0:T(8,128)(2,1)} %bitcast.104), custom_call_target="tpu_custom_call" | custom-call | tf_op jit(solution)/shard_map/d_proj_exchange/pallas_call | solution.py:709
  572.6 5.5 convolution_convert_fusion.2
  578.0 18.7 %d_mixed_fold.1 = bf16[576,512]{1,0:T(8,128)(2,1)} custom-call(bf16[4,576,512]{2,1,0:T(8,128)(2,1)} %bitcast.109), custom_call_target="tpu_custom_call" | custom-call | tf_op jit(solution)/shard_map/d_mixed_fold/pallas_call | solution.py:709
  596.7 7.2 multiply_reduce_fusion
  604.0 11.3 %multiply_convert_fusion = bf16[9,512,512]{1,2,0:T(8,128)(2,1)} fusion(f32[9,512,512]{1,2,0:T(8,128)} %get-tuple-element.96, f32[9,512]{1,0:T(8,128)S(1)} %get-tuple-element.95, f32[9,512,512]{1,2,0:T(8,128)} %get-tuple-element.94, f32[9,512]{1,0:T(8,128)S(1)} %copy-done.33), kind=kLoop, calls=%fused_computation.4 | loop fusion | flops 9437184 | bytes 23629824 | tf_op jit(solution)/shard_map/convert_element_type | solution.py:1316
  615.3 4.0 convolution_multiply_fusion
  621.9 5.4 fusion.27
  627.4 10.1 %fusion.10 = (f32[2304]{0:T(1024)S(1)}, bf16[512,2304]{1,0:T(8,128)(2,1)}) fusion(bf16[4,128,2304]{2,1,0:T(8,128)(2,1)S(1)} %copy-done.1, f32[512]{0:T(512)S(1)} %copy-done.37, bf16[2304,2304]{1,0:T(8,128)(2,1)} %bitcast.131, bf16[576,512]{1,0:T(8,128)(2,1)S(1)} %bitcast.146, bf16[576,512]{1,0:T(8,128)(2,1)S(1)} %bitcast.124, bf16[576,512]{1,0:T(8,128)(2,1)S(1)} %bitcast.122), kind=kOutput, calls=%fused_computation.21 | convolution fusion | flops 4088067840 | bytes 14756864 | tf_op jit(solution)/shard_map/dot_general | solution.py:1332
  638.2 4.1 convolution_convert_fusion.6
  642.4 4.7 convolution_convert_fusion.1
  647.1 7.0 pad_maximum_fusion.refs_0_
  654.1 229.5 %last_reduce.1 = (bf16[128,2304]{1,0:T(8,128)(2,1)}, f32[32,2,288]{2,1,0:T(2,128)}, f32[288,2304]{1,0:T(8,128)}, f32[288,2304]{1,0:T(8,128)}, f32[288,2304]{1,0:...) custom-call(bf16[4,2,288,2304]{3,2,1,0:T(8,128)(2,1)} %pad_maximum_fusion.refs_, ...), custom_call_target="tpu_custom_call" | custom-call | tf_op jit(solution)/shard_map/last_reduce/pallas_call | solution.py:709
  886.7 3.1 fusion.42
  889.8 1.5 copy.58
  895.5 1.8 copy-done.11
  898.8 3.4 copy.62
  903.7 3.2 copy.63
  907.7 2.8 copy.64
  (172 shorter events, 31.3 us)
Async XLA Ops:
  7.2 614.4 %reduce-scatter.3.cloned.1.call-start = ((), (), s32[]{:S(2)}) async-start(), calls=%async_computation.2 | async-start | bytes 11796480 | tf_op jit(solution)/shard_map/reduce_scatter | solution.py:1297
  163.7 8.5 copy-start.23
  172.2 5.5 copy-start.32
  341.1 11.7 %slice-start.12 = ((s8[9437184]{0:T(1024)(128)(4,1)}), s8[4194304]{0:T(1024)(128)(4,1)S(1)}, s32[]{:S(2)}) async-start(s8[9437184]{0:T(1024)(128)(4,1)} %bitcast.141), calls=%async_computation.16 | async-start | bytes 8388608
  343.7 9.1 copy-start.3
  343.7 9.1 copy-start.5
  343.7 9.1 slice-start.13
  343.7 9.1 slice-start.14
  343.7 16.0 %slice-start.6 = ((s8[9437184]{0:T(1024)(128)(4,1)}), s8[4194304]{0:T(1024)(128)(4,1)S(1)}, s32[]{:S(2)}) async-start(s8[9437184]{0:T(1024)(128)(4,1)} %bitcast.132), calls=%async_computation.10 | async-start | bytes 8388608
  343.7 16.0 %slice-start.7 = ((s8[9437184]{0:T(1024)(128)(4,1)}), s8[4194304]{0:T(1024)(128)(4,1)S(1)}, s32[]{:S(2)}) async-start(s8[9437184]{0:T(1024)(128)(4,1)} %bitcast.132), calls=%async_computation.11 | async-start | bytes 8388608
  352.8 6.9 slice-start.8
  352.9 6.9 copy-start.43
  377.2 509.4 %reduce-scatter.5.cloned.1.call-start = ((), (), s32[]{:S(2)}) async-start(), calls=%async_computation.3 | async-start | bytes 2949120 | tf_op jit(solution)/shard_map/reduce_scatter | solution.py:1298
  380.1 8.3 copy-start.10
  380.1 18.5 %slice-start.9 = ((s8[9437184]{0:T(1024)(128)(4,1)}), s8[4194304]{0:T(1024)(128)(4,1)S(1)}, s32[]{:S(2)}) async-start(s8[9437184]{0:T(1024)(128)(4,1)} %bitcast.135), calls=%async_computation.13 | async-start | bytes 8388608
  380.1 18.5 %slice-start.10 = ((s8[9437184]{0:T(1024)(128)(4,1)}), s8[4194304]{0:T(1024)(128)(4,1)S(1)}, s32[]{:S(2)}) async-start(s8[9437184]{0:T(1024)(128)(4,1)} %bitcast.135), calls=%async_computation.14 | async-start | bytes 8388608
  388.5 10.2 %slice-start.11 = ((s8[9437184]{0:T(1024)(128)(4,1)}), s8[1048576]{0:T(1024)(128)(4,1)S(1)}, s32[]{:S(2)}) async-start(s8[9437184]{0:T(1024)(128)(4,1)} %bitcast.135), calls=%async_computation.15 | async-start | bytes 2097152
  398.8 5.5 copy-start.6
  404.2 9.1 copy-start.4
  404.2 9.1 copy-start.9
  425.6 134.0 %copy-start.8 = (bf16[128,2304]{1,0:T(8,128)(2,1)S(1)}, bf16[128,2304]{1,0:T(8,128)(2,1)}, u32[]{:S(2)}) copy-start(bf16[128,2304]{1,0:T(8,128)(2,1)} %param.25) | copy-start | bytes 1769476
  425.6 134.0 %copy-start.39 = (f32[128]{0:T(128)S(1)}, f32[128]{0:T(128)}, u32[]{:S(2)}) copy-start(f32[128]{0:T(128)} %get-tuple-element.91) | copy-start | bytes 1540
  578.0 18.7 %copy-start.24 = (bf16[576,512]{1,0:T(8,128)(2,1)S(1)}, bf16[576,512]{1,0:T(8,128)(2,1)}, u32[]{:S(2)}) copy-start(bf16[576,512]{1,0:T(8,128)(2,1)} %slice.127) | copy-start | bytes 1769476
  578.0 18.7 %copy-start.33 = (f32[9,512]{1,0:T(8,128)S(1)}, f32[9,512]{1,0:T(8,128)}, u32[]{:S(2)}) copy-start(f32[9,512]{1,0:T(8,128)} %copy-done.32) | copy-start | bytes 55300
  603.9 11.4 %copy-start.18 = (bf16[9,32,512]{2,1,0:T(8,128)(2,1)S(1)}, bf16[9,32,512]{2,1,0:T(8,128)(2,1)}, u32[]{:S(2)}) copy-start(bf16[9,32,512]{2,1,0:T(8,128)(2,1)} %get-tuple-element.76) | copy-start | bytes 884740
  603.9 11.4 %copy-start.19 = (bf16[9,32,512]{2,1,0:T(8,128)(2,1)S(1)}, bf16[9,32,512]{2,1,0:T(8,128)(2,1)}, u32[]{:S(2)}) copy-start(bf16[9,32,512]{2,1,0:T(8,128)(2,1)} %get-tuple-element.77) | copy-start | bytes 884740
  615.3 4.1 copy-start.16
  615.3 4.1 copy-start.17
  621.9 5.4 copy-start.1
  621.9 5.4 copy-start.26
  621.9 5.4 copy-start.37
  627.3 10.2 %copy-start.44 = (bf16[9,64,512]{2,1,0:T(8,128)(2,1)}, bf16[9,64,512]{2,1,0:T(8,128)(2,1)S(1)}, u32[]{:S(2)}) copy-start(bf16[9,64,512]{2,1,0:T(8,128)(2,1)S(1)} %fusion.27) | copy-start | bytes 1769476
  627.4 10.2 %copy-start.31 = (f32[8,1,288]{2,1,0:T(1,128)S(1)}, f32[8,1,288]{2,1,0:T(1,128)}, u32[]{:S(2)}) copy-start(f32[8,1,288]{2,1,0:T(1,128)} %stack_reshape.7) | copy-start | bytes 27652
  627.4 10.9 %copy-start.20 = (bf16[4,128,576]{2,1,0:T(8,128)(2,1)S(1)}, bf16[4,128,576]{2,1,0:T(8,128)(2,1)}, u32[]{:S(2)}) copy-start(bf16[4,128,576]{2,1,0:T(8,128)(2,1)} %d_proj_exchange.1) | copy-start | bytes 1769476
  638.2 4.1 copy-start.15
  638.2 4.1 copy-start.27
  638.2 4.1 copy-start.45
  654.1 231.1 %copy-start.2 = (bf16[128,2304]{1,0:T(8,128)(2,1)S(1)}, bf16[128,2304]{1,0:T(8,128)(2,1)}, u32[]{:S(2)}) copy-start(bf16[128,2304]{1,0:T(8,128)(2,1)} %refs_8_.1) | copy-start | bytes 1769476
  654.1 231.1 %copy-start.30 = (f32[2304]{0:T(1024)S(1)}, f32[2304]{0:T(1024)}, u32[]{:S(2)}) copy-start(f32[2304]{0:T(1024)} %copy-done.29) | copy-start | bytes 27652
  654.1 232.5 %copy-start.7 = (bf16[128,2304]{1,0:T(8,128)(2,1)S(1)}, bf16[128,2304]{1,0:T(8,128)(2,1)}, u32[]{:S(2)}) copy-start(bf16[128,2304]{1,0:T(8,128)(2,1)} %get-tuple-element.41) | copy-start | bytes 1769476
  654.1 232.6 %copy-start.40 = (f32[128]{0:T(128)S(1)}, f32[128]{0:T(128)}, u32[]{:S(2)}) copy-start(f32[128]{0:T(128)} %get-tuple-element.91) | copy-start | bytes 1540
  654.1 232.6 %copy-start.42 = (f32[128]{0:T(128)S(1)}, f32[128]{0:T(128)}, u32[]{:S(2)}) copy-start(f32[128]{0:T(128)} %copy-done.41) | copy-start | bytes 1540
  889.7 4.2 copy-start.12
  892.5 6.4 slice-start.4
  894.0 4.9 slice-start.5
  897.3 4.9 slice-start.2
  898.8 4.8 slice-start.3
  898.8 8.0 slice-start
  (17 other events, 38.0 us)
Sparse Core Ops, SparseCore 0:
  377.4 113.9 reduce-scatter.2
  621.7 55.3 reduce-scatter.4

commit v4 on v1

v4 whole, which is shorter than its diff:
```python
import functools
import math

import jax
import jax.numpy as jnp
from jax import lax
from jax.experimental import pallas as pl
from jax.experimental.pallas import tpu as pltpu
from jax.sharding import PartitionSpec as P

H = 36
A = 4
X = 2

branch_scale = 1.4 / math.sqrt(40.0)
norm_eps = 1e-05
rope_base = 10000.0
masked_score = -1e30
MESH = pl.DeviceIdType.MESH
bf = jnp.bfloat16
f32 = jnp.float32
DMA = pltpu.SemaphoreType.DMA


class Place:
    def __init__(self, B):
        self.B = B
        s, r = lax.axis_index("shard"), lax.axis_index("replica")
        self.s, self.r = s, r
        self.a, self.b = s // B, s % B
        self.x, self.c = r // X, r % X
        self.rx = (1 - self.x) * X + self.c
        self.rc = self.x * X + 1 - self.c

    def line(self, a):
        return (a * self.B + self.b, self.r)

    def side(self, b):
        return (self.a * self.B + b, self.r)

    @property
    def over_x(self):
        return (self.s, self.rx)

    @property
    def over_core(self):
        return (self.s, self.rc)


def greet(place, a_peers=True, b_peers=False, r_peers=True, everyone=None):
    barrier = pltpu.get_barrier_semaphore()

    def signal(device):
        pl.semaphore_signal(barrier, inc=1, device_id=device, device_id_type=MESH)

    if everyone is not None:
        S, R = everyone

        def one(k, carry):
            signal((lax.rem(place.s + k // R, S), lax.rem(place.r + k % R, R)))
            return carry

        lax.fori_loop(1, S * R, one, 0)
        pl.semaphore_wait(barrier, S * R - 1)
        return
    count = 0
    if a_peers:
        for k in range(1, A):
            signal(place.line((place.a + k) % A))
            count += 1
    if b_peers:
        for k in range(1, place.B):
            signal(place.side((place.b + k) % place.B))
            count += 1
    if r_peers:
        for k in range(1, 4):
            signal((place.s, (place.r + k) % 4))
            count += 1
    pl.semaphore_wait(barrier, count)


def remote(src, dst, send, recv, device):
    return pltpu.make_async_remote_copy(
        src_ref=src, dst_ref=dst, send_sem=send, recv_sem=recv, device_id=device,
        device_id_type=MESH,
    )


def add_into(dst, first, second, tile=32):
    rows = dst.shape[0]
    tile = math.gcd(rows, tile) if math.gcd(rows, tile) >= 16 else rows

    def step(i, carry):
        at = pl.ds(pl.multiple_of(i * tile, tile), tile)
        dst[at, :] = (first[at, :].astype(f32) + second[at, :].astype(f32)).astype(dst.dtype)
        return carry

    lax.fori_loop(0, rows // tile, step, 0)


def run_flows(flows, turns=()):
    ended = set()

    def step(at):
        if at not in ended:
            try:
                next(flows[at])
            except StopIteration:
                ended.add(at)

    for at in turns:
        step(at)
    while len(ended) < len(flows):
        for at in range(len(flows)):
            step(at)


def halves(rows):
    return 2 if rows % 32 == 0 else 1


def piece(ref, at, h, parts):
    if parts == 1:
        return ref.at[at]
    rows = ref.shape[-2] // parts
    index = at if isinstance(at, tuple) else (at,)
    return ref.at[index + (pl.ds(h * rows, rows),)]


def widen_sems():
    return [DMA((A,)), DMA((X,)), DMA((A, 2)), DMA((A, 2)), DMA((X, A, 2)), DMA((1,))]


def widen_flow(place, own, out, sems):
    line_recv, _, line_send, over_x, over_core, local = sems
    a, x, c = place.a, place.x, place.c
    keep = pltpu.make_async_copy(own, out.at[x, a, c], local.at[0])
    keep.start()

    def to_line(src, block, way):
        at = 0 if way > 0 else 1
        return remote(
            src, out.at[x, block, c], line_send.at[block, at], line_recv.at[block],
            place.line(a + way),
        )

    def to_x(src, block):
        return remote(
            src, out.at[x, block, c], over_x.at[block, 0], over_x.at[block, 1], place.over_x
        )

    def to_core(src, side, block):
        return remote(
            src, out.at[side, block, c], over_core.at[side, block, 0],
            over_core.at[side, block, 1], place.over_core,
        )

    @pl.when(a < A - 1)
    def _():
        to_line(own, a, 1).start()

    @pl.when(a > 0)
    def _():
        to_line(own, a, -1).start()

    to_x(own, a).start()
    to_core(own, x, a).start()

    def pass_x(k):
        for ok, block in ((a - k >= 0, a - k), (a + k < A, a + k)) if k else ((None, a),):
            def go():
                src = out.at[1 - x, block, c]
                to_x(src, block).wait_recv()
                to_core(src, 1 - x, block).start()

            go() if ok is None else pl.when(ok)(go)

    for k in range(1, A):
        yield
        for way in (1, -1):
            block = a - way * k

            @pl.when((block >= 0) & (block < A))
            def _():
                src = out.at[x, block, c]
                to_line(src, block, way).wait_recv()

                @pl.when((a + way >= 0) & (a + way < A))
                def _():
                    to_line(src, block, way).start()

                to_x(src, block).start()
                to_core(src, x, block).start()

        yield
        pass_x(k - 1)
    yield
    pass_x(A - 1)
    yield
    keep.wait()
    for block in range(A):
        src = out.at[x, block, c]

        @pl.when((a < A - 1) & (block <= a))
        def _():
            to_line(src, block, 1).wait_send()

        @pl.when((a > 0) & (block >= a))
        def _():
            to_line(src, block, -1).wait_send()

        to_x(src, block).wait_send()
        for side in range(X):
            to_core(src, side, block).wait()


def shrink_scratch(rows, width):
    block = (rows, width)
    P_ = halves(rows)
    return [
        pltpu.VMEM((X, A) + block, bf),
        pltpu.VMEM((X, A) + block, bf),
        pltpu.VMEM((A,) + block, bf),
        pltpu.VMEM((A + 1,) + block, bf),
        DMA((X, A, P_)), DMA((X, A, P_, 2)), DMA((A, P_, 2)), DMA((2, A, P_, 2)),
    ]


def far_first(a, i):
    inner = (3, 0, 2, 1)[i]
    return jnp.where(a == 0, 3 - i, jnp.where(a == 1, inner, jnp.where(a == 2, 3 - inner, i)))


def line_slots(place, sums, landing, sems, parts, ready, final, near=False):
    a = place.a
    last = 2 * A - 3 if near else A - 1

    def part(ref, h):
        if parts == 1:
            return ref
        rows = ref.shape[0] // parts
        return ref.at[pl.ds(h * rows, rows)]

    def hop(d, h, way):
        at = 0 if way > 0 else 1
        return remote(
            part(sums(d), h), part(landing(d, way), h), sems.at[at, d, h, 0],
            sems.at[at, d, h, 1], place.line(a + way),
        )

    def take(d, h, way):
        @pl.when((a - way >= 0) & (a - way < A))
        def _():
            hop(d, h, way).wait_recv()
            here = part(sums(d), h)
            add_into(here, here, part(landing(d, way), h))

    for t in range(last + 1):
        for way in (1, -1):
            at = a if way > 0 else A - 1 - a
            to = t - at + 1 if near else A - 1 - t + at
            d = to if way > 0 else A - 1 - to

            @pl.when((to > at) & (to < A))
            def _():
                for h in range(parts):
                    ready(d, h)
                    take(d, h, way)
                    hop(d, h, way).start()

        if t == last:
            for h in range(parts):
                ready(a, h)
                take(a, h, 1)
                take(a, h, -1)
                final(h)
        yield
    for d in range(A):
        for h in range(parts):
            for way in (1, -1):
                @pl.when((d - a) * way > 0)
                def _():
                    hop(d, h, way).wait_send()


def share_sems():
    return [DMA((2,)), DMA((X, 2)), DMA((1,))]


def share_flow(place, own, out, sems, ready=None):
    x_sem, core_sem, local = sems
    r, x, c = place.r, place.x, place.c
    if ready is not None:
        yield
        ready()
    keep = pltpu.make_async_copy(own, out.at[r], local.at[0])
    to_x = remote(own, out.at[r], x_sem.at[0], x_sem.at[1], place.over_x)
    near = remote(own, out.at[r], core_sem.at[x, 0], core_sem.at[x, 1], place.over_core)
    far = remote(
        out.at[place.rx], out.at[place.rx], core_sem.at[1 - x, 0], core_sem.at[1 - x, 1],
        place.over_core,
    )
    to_x.start()
    near.start()
    keep.start()
    yield
    to_x.wait_recv()
    far.start()
    yield
    keep.wait()
    to_x.wait_send()
    near.wait()
    far.wait()


def spread_sems(B, parts=1):
    return [DMA((A, parts)), DMA((A, 2, parts)), DMA((B, A, parts, 2)), DMA((1,))]


def spread_flow(place, own, out, sems, parts=1):
    line_recv, line_send, side, local = sems
    a, b, B = place.a, place.b, place.B
    keep = pltpu.make_async_copy(own, out.at[a, b], local.at[0])
    keep.start()

    def half(h):
        return own if parts == 1 else own.at[pl.ds(h * own.shape[0] // parts, own.shape[0] // parts)]

    def to_line(src, block, h, way):
        return remote(
            src, piece(out, (block, b), h, parts), line_send.at[block, 0 if way > 0 else 1, h],
            line_recv.at[block, h], place.line(a + way),
        )

    def to_side(src, block, h, k):
        return remote(
            src, piece(out, (block, b), h, parts), side.at[k, block, h, 0],
            side.at[k, block, h, 1], place.side((b + k) % B),
        )

    for h in range(parts):
        @pl.when(a < A - 1)
        def _():
            to_line(half(h), a, h, 1).start()

        @pl.when(a > 0)
        def _():
            to_line(half(h), a, h, -1).start()

        for k in range(1, B):
            to_side(half(h), a, h, k).start()
    for step in range(1, A):
        for h in range(parts):
            yield
            for way in (1, -1):
                block = a - way * step

                @pl.when((block >= 0) & (block < A))
                def _():
                    src = piece(out, (block, b), h, parts)
                    to_line(src, block, h, way).wait_recv()

                    @pl.when((a + way >= 0) & (a + way < A))
                    def _():
                        to_line(src, block, h, way).start()

                    for k in range(1, B):
                        to_side(src, block, h, k).start()

    yield
    keep.wait()
    for block in range(A):
        for h in range(parts):
            src = piece(out, (block, b), h, parts)

            @pl.when((a < A - 1) & (block <= a))
            def _():
                to_line(src, block, h, 1).wait_send()

            @pl.when((a > 0) & (block >= a))
            def _():
                to_line(src, block, h, -1).wait_send()

            for k in range(1, B):
                to_side(src, block, h, k).wait()


def columns_sems(B):
    return [DMA((A, 2)), DMA((B, A, 2)), DMA((1,))]


def columns_flow(place, own, out, sems):
    line, side, local = sems
    a, b, B = place.a, place.b, place.B
    keep = pltpu.make_async_copy(own.at[a], out.at[a, b], local.at[0])
    keep.start()

    def to_line(k):
        to = (a + k) % A
        return remote(own.at[to], out.at[a, b], line.at[k, 0], line.at[k, 1], place.line(to))

    def to_side(src, block, k):
        return remote(
            src, out.at[block, b], side.at[k, block, 0], side.at[k, block, 1],
            place.side((b + k) % B),
        )

    for k in range(1, A):
        to_line(k).start()
    for k in range(1, B):
        to_side(own.at[a], a, k).start()
    for k in (1, 3, 2):
        yield
        to_line(k).wait_recv()
        block = (a + A - k) % A
        for j in range(1, B):
            to_side(out.at[block, b], block, j).start()
    yield
    keep.wait()
    for k in range(1, A):
        to_line(k).wait_send()
    for block in range(A):
        for k in range(1, B):
            to_side(out.at[block, b], block, k).wait()


def sides_sems(B):
    return [DMA((B, 2)), DMA((1,))]


def sides_flow(place, own, out, sems):
    side, local = sems
    b, B = place.b, place.B
    keep = pltpu.make_async_copy(own, out.at[b], local.at[0])
    keep.start()
    copies = [
        remote(own, out.at[b], side.at[k, 0], side.at[k, 1], place.side((b + k) % B))
        for k in range(1, B)
    ]
    for copy in copies:
        copy.start()
    yield
    keep.wait()
    for copy in copies:
        copy.wait()


ANY = pl.BlockSpec(memory_space=pl.ANY)
VMEM = pl.BlockSpec(memory_space=pltpu.VMEM)


def call(kernel, name, collective_id, outs, out_specs, scratch, args, in_specs):
    return pl.pallas_call(
        kernel,
        out_shape=outs,
        in_specs=in_specs,
        out_specs=out_specs,
        scratch_shapes=scratch,
        name=name,
        compiler_params=pltpu.CompilerParams(
            collective_id=collective_id, has_side_effects=True, vmem_limit_bytes=63 * 2**20
        ),
    )(*args)


def shape(*dims, dtype=bf):
    return jax.ShapeDtypeStruct(dims, dtype)


def split_refs(refs, *sizes):
    found, at = [], 0
    for size in sizes:
        found.append(refs[at : at + size])
        at += size
    return found


def select(rows, cols, shift, at, width):
    j = lax.broadcasted_iota(jnp.int32, (1, cols), 1) - at
    wanted = jnp.where((j >= 0) & (j < width), j + shift, -1)
    row = lax.broadcasted_iota(jnp.int32, (rows, cols), 0)
    return jnp.where(row == wanted, 1.0, 0.0).astype(bf)


def rope(ref, at, cosine, sine, out, to, head_dim):
    half = head_dim // 2
    former, latter = ref[pl.ds(at, half), :], ref[pl.ds(at + half, half), :]
    out[pl.ds(to, half), :] = (former * cosine - latter * sine).astype(out.dtype)
    out[pl.ds(to + half, half), :] = (latter * cosine + former * sine).astype(out.dtype)


def attention_forward(B, weights, gates, w_down, gains, tokens, cotangent, ids):
    wrows, width = weights[0].shape
    rows = tokens.shape[0]
    group = 4 * rows
    ff = gates[0].shape[1]
    wcols = width // 4
    head_dim = width // H
    heads = H // 4
    sub = ff // (A * B * 4)
    pad = -(-sub // 16) * 16
    fcols = B * pad
    wide = 384
    span = -(-wcols // 128) * 128
    pair = 2 * wcols
    parts = halves(wrows)
    trio = 3
    score_scale = 1.0 / math.sqrt(head_dim)

    def kernel(*refs):
        w_in, g_in, ins, outs, scratch, refs = split_refs(refs, 4, 2, 8, 12, 18, 100)
        wd_in, gain_in, tok_in, cot_in, seq_row, seq_col, blk_row, blk_col = ins
        (w4_out, gain_out, tok_out, d_out, gu_out, dn_out, qkv_out, mixed_out, after_out,
         n2_out, table_out, normed_t) = outs
        (w_all, g_all, wd_all, own4, gu_own, dn_own, own_gain, gain_all, tok_all, d_own, w4_all,
         normed, raw, bias, mixed, proj, proj_all, load) = scratch
        s1, s2, s3, s4, s5, s6, s7 = split_refs(refs, 4, 4, 3, 6, 3, 2, 100)
        qkv, mix_x, mix_core, ex_sem, save = s7
        place = Place(B)
        r, x, c = place.r, place.x, place.c
        loads = [pltpu.make_async_copy(w, w_all.at[i], load.at[i]) for i, w in enumerate(w_in)]
        loads += [
            pltpu.make_async_copy(w, g_all.at[i], load.at[4 + i]) for i, w in enumerate(g_in)
        ]
        loads.append(pltpu.make_async_copy(wd_in, wd_all, load.at[6]))
        for copy in loads:
            copy.start()
        start = pl.multiple_of(r * wcols // 128 * 128, 128)
        shift = r * wcols - start
        for i in range(2):
            total = jnp.zeros((wrows, pair), f32)
            for j in range(2):
                loads[2 * i + j].wait()
                total += jnp.dot(
                    w_all[2 * i + j, :, pl.ds(start, span)],
                    select(span, pair, shift, j * wcols, wcols), preferred_element_type=f32,
                )
            own4[:, i * pair : (i + 1) * pair] = total.astype(bf)
        for k in range(width // wide):
            own_gain[:, k * wide : (k + 1) * wide] = jnp.dot(
                gain_in[...], select(wrows, wide, 0, place.s * wrows - k * wide, wrows),
                preferred_element_type=f32,
            )
        greet(place, True, True, True)

        def prepare():
            for i in range(2):
                loads[4 + i].wait()
            loads[6].wait()

            def one(n, carry):
                i, block = n // A, n % A
                total = jnp.zeros((wrows, fcols), f32)
                for j in range(B):
                    first = ((block * B + j) * 4 + r) * sub
                    at = pl.multiple_of(jnp.minimum(first // 128 * 128, ff - wide), 128)
                    total += jnp.dot(
                        g_all[i, :, pl.ds(at, wide)],
                        select(wide, fcols, first - at, j * pad, sub),
                        preferred_element_type=f32,
                    )
                at = pl.multiple_of(i * fcols, 128)
                gu_own[block, :, pl.ds(at, fcols)] = total.astype(bf)
                return carry

            lax.fori_loop(0, 2 * A, one, 0)
            row = lax.broadcasted_iota(jnp.int32, (pad, ff // (A * B)), 0)
            col = lax.broadcasted_iota(jnp.int32, (pad, ff // (A * B)), 1)
            pick = jnp.where((col - r * sub == row) & (row < sub), 1.0, 0.0).astype(bf)
            tile = 768

            def down(n, carry):
                at = pl.ds(pl.multiple_of(n * tile, tile), tile)
                dn_own[:, at] = jnp.dot(
                    pick, wd_all[:, at], preferred_element_type=f32
                ).astype(bf)
                return carry

            lax.fori_loop(0, width // tile, down, 0)
            d_own[...] = (branch_scale * cot_in[...].astype(f32)).astype(bf)
            less = jnp.where(seq_col[...] < seq_row[...], 1.0, 0.0)
            earlier = jnp.sum(less, axis=0, keepdims=True)
            at = lax.broadcasted_iota(jnp.int32, (1, group), 1).astype(f32) - earlier
            half = head_dim // 2
            index = lax.broadcasted_iota(jnp.int32, (half, group), 0).astype(f32)
            angle = at * jnp.exp(index * (-2.0 * math.log(rope_base) / head_dim))
            table_out[0] = jnp.cos(angle)
            table_out[1] = jnp.sin(angle)
            allowed = (seq_col[...] == seq_row[...]) & (blk_col[...] <= blk_row[...])
            bias[...] = jnp.where(allowed, 0.0, masked_score)
            yield
            total = jnp.zeros((8, width), f32)
            for block in range(A):
                for side in range(B):
                    total += gain_all[block, side]
            gain_out[...] = total
            for i in range(4):
                value = tok_all[i].astype(f32)
                factor = lax.rsqrt(jnp.mean(value * value, axis=1, keepdims=True) + norm_eps)
                value = value * factor * total[0:1]
                at = slice(i * rows, (i + 1) * rows)
                normed[at, :] = value.astype(bf)
                normed_t[:, at] = value.T.astype(bf)

        def share_piece(k):
            at = pl.ds(k * trio * head_dim, trio * head_dim)
            own = mixed.at[r, at]
            far = mixed.at[place.rx, at]
            return (
                remote(own, own, mix_x.at[k, 0], mix_x.at[k, 1], place.over_x),
                remote(own, own, mix_core.at[x, k, 0], mix_core.at[x, k, 1], place.over_core),
                remote(
                    far, far, mix_core.at[1 - x, k, 0], mix_core.at[1 - x, k, 1],
                    place.over_core,
                ),
            )

        pieces = heads // trio

        def attend():
            step = 256

            def project(n, carry):
                cols = pl.ds(pl.multiple_of(span - 128 + n * step, 128), step)
                w = w4_all[:, :, :, cols].reshape(width, step)
                at = pl.ds(pl.multiple_of(n * step, step), step)
                raw[at, :] = product(normed[...], w).T
                return carry

            lax.fori_loop(0, (width - span + 128) // step, project, 0)
            skip = wcols - (span - 128)
            cosine, sine = table_out[0], table_out[1]

            def turn(n, carry):
                at = pl.multiple_of(wcols + n * head_dim, 32)
                rope(raw, pl.multiple_of(skip + at, 32), cosine, sine, qkv, at, head_dim)
                return carry

            lax.fori_loop(0, 2 * heads, turn, 0)
            qkv[:wcols, :] = raw[pl.ds(skip, wcols), :].astype(bf)
            pltpu.make_async_copy(qkv, qkv_out, save.at[0]).start()
            yield

            def head(n, carry):
                at = lambda part: pl.ds(pl.multiple_of(part * wcols + n * head_dim, 64), head_dim)
                scores = across(qkv[at(2), :], qkv[at(1), :]) * score_scale + bias[...]
                top = jnp.max(scores, axis=0, keepdims=True)
                powers = jnp.exp(scores - top)
                probs = powers * (1.0 / jnp.sum(powers, axis=0, keepdims=True))
                mixed[r, at(0), :] = product(qkv[at(0), :], probs.astype(bf)).astype(bf)
                return carry

            for k in range(pieces):
                lax.fori_loop(k * trio, (k + 1) * trio, head, 0)
                to_x, near, far = share_piece(k)
                to_x.start()
                near.start()
                if k:
                    to_x, near, far = share_piece(k - 1)
                    to_x.wait_recv()
                    far.start()
                yield
            to_x, near, far = share_piece(pieces - 1)
            to_x.wait_recv()
            far.start()
            for k in range(pieces):
                to_x, near, far = share_piece(k)
                near.wait_recv()
                far.wait_recv()
            everyone = mixed[...].reshape(width, group)
            value = across(everyone, w4_all[:, :, :, :span].reshape(width, span))
            proj[...] = value.astype(bf).reshape(4, rows, span)
            proj_all[r] = proj[r]
            copies = []
            for k in (2, 3, 1):
                to = (r + k) % 4
                copies.append(
                    remote(
                        proj.at[to], proj_all.at[r], ex_sem.at[k, 0], ex_sem.at[k, 1],
                        (place.s, to),
                    )
                )
                copies[-1].start()
            saved = pltpu.make_async_copy(mixed, mixed_out, save.at[1])
            saved.start()
            yield
            for copy in copies:
                copy.wait()
            own = tok_all[r].astype(f32)
            halves_ = []
            for side in range(2):
                total = jnp.zeros((rows, pair), f32)
                for core in range(2):
                    total += jnp.dot(
                        proj_all[side * 2 + core],
                        select(span, pair, 0, core * wcols, wcols), preferred_element_type=f32,
                    )
                at = slice(side * pair, (side + 1) * pair)
                halves_.append(own[:, at] + branch_scale * total)
                after_out[:, at] = halves_[-1]
            mean = sum(jnp.sum(v * v, axis=1, keepdims=True) for v in halves_) / width
            factor = lax.rsqrt(mean + norm_eps)
            for side in range(2):
                at = slice(side * pair, (side + 1) * pair)
                n2_out[:, at] = (halves_[side] * factor * gain_out[1:2, at]).astype(bf)
            yield
            saved.wait()
            pltpu.make_async_copy(qkv, qkv_out, save.at[0]).wait()
            for k in range(pieces):
                to_x, near, far = share_piece(k)
                to_x.wait_send()
                near.wait_send()
                far.wait_send()

        def weights_flow():
            yield from spread_flow(place, own4, w4_all, s1, parts)
            pltpu.make_async_copy(w4_all, w4_out, save.at[2]).start()

        run_flows(
            [
                weights_flow(),
                share_flow(place, tok_in, tok_all, s3),
                spread_flow(place, own_gain, gain_all, s2),
                prepare(),
                widen_flow(place, d_own, d_out, s4),
                columns_flow(place, gu_own, gu_out, s5),
                sides_flow(place, dn_own, dn_out, s6),
                attend(),
            ],
            (0, 1, 2, 3, 1, 1, 1, 2, 2, 2, 2, 2, 3, 3) + (0,) * (3 * parts) + (4, 5, 6, 0, 0)
            + (4, 7, 4, 5, 7, 4, 5, 7, 4, 5, 7, 4, 4, 5, 7, 4),
        )
        saved = pltpu.make_async_copy(tok_all, tok_out, save.at[1])
        saved.start()
        saved.wait()
        pltpu.make_async_copy(w4_all, w4_out, save.at[2]).wait()

    block = (rows, width)
    return call(
        kernel, "attention_forward", 1,
        [
            shape(A, B, wrows, 4 * wcols), shape(8, width, dtype=f32), shape(4, *block),
            shape(X, A, X, *block), shape(A, B, wrows, 2 * fcols), shape(B, pad, width),
            shape(3 * wcols, group), shape(4, wcols, group), shape(*block, dtype=f32),
            shape(*block), shape(2, head_dim // 2, group, dtype=f32), shape(width, group),
        ],
        [ANY, VMEM, ANY, ANY, ANY, ANY, ANY, ANY, VMEM, VMEM, VMEM, VMEM],
        [
            pltpu.VMEM((4, wrows, width), bf), pltpu.VMEM((2, wrows, ff), bf),
            pltpu.VMEM(w_down.shape, bf), pltpu.VMEM((wrows, 4 * wcols), bf),
            pltpu.VMEM((A, wrows, 2 * fcols), bf), pltpu.VMEM((pad, width), bf),
            pltpu.VMEM((8, width), f32), pltpu.VMEM((A, B, 8, width), f32),
            pltpu.VMEM((4,) + block, bf), pltpu.VMEM(block, bf),
            pltpu.VMEM((A, B, wrows, 4 * wcols), bf), pltpu.VMEM((group, width), bf),
            pltpu.VMEM((width - span + 128, group), f32), pltpu.VMEM((group, group), f32),
            pltpu.VMEM((4, wcols, group), bf), pltpu.VMEM((4, rows, span), bf),
            pltpu.VMEM((4, rows, span), bf), DMA((7,)),
        ]
        + spread_sems(B, parts) + spread_sems(B) + share_sems() + widen_sems() + columns_sems(B)
        + sides_sems(B)
        + [
            pltpu.VMEM((3 * wcols, group), bf), DMA((3, 2)), DMA((X, 3, 2)), DMA((4, 2)),
            DMA((3,)),
        ],
        [*weights, *gates, w_down, gains, tokens, cotangent, *ids],
        [ANY] * 7 + [VMEM, ANY] + [VMEM] * 5,
    )


def feed_forward(B, normed_two, d_down, gate_up, down):
    rows, width = normed_two.shape
    fcols = down.shape[0]
    every = X * A * X * rows
    pair = X * rows
    parts = halves(rows)
    wide = 768
    tile = 384

    wrows = gate_up.shape[0] // (A * B)
    pad = fcols // B
    many = 1152

    def kernel(n_in, d_in, gu_in, dn_in, out, f_out, ggu_out, gd_out, *refs):
        bufs, (line_recv, line_send, over_x, over_core), sems = split_refs(refs, 11, 4, 100)
        n_all, d_all, gu, dn, part, hid, d_gu, from_core, from_x, landed, g_all = bufs
        (g_down, load, core_sem, x_sem, line_sem, gu_side, gd_side, gu_sem, gd_sem, f_core, f_x,
         free, f_line) = sems
        place = Place(B)
        a, x, c = place.a, place.x, place.c
        loads = [
            pltpu.make_async_copy(n_in, n_all.at[x, a, c], load.at[0]),
            pltpu.make_async_copy(gu_in, gu, load.at[1]),
            pltpu.make_async_copy(dn_in, dn, load.at[2]),
            pltpu.make_async_copy(d_in, d_all, load.at[3]),
        ]
        for copy in loads:
            copy.start()
        greet(place, True, True, True)

        def to_line(block, way):
            src = n_all.at[x, block, c]
            return remote(
                src, src, line_send.at[block, (1 - way) // 2], line_recv.at[block],
                place.line(a + way),
            )

        def to_x(block):
            src = n_all.at[x, block, c]
            return remote(src, src, over_x.at[block, 0], over_x.at[block, 1], place.over_x)

        def to_core(side, block):
            src = n_all.at[side, block, c]
            return remote(
                src, src, over_core.at[side, block, 0], over_core.at[side, block, 1],
                place.over_core,
            )

        def sum_core(side, d, h):
            return remote(
                piece(part, (side, d, 1 - c), h, parts), piece(from_core, (side, d), h, parts),
                core_sem.at[side, d, h, 0], core_sem.at[side, d, h, 1], place.over_core,
            )

        def sum_x(d, h):
            return remote(
                piece(part, (1 - x, d, c), h, parts), piece(from_x, d, h, parts),
                x_sem.at[d, h, 0], x_sem.at[d, h, 1], place.over_x,
            )

        def merge(side, d, h):
            sum_core(side, d, h).wait_recv()
            here = piece(part, (side, d, c), h, parts)
            add_into(here, here, piece(from_core, (side, d), h, parts))

        def send_sum(d):
            for h in range(parts):
                merge(1 - x, d, h)
                sum_x(d, h).start()

        loads[0].wait()

        @pl.when(a < A - 1)
        def _():
            to_line(a, 1).start()

        @pl.when(a > 0)
        def _():
            to_line(a, -1).start()

        to_x(a).start()
        to_core(x, a).start()
        for copy in loads[1:]:
            copy.wait()

        def nearest(i):
            left = jnp.where(a == 1, jnp.where(i == 1, 0, i), jnp.where(i == 0, 0, i))
            left = jnp.where((a == 1) & (i == 0), 1, left)
            right = jnp.where(a == 2, jnp.where(i == 0, 2, jnp.where(i == 1, 1, 3)), A - 1 - i)
            right = jnp.where((a == 2) & (i == A - 1), 0, right)
            return jnp.where(a < 2, left, right)

        def item(j):
            near = (j == 0) | ((j % 2 == 1) & (j < 2 * A - 1))
            i = jnp.where(near, (j + 1) // 2, jnp.where(j == 2 * A - 1, A - 1, j // 2 - 1))
            return near, nearest(i)

        def compute(side, block):
            n = n_all[side, block].reshape(pair, width)
            d = d_all[side, block].reshape(pair, width)
            both = product(n, gu[...])
            gate, up = both[:, :fcols], both[:, fcols:]
            d_hidden = against(d, dn[...])
            sig = jax.nn.sigmoid(gate)
            at = pl.ds(pl.multiple_of((side * A + block) * pair, pair), pair)
            hid[at, :] = (gate * sig * up).astype(bf)
            d_gate = (d_hidden * up * sig * (1.0 + gate * (1.0 - sig))).astype(bf)
            d_up = (d_hidden * gate * sig).astype(bf)
            both = jnp.concatenate([d_gate, d_up], axis=1)
            d_gu[at, :] = both
            for k in range(width // wide):
                cols = pl.ds(k * wide, wide)
                value = against(both, gu[cols, :]).astype(bf)
                part[side, block, :, :, cols] = value.reshape(X, rows, wide)

        def arrive(j, carry):
            near, block = item(j)
            side = jnp.where(near, x, 1 - x)

            @pl.when(near & (j > 0))
            def _():
                way = jnp.where(block < a, 1, -1)
                to_line(block, way).wait_recv()

                @pl.when((a + way >= 0) & (a + way < A))
                def _():
                    to_line(block, way).start()

                to_x(block).start()
                to_core(x, block).start()

            @pl.when(jnp.logical_not(near))
            def _():
                to_x(block).wait_recv()
                to_core(1 - x, block).start()

            to_core(side, block).wait_recv()
            compute(side, block)
            for h in range(parts):
                sum_core(side, block, h).start()

            before, last = item(jnp.maximum(j - 1, 0))

            @pl.when((j > 3) & jnp.logical_not(before))
            def _():
                send_sum(last)

            return carry

        lax.fori_loop(0, 2 * A, arrive, 0)
        send_sum(nearest(A - 1))
        send_sum(a)

        def ready(d, h):
            merge(x, d, h)
            sum_x(d, h).wait_recv()
            here = piece(part, (x, d, c), h, parts)
            add_into(here, here, piece(from_x, d, h, parts))

        piece_rows = rows // parts

        def final(h):
            at = pl.ds(h * piece_rows, piece_rows)
            out[at, :] = part[x, a, c, at, :]

        chain = line_slots(
            place, lambda d: part.at[x, d, c], lambda d, way: landed.at[d + (way > 0)], line_sem,
            parts, ready, final, near=True,
        )

        def grad_down(k, carry):
            at = pl.ds(pl.multiple_of(k * tile, tile), tile)
            d = d_all[:, :, :, :, at].reshape(every, tile)
            g_down[:, at] = across(hid[...], d).astype(bf)
            return carry

        def grad_gate_up(k, carry):
            at = pl.ds(pl.multiple_of(k * many, many), many)
            n = n_all[:, :, :, :, at].reshape(every, many)
            count = many // wrows
            for i in range(2):
                cols = pl.ds(i * fcols, fcols)
                value = across(n, d_gu[:, cols]).astype(bf)
                g_all[pl.ds(k * count, count), :, cols] = value.reshape(count, wrows, fcols)
            return carry

        def aside(d, k):
            to = (place.b + k) % B
            return remote(
                g_all.at[d * B + to], gu_side.at[k - 1, d], gu_sem.at[k, d, 0],
                gu_sem.at[k, d, 1], place.side(to),
            )

        def aside_down(k):
            to = (place.b + k) % B
            at = pl.ds(pl.multiple_of(to * pad, 16), pad)
            return remote(
                g_down.at[at], gd_side.at[k - 1], gd_sem.at[k, 0], gd_sem.at[k, 1], place.side(to)
            )

        def forward(k, carry):
            side, block = k // A, k % A
            at = pl.ds(pl.multiple_of(k * pair, pair), pair)
            for i in range(width // wide):
                cols = pl.ds(i * wide, wide)
                value = product(hid[at, :], dn[:, cols]).astype(bf)
                d_all[side, block, :, :, cols] = value.reshape(X, rows, wide)
            return carry

        mine = pl.ds(pl.multiple_of(place.b * pad, 16), pad)
        outs = [pltpu.make_async_copy(g_down.at[mine], gd_out, load.at[0])] + [
            pltpu.make_async_copy(g_all.at[d * B + place.b], ggu_out.at[d], load.at[1 + d])
            for d in range(A)
        ]

        def out_core(side, d):
            return remote(
                d_all.at[side, d, 1 - c], n_all.at[side, d, 0], f_core.at[side, d, 0],
                f_core.at[side, d, 1], place.over_core,
            )

        def out_x(d):
            return remote(
                d_all.at[1 - x, d, c], n_all.at[0, d, 1], f_x.at[d, 0], f_x.at[d, 1],
                place.over_x,
            )

        def out_merge(side, d):
            out_core(side, d).wait_recv()
            here = d_all.at[side, d, c]
            add_into(here, here, n_all.at[side, d, 0])
        def out_ready(d, h):
            out_merge(x, d)
            out_x(d).wait_recv()
            here = d_all.at[x, d, c]
            add_into(here, here, n_all.at[0, d, 1])

        def out_final(h):
            pltpu.make_async_copy(d_all.at[x, a, c], f_out, load.at[1 + A]).start()

        def out_landing(d, way):
            return part.at[0, d, 1 - c] if way > 0 else n_all.at[1, d, 1]

        out_chain = line_slots(
            place, lambda d: d_all.at[x, d, c], out_landing, f_line, 1, out_ready, out_final
        )

        lax.fori_loop(0, width // tile, grad_down, 0)
        for k in range(1, B):
            aside_down(k).start()
        next(chain)
        for k in range(width // many):
            grad_gate_up(k, 0)
            for d in range(k * many // (wrows * B), (k + 1) * many // (wrows * B)):
                for j in range(1, B):
                    aside(d, j).start()
            next(chain)
        for d in range(A):
            to_x(d).wait_send()
            for side in range(X):
                to_core(side, d).wait_send()
                for h in range(parts):
                    sum_core(side, d, h).wait_send()

            @pl.when((a < A - 1) & (d <= a))
            def _():
                to_line(d, 1).wait_send()

            @pl.when((a > 0) & (d >= a))
            def _():
                to_line(d, -1).wait_send()

        def tell(device):
            pl.semaphore_signal(free, inc=1, device_id=device, device_id_type=MESH)

        tell(place.over_core)
        tell(place.over_x)

        for k in range(1, A):
            tell(place.line((a + k) % A))

        lax.fori_loop(0, X * A, forward, 0)
        pl.semaphore_wait(free, A + 1)
        for side in (1 - x, x):
            for i in range(A):
                out_core(side, far_first(a, i)).start()
        next(chain)
        for i in range(A):
            d = far_first(a, i)
            out_merge(1 - x, d)
            out_x(d).start()
        for _ in chain:
            pass
        for k in range(1, B):
            aside_down(k).wait_recv()
            add_into(g_down.at[mine], g_down.at[mine], gd_side.at[k - 1])
        outs[0].start()
        next(out_chain)
        for d in range(A):
            for k in range(1, B):
                aside(d, k).wait_recv()
                here = g_all.at[d * B + place.b]
                add_into(here, here, gu_side.at[k - 1, d])
            outs[1 + d].start()
        for _ in out_chain:
            pass
        pltpu.make_async_copy(d_all.at[x, a, c], f_out, load.at[1 + A]).wait()
        for copy in outs:
            copy.wait()
        for k in range(1, B):
            aside_down(k).wait_send()
            for d in range(A):
                aside(d, k).wait_send()
        for d in range(A):
            out_x(d).wait_send()
            for side in range(X):
                out_core(side, d).wait_send()
            for h in range(parts):
                sum_x(d, h).wait_send()

    block = (rows, width)
    return call(
        kernel, "feed_forward", 2,
        [
            shape(*block), shape(*block), shape(A, wrows, 2 * fcols),
            shape(pad, width),
        ],
        [VMEM, ANY, ANY, ANY],
        [
            pltpu.VMEM((X, A, X) + block, bf), pltpu.VMEM((X, A, X) + block, bf),
            pltpu.VMEM(gate_up.shape, bf), pltpu.VMEM(down.shape, bf),
            pltpu.VMEM((X, A, X) + block, bf), pltpu.VMEM((every, fcols), bf),
            pltpu.VMEM((every, 2 * fcols), bf), pltpu.VMEM((X, A) + block, bf),
            pltpu.VMEM((A,) + block, bf), pltpu.VMEM((A + 1,) + block, bf),
            pltpu.VMEM((A * B, wrows, 2 * fcols), bf),
            DMA((A,)), DMA((A, 2)), DMA((A, 2)), DMA((X, A, 2)),
            pltpu.VMEM((fcols, width), bf), DMA((2 + A,)), DMA((X, A, parts, 2)),
            DMA((A, parts, 2)), DMA((2, A, parts, 2)),
            pltpu.VMEM((B - 1, A, wrows, 2 * fcols), bf), pltpu.VMEM((B - 1, pad, width), bf),
            DMA((B, A, 2)), DMA((B, 2)), DMA((X, A, 2)), DMA((A, 2)), pltpu.SemaphoreType.REGULAR,
            DMA((2, A, 1, 2)),
        ],
        [normed_two, d_down, gate_up, down],
        [ANY] * 4,
    )


def fold_scratch(rows, width):
    block = (rows, width)
    return [
        pltpu.VMEM((X * X,) + block, bf), pltpu.VMEM((X,) + block, bf), pltpu.VMEM(block, bf),
        DMA((X, 2)), DMA((2,)),
    ]


def fold_flow(place, scratch):
    part, from_core, from_x, core_sem, x_sem = scratch
    x, c = place.x, place.c

    def to_core(i):
        return remote(
            part.at[i * X + 1 - c], from_core.at[i], core_sem.at[i, 0], core_sem.at[i, 1],
            place.over_core,
        )

    def merge(i):
        to_core(i).wait_recv()
        here = part.at[i * X + c]
        add_into(here, here, from_core.at[i])

    to_x = remote(part.at[place.rx], from_x, x_sem.at[0], x_sem.at[1], place.over_x)
    to_core(1 - x).start()
    to_core(x).start()
    yield
    merge(1 - x)
    to_x.start()
    merge(x)
    yield
    to_x.wait_recv()
    here = part.at[place.r]
    add_into(here, here, from_x)
    yield
    to_x.wait_send()
    for i in range(X):
        to_core(i).wait_send()


def grad_scratch(B, rows, width):
    block = (rows, width)
    P_ = halves(rows)
    return [
        pltpu.VMEM((A,) + block, bf),
        pltpu.VMEM((B - 1, A) + block, bf),
        pltpu.VMEM((A + 1,) + block, bf),
        DMA((1,)), DMA((B, A, P_, 2)), DMA((2, A, P_, 2)),
        DMA((P_, 2)), DMA((X, P_, 2)), DMA((P_,)),
    ]


def grad_flow(place, produce, tile, sent, out, scratch):
    sums, from_side, landed, stage_sem, side_sem, line_sem, x_sem, core_sem, local = scratch
    b, B, r, x = place.b, place.B, place.r, place.x
    parts = halves(out.shape[1])
    wide = out.shape[2]

    def to_side(k, d, h):
        return remote(
            piece(sent, (k - 1, d), h, parts), piece(from_side, (k - 1, d), h, parts),
            side_sem.at[k, d, h, 0], side_sem.at[k, d, h, 1], place.side((b + k) % B),
        )

    for i in range(A):
        d = far_first(place.a, i)
        for k in range(1, B):
            tile[:, :wide] = produce(d * B + (b + k) % B)
            copy = pltpu.make_async_copy(
                tile.at[:, pl.ds(0, wide)], sent.at[k - 1, d], stage_sem.at[0]
            )
            copy.start()
            if k == 1:
                sums[d] = produce(d * B + b)
            copy.wait()
            for h in range(parts):
                to_side(k, d, h).start()
        yield

    def ready(d, h):
        for k in range(1, B):
            to_side(k, d, h).wait_recv()
            here = piece(sums, d, h, parts)
            add_into(here, here, piece(from_side, (k - 1, d), h, parts))

    def keep(src, h):
        return pltpu.make_async_copy(src, piece(out, r, h, parts), local.at[h])

    def to_x(src, h):
        return remote(src, piece(out, r, h, parts), x_sem.at[h, 0], x_sem.at[h, 1], place.over_x)

    def near(src, h):
        return remote(
            src, piece(out, r, h, parts), core_sem.at[x, h, 0], core_sem.at[x, h, 1],
            place.over_core,
        )

    def far(h):
        src = piece(out, place.rx, h, parts)
        return remote(
            src, src, core_sem.at[1 - x, h, 0], core_sem.at[1 - x, h, 1], place.over_core
        )

    def final(h):
        src = piece(sums, place.a, h, parts)
        to_x(src, h).start()
        near(src, h).start()
        keep(src, h).start()

    yield from line_slots(
        place, lambda d: sums.at[d], lambda d, way: landed.at[d + (way > 0)], line_sem, parts,
        ready, final,
    )
    for h in range(parts):
        src = piece(out, r, h, parts)
        keep(src, h).wait()
        near(src, h).wait()
    yield
    for h in range(parts):
        src = piece(out, r, h, parts)
        to_x(src, h).wait_recv()
        far(h).start()
    yield
    for h in range(parts):
        to_x(piece(out, r, h, parts), h).wait_send()
    for d in range(A):
        for h in range(parts):
            for k in range(1, B):
                to_side(k, d, h).wait_send()
    for h in range(parts):
        far(h).wait()


def owners_flow(place, own, out, sems):
    line, local = sems
    a = place.a
    keep = pltpu.make_async_copy(own.at[a], out.at[a], local.at[0])
    keep.start()
    copies = []
    for k in (1, 3, 2):
        to = (a + k) % A
        copies.append(
            remote(own.at[to], out.at[a], line.at[k, 0], line.at[k, 1], place.line(to))
        )
        copies[-1].start()
    yield
    keep.wait()
    for copy in copies:
        copy.wait()


def attention_backward(
    B, S, d_n2, after_attn, cotangent, gains, w4, qkv, mixed, tokens, normed_t, tables, ids,
    g_gate_up, g_down,
):
    rows, width = d_n2.shape
    group = 4 * rows
    wrows, wcols = width // S, width // 4
    head_dim = width // H
    heads = H // 4
    wide = 384
    span = -(-wcols // 128) * 128
    skip = wcols - (span - 128)
    tail = width - span + 128
    pair = 2 * wcols
    score_scale = 1.0 / math.sqrt(head_dim)
    widths = (span, span, pair)
    parts = halves(wrows)

    def window(s):
        return pl.multiple_of(jnp.minimum(s * wrows // 128 * 128, width - wide), 128)

    def kernel(*refs):
        ins, ids_in, outs, mids, own, refs = split_refs(refs, 12, 4, 2, 9, 15, 100)
        (dn2_in, after_in, cot_in, gain_in, w4_in, qkv_in, mixed_in, tok_in, nt_in, table_in,
         gu_in, gd_in) = ins
        seq_row, seq_col, blk_row, blk_col = ids_in
        gt_out, gain_out = outs
        all_o, all_v, all_qk, sent_o, sent_v, sent_qk, gu_cols, gu_all, gd_all = mids
        (w4, qkv_, mix, tok, n_t, bias, factors, d_nat, ex_send, ex_all, d_after, tile,
         own_gain, gain_all, load) = own
        f1, f2, g1, g2, g3, u1, u2, u3, (ex_sem, gain_sem) = split_refs(
            refs, 5, 5, 9, 9, 9, 2, 3, 3, 2
        )
        place = Place(B)
        r, x, c = place.r, place.x, place.c
        loads = [
            pltpu.make_async_copy(src, dst, load.at[i])
            for i, (src, dst) in enumerate(
                [(w4_in, w4), (mixed_in, mix), (qkv_in, qkv_), (nt_in, n_t), (tok_in, tok)]
            )
        ]
        for copy in loads:
            copy.start()
        part1, part2 = f1[0], f2[0]
        d_t = mix
        gain_one, gain_two = gain_in[0:1], gain_in[1:2]
        own_gain[...] = jnp.zeros_like(own_gain)
        step = 32

        def back_two(i, carry):
            at = pl.ds(pl.multiple_of(i * step, step), step)
            after = after_in[at, :]
            d = dn2_in[at, :].astype(f32)
            factor = lax.rsqrt(jnp.mean(after * after, axis=1, keepdims=True) + norm_eps)
            own_gain[1:2, :] += jnp.sum(d * after * factor, axis=0, keepdims=True)
            u = d * gain_two
            mean = jnp.mean(u * after, axis=1, keepdims=True)
            d_after[at, :] = (
                cot_in[at, :].astype(f32) + factor * u - after * (factor * factor * factor) * mean
            )
            return carry

        lax.fori_loop(0, rows // step, back_two, 0)
        d_proj = (branch_scale * d_after[...]).astype(bf)
        for k in range(4):
            at = k * wcols // 128 * 128
            ex_send[k] = product(
                d_proj[:, at : at + span], select(span, span, k * wcols - at, 0, wcols)
            ).astype(bf)
        ex_all[r] = ex_send[r]
        greet(place, everyone=(S, 4))
        exchange = []
        for k in (2, 3, 1):
            to = (r + k) % 4
            exchange.append(
                remote(
                    ex_send.at[to], ex_all.at[r], ex_sem.at[k, 0], ex_sem.at[k, 1],
                    (place.s, to),
                )
            )
            exchange[-1].start()

        def at_head(part, n):
            return pl.ds(pl.multiple_of(part * wcols + n * head_dim, 64), head_dim)

        def probs_of(n):
            scores = across(qkv_[at_head(2, n), :], qkv_[at_head(1, n), :]) * score_scale
            scores = scores + bias[...].astype(f32)
            powers = jnp.exp(scores - jnp.max(scores, axis=0, keepdims=True))
            return powers * (1.0 / jnp.sum(powers, axis=0, keepdims=True))

        def compute():
            allowed = (seq_col[...] == seq_row[...]) & (blk_col[...] <= blk_row[...])
            bias[...] = jnp.where(allowed, 0.0, masked_score).astype(bf)
            for i in range(4):
                loads[4].wait() if i == 0 else None
                value = tok[i].astype(f32)
                factors[i * rows : (i + 1) * rows, :] = lax.rsqrt(
                    jnp.mean(value * value, axis=1, keepdims=True) + norm_eps
                )
            for copy in loads[:4]:
                copy.wait()
            for copy in exchange:
                copy.wait()
            d_proj = ex_all[...].reshape(group, span)
            for i in (1 - c, c):
                for side in range(X):
                    k = side * X + i
                    at = pl.ds(pl.multiple_of(k * wcols, 64), wcols)
                    part1[k] = against(w4[at, :span], d_proj).astype(bf)
            yield

            def values_back(n, carry):
                d_m = part1[r, pl.ds(pl.multiple_of(n * head_dim, 64), head_dim), :]
                value = against(d_m, probs_of(n).astype(bf))
                at = pl.ds(pl.multiple_of(skip + n * head_dim, 64), head_dim)
                d_t[at, :] = value.astype(bf)
                return carry

            def flip(n, carry):
                at = pl.ds(pl.multiple_of(n * 128, 128), 128)
                d_nat[:, at] = d_t[at, :].astype(f32).T.astype(bf)
                return carry

            d_t[:skip, :] = jnp.zeros((skip, group), bf)
            lax.fori_loop(0, heads, values_back, 0)
            lax.fori_loop(0, span // 128, flip, 0)
            yield
            cosine, sine = table_in[0], table_in[1]
            half = head_dim // 2

            def turn_back(value, at):
                former, latter = value[:half], value[half:]
                d_t[pl.ds(at, half), :] = (former * cosine + latter * sine).astype(bf)
                d_t[pl.ds(at + half, half), :] = (latter * cosine - former * sine).astype(bf)

            def scores_back(n, carry):
                d_m = part1[r, pl.ds(pl.multiple_of(n * head_dim, 64), head_dim), :]
                probs = probs_of(n)
                d_probs = across(qkv_[at_head(0, n), :], d_m)
                d_s = probs * (d_probs - jnp.sum(d_probs * probs, axis=0, keepdims=True))
                d_s = d_s.astype(bf)
                at = pl.multiple_of(span + n * head_dim, 64)
                turn_back(product(qkv_[at_head(2, n), :], d_s) * score_scale, at)
                turn_back(
                    against(qkv_[at_head(1, n), :], d_s) * score_scale,
                    pl.multiple_of(at + wcols, 64),
                )
                return carry

            for k in range(3):
                lax.fori_loop(heads * k // 3, heads * (k + 1) // 3, scores_back, 0)
                if k < 2:
                    yield
            lax.fori_loop(span // 128, tail // 128, flip, 0)
            yield

            def inputs_back(n, carry):
                at = pl.ds(pl.multiple_of(n * wide, 128), wide)
                value = against(d_nat[...], w4[at, pl.ds(span - 128, tail)])
                x_f = tok[:, :, at].reshape(group, wide).astype(f32) * factors[...]
                own_gain[0:1, at] = jnp.sum(value * x_f, axis=0, keepdims=True)
                part2[:, :, at] = value.astype(bf).reshape(4, rows, wide)
                return carry

            lax.fori_loop(0, width // wide, inputs_back, 0)

        def row_block(ref, k):
            if wrows % 16 == 0:
                return ref[pl.ds(pl.multiple_of(k * wrows, 16), wrows), :]
            return product(select(wrows, width, 0, k * wrows, wrows), ref[...]).astype(bf)

        def make_o(k):
            return product(row_block(mix, k), ex_all[...].reshape(group, span)).astype(bf)

        def make_v(k):
            return product(row_block(n_t, k), d_nat[:, :span]).astype(bf)

        def make_qk(k):
            return product(row_block(n_t, k), d_nat[:, span:]).astype(bf)

        def gains_flow():
            def copy(k):
                to = lax.rem(place.s + k // 4, S)
                return remote(
                    own_gain.at[:, pl.ds(window(to), wide)], gain_all.at[k], gain_sem.at[k, 0],
                    gain_sem.at[k, 1], (to, lax.rem(r + k % 4, 4)),
                )

            def begin(k, carry):
                copy(k).start()
                return carry

            def end(k, total):
                copy(k).wait()
                return total + gain_all[k]

            start = window(place.s)
            lax.fori_loop(1, 4 * S, begin, 0)
            yield
            total = lax.fori_loop(1, 4 * S, end, own_gain[:, pl.ds(start, wide)])
            pick = select(wide, wide, place.s * wrows - start, 0, wrows)
            value = jnp.zeros_like(total)
            for _ in range(3):
                low = total.astype(bf)
                value += product(low, pick)
                total = total - low.astype(f32)
            gain_out[...] = value

        def input_end():
            def back_one(i, carry):
                at = pl.ds(pl.multiple_of(i * step, step), step)
                value = tok[r, at, :].astype(f32)
                d = part2[r, at, :].astype(f32)
                factor = lax.rsqrt(jnp.mean(value * value, axis=1, keepdims=True) + norm_eps)
                u = d * gain_one
                mean = jnp.mean(u * value, axis=1, keepdims=True)
                gt_out[at, :] = (
                    d_after[at, :] + factor * u - value * (factor * factor * factor) * mean
                ).astype(bf)
                return carry

            lax.fori_loop(0, rows // step, back_one, 0)
            yield

        M, O, V, Q, F1, F2, GU, SU, SD, G, T = range(11)
        flows = [
            compute(),
            grad_flow(place, make_o, tile, sent_o, all_o, g1),
            grad_flow(place, make_v, tile, sent_v, all_v, g2),
            grad_flow(place, make_qk, tile, sent_qk, all_qk, g3),
            fold_flow(place, f1),
            fold_flow(place, f2),
            owners_flow(place, gu_in, gu_cols, u1),
            share_flow(place, gu_cols, gu_all, u2),
            share_flow(place, gd_in, gd_all, u3),
            gains_flow(),
            input_end(),
        ]
        turns = [
            GU, M, F1, O, O, O, O, F1, F1, F1, SD, M, GU, SU, V, V, V, V, M, O, M, O, M, Q, Q, Q,
            Q, O, O, M, F2, G, V, F2, V, SD, SD, O, V, V, V, F2, F2, T, SU, SU, O, V, Q, V, G, Q,
        ]
        run_flows(flows, turns)

    block = (rows, width)
    o_block, q_block = (wrows, span), (wrows, pair)
    blocks = [(wrows, w) for w in widths]
    return call(
        kernel, "attention_backward", 3,
        [
            shape(*block), shape(8, wide, dtype=f32),
        ]
        + [shape(4, *v) for v in blocks] + [shape(B - 1, A, *v) for v in blocks]
        + [shape(*g_gate_up.shape), shape(4, *g_gate_up.shape), shape(4, *g_down.shape)],
        [VMEM, VMEM] + [ANY] * 9,
        [
            pltpu.VMEM((width, width), bf), pltpu.VMEM((3 * wcols, group), bf),
            pltpu.VMEM((width, group), bf), pltpu.VMEM((4,) + block, bf),
            pltpu.VMEM((width, group), bf), pltpu.VMEM((group, group), bf),
            pltpu.VMEM((group, 1), f32),
            pltpu.VMEM((group, tail), bf), pltpu.VMEM((4, rows, span), bf),
            pltpu.VMEM((4, rows, span), bf), pltpu.VMEM(block, f32), pltpu.VMEM((wrows, pair), bf),
            pltpu.VMEM((8, width), f32), pltpu.VMEM((4 * S, 8, wide), f32), DMA((5,)),
        ]
        + fold_scratch(wcols, group) + fold_scratch(*block)
        + grad_scratch(B, wrows, span) + grad_scratch(B, wrows, span)
        + grad_scratch(B, wrows, pair)
        + [DMA((A, 2)), DMA((1,))] + share_sems() + share_sems()
        + [DMA((4, 2)), DMA((4 * S, 2))],
        [
            d_n2, after_attn, cotangent, gains, w4, qkv, mixed, tokens, normed_t, tables,
            g_gate_up, g_down, *ids,
        ],
        [VMEM] * 4 + [ANY] * 5 + [VMEM] + [ANY] * 2 + [VMEM] * 4,
    )


def lay_out(S, ff, out, value, query_key, gate_up, down):
    wrows, span = out.shape[1:]
    pair = query_key.shape[2]
    wcols = pair // 2
    width = 4 * wcols
    skip = wcols - (span - 128)
    sub = ff // (S * 4)
    pad = down.shape[1]
    fcols = gate_up.shape[3] // 2
    B = fcols // pad
    drows = ff // S
    steps = 9 if wrows % 144 == 0 else 1
    rows, cols = wrows // steps, width // steps

    def kernel(o_in, v_in, qk_in, gu_in, d_in, o_out, q_out, k_out, v_out, g_out, u_out, d_out):
        def beside(ref, at, to):
            for side in range(2):
                parts = [
                    ref[side * 2 + core].astype(f32)[:, at : at + wcols] for core in range(2)
                ]
                to[:, side * pair : (side + 1) * pair] = jnp.concatenate(parts, axis=1)

        beside(o_in, 0, o_out)
        beside(v_in, skip, v_out)
        beside(qk_in, 0, q_out)
        beside(qk_in, wcols, k_out)
        for i, to in enumerate((g_out, u_out)):
            parts = []
            for m in range(4 * S):
                s = m // 4
                at = i * fcols + s % B * pad
                parts.append(gu_in[m % 4, s // B].astype(f32)[:, at : at + sub])
            to[...] = jnp.concatenate(parts, axis=1)
        d_out[...] = jnp.concatenate([d_in[k].astype(f32)[:sub] for k in range(4)], axis=0)

    def by_rows(ref):
        lead = len(ref.shape) - 2
        return pl.BlockSpec(
            ref.shape[:lead] + (rows, ref.shape[-1]), lambda i: (0,) * lead + (i, 0)
        )

    outs = [shape(wrows, width, dtype=f32)] * 4 + [shape(wrows, ff, dtype=f32)] * 2
    return pl.pallas_call(
        kernel,
        grid=(steps,),
        out_shape=outs + [shape(drows, width, dtype=f32)],
        in_specs=[by_rows(v) for v in (out, value, query_key, gate_up)]
        + [pl.BlockSpec((4, pad, cols), lambda i: (0, 0, i))],
        out_specs=[by_rows(v) for v in outs] + [pl.BlockSpec((drows, cols), lambda i: (0, i))],
        name="lay_out",
        compiler_params=pltpu.CompilerParams(vmem_limit_bytes=60 * 2**20),
    )(out, value, query_key, gate_up, down)


def product(left_side, right_side):
    return jnp.dot(left_side, right_side, preferred_element_type=f32)


def against(left_side, right_side):
    return lax.dot_general(
        left_side, right_side, (((1,), (1,)), ((), ())), preferred_element_type=f32
    )


def across(left_side, right_side):
    return lax.dot_general(
        left_side, right_side, (((0,), (0,)), ((), ())), preferred_element_type=f32
    )


def body(
    tokens,
    attn_gain,
    w_query,
    w_key,
    w_value,
    w_out,
    ffn_gain,
    w_gate,
    w_up,
    w_down,
    seq_ids,
    block_ids,
    cotangent,
):
    S = lax.axis_size("shard")
    R = lax.axis_size("replica")
    B = S // A
    rows, width = tokens.shape
    ff = w_gate.shape[1]
    wrows = width // S
    ids = (seq_ids[None, :], seq_ids[:, None], block_ids[None, :], block_ids[:, None])
    gains = jnp.pad(jnp.stack([attn_gain, ffn_gain]), ((0, 6), (0, 0)))
    (
        w4, gains, tokens_group, d_down, gate_up, down_w, qkv, mixed_all, after_attn, normed_two,
        tables, normed_t,
    ) = attention_forward(
        B, [w_out, w_value, w_query, w_key], [w_gate, w_up], w_down, gains, tokens, cotangent, ids
    )
    d_n2, ffn_out, g_gate_up, g_down = feed_forward(
        B, normed_two, d_down, gate_up.reshape(width, -1), down_w.reshape(-1, width)
    )
    grad_tokens, gain_sums, *parts = attention_backward(
        B, S, d_n2, after_attn, cotangent, gains, w4.reshape(width, width), qkv,
        mixed_all.reshape(width, -1), tokens_group, normed_t, tables, ids, g_gate_up, g_down,
    )
    g_out, g_query, g_key, g_value, g_gate, g_up, g_down = lay_out(
        S, ff, *parts[:3], *parts[7:]
    )
    result = after_attn + branch_scale * ffn_out.astype(f32)
    return (
        result.astype(bf), grad_tokens, gain_sums[0, :wrows], g_query, g_key, g_value, g_out,
        gain_sums[1, :wrows], g_gate, g_up, g_down,
    )


def solution(mesh):
    split = P(("shard", "replica"), None)
    vec, mat = P("shard"), P("shard", None)
    in_specs = (split, vec, mat, mat, mat, mat, vec, mat, mat, mat, vec, vec, split)
    out_specs = (split, split, vec, mat, mat, mat, mat, vec, mat, mat, mat)
    return jax.shard_map(body, mesh=mesh, in_specs=in_specs, out_specs=out_specs, check_vma=False)
```

time: 1630 us -> 618 us (0.38)
  waiting for transfers between devices: 1030 us -> 0 us
  Pallas kernels: 0 us -> 601 us
  blocking collectives: 236 us -> 0 us
  matrix products: 154 us -> 0 us
  local copies, waits for them, and re-layouts: 124 us -> 6.63 us
  other arithmetic: 55.4 us -> 2.97 us
    pallas_call x0 -> x4, Pallas kernels: none -> 601 us  [the longest x3 584 us: call(): pl.pallas_call(kernel, out_shape=outs, in_specs=in_specs, out_specs=out_s...]
    all_gather x14 -> x0, waiting for transfers between devices: 540 us -> none  [the longest x1 150 us: body(): w4 = lax.all_gather(w4, 'shard', axis=0, tiled=True)]
    reduce_scatter x7 -> x0, waiting for transfers between devices: 292 us -> none  [the longest x2 146 us: shrink(): v = lax.psum_scatter(v, 'replica', scatter_dimension=0, tiled=True)]
    unnamed x25 -> x0, waiting for transfers between devices: 199 us -> none
    all_to_all x6 -> x0, blocking collectives: 173 us -> none  [the longest x2 98.1 us: spread(): w = lax.all_to_all(w, 'shard', 0, 0, axis_index_groups=a_groups, tiled=True)]
    dot_general x20 -> x0, matrix products: 149 us -> none  [the longest x5 48.6 us: against(): lax.dot_general(left_side, right_side, (((1,), (1,)), ((), ())), preferre...]
    convert_element_type x7 -> x0, local copies, waits for them, and re-layouts: 45.2 us -> none  [the longest x4 35.1 us: collect(): return g.transpose(2, 1, 0, 3).reshape(wrows, ff).astype(jnp.float32)]
    psum x1 -> x0, blocking collectives: 42.6 us -> none  [body(): lax.psum(jnp.stack([gain_one_part, gain_two_part]), ('shard', 'replica'))]
  transfers between devices with their start and end apart: 23 -> 0, of which waited for: 20 -> 0; matrix products, arithmetic and copies ran while one was open for 15% -> 0% of each run, Pallas kernels for 0% -> 0%
where the time goes in v4:
time: 618 us; the launch traced here: 612 us
  Pallas kernels  601 us (97%)
  local copies, waits for them, and re-layouts  6.63 us (1%)
    pallas_call x3, Pallas kernels, call(): pl.pallas_call(kernel, out_shape=outs, in_specs=in_specs, out_specs=out_s...  584 us
    pallas_call x1, Pallas kernels, lay_out(): pl.pallas_call(kernel, grid=(steps,), out_shape=outs + [shape(drows, widt...  17.6 us

profile of v4, /device:TPU:9, one launch (start us, length us, event | category | flops | bytes accessed | tf_op | source)
XLA Modules:
  0.0 611.7 jit_solution(16856007409078982954)
XLA Ops:
  0.6 0.7 stack.9
  1.3 0.7 stack.10
  2.0 0.6 fusion.2.refs_7_
  2.6 1.5 copy.25.refs_13_.refs_15_
  4.1 1.5 copy.24.refs_11_.refs_13_
  5.7 209.7 %attention_forward.1 = (bf16[4,2,288,2304]{3,2,1,0:T(8,128)(2,1)}, f32[8,2304]{1,0:T(8,128)}, bf16[4,128,2304]{2,1,0:T(8,128)(2,1)}, bf16[2,4,2,128,2304]{4,3,2,...) custom-call(bf16[288,2304]{1,0:T(8,128)(2,1)} %refs_0_.1, ...), custom_call_target="tpu_custom_call" | custom-call | tf_op jit(solution)/shard_map/attention_forward/pallas_call | solution.py:453
  215.4 178.9 %feed_forward.1 = (bf16[128,2304]{1,0:T(8,128)(2,1)}, bf16[128,2304]{1,0:T(8,128)(2,1)}, bf16[4,288,768]{2,1,0:T(8,128)(2,1)}, bf16[192,2304]{1,0:T(8,128)(2,1)}) custom-call(bf16[128,2304]{1,0:T(8,128)(2,1)} %get-tuple-element.42.n_in, bf16[2,4,2,128,2304]{4,3,2,1,0:T(8,128)(2,1)} %get-tuple-element.43.d_in, bf16[2304,768]{1,0:T(8,128)(2,1)} %bitcast.9, ...), custom_call_target="tpu_custom_call" | custom-call | tf_op jit(solution)/shard_map/feed_forward/pallas_call | solution.py:453
  394.4 2.4 add_convert_fusion
  396.7 195.0 %attention_backward.1 = (bf16[128,2304]{1,0:T(8,128)(2,1)}, f32[8,384]{1,0:T(8,128)}, bf16[4,288,640]{2,1,0:T(8,128)(2,1)}, bf16[4,288,640]{2,1,0:T(8,128)(2,1)}...) custom-call(bf16[128,2304]{1,0:T(8,128)(2,1)} %get-tuple-element.47., ...), custom_call_target="tpu_custom_call" | custom-call | tf_op jit(solution)/shard_map/attention_backward/pallas_call | solution.py:453
  591.7 1.4 slice_reduce_fusion
  593.1 0.0 copy-start
  593.1 17.6 %lay_out.1 = (f32[288,2304]{1,0:T(8,128)}, f32[288,2304]{1,0:T(8,128)}, f32[288,2304]{1,0:T(8,128)}, f32[288,2304]{1,0:T(8,128)}, f32[288,5760]{1,0:T(8,128)}, /*index=5*/f32[288,5760]{1,0:T(8,128)}, f32[720,2304]{1,0:T(8,128)}) custom-call(bf16[4,288,640]{2,1,0:T(8,128)(2,1)} %get-tuple-element.59.o_in, bf16[4,288,640]{2,1,0:T(8,128)(2,1)} %get-tuple-element.60.v_in, ...), custom_call_target="tpu_custom_call" | custom-call | tf_op jit(solution)/shard_map/lay_out/pallas_call | solution.py:1588
  610.7 0.0 copy-done
  610.7 0.8 copy.29
Async XLA Ops:
  593.1 17.6 %copy-start = (bf16[128,2304]{1,0:T(8,128)(2,1)S(1)}, bf16[128,2304]{1,0:T(8,128)(2,1)}, u32[]{:S(2)}) copy-start(bf16[128,2304]{1,0:T(8,128)(2,1)} %get-tuple-element.85) | copy-start | bytes 1769476

commit v5 on v4

--- a/solution.py
+++ b/solution.py
@@ -482,6 +482,15 @@
     return jnp.where(row == wanted, 1.0, 0.0).astype(bf)
 
 
+def select_mixed(rows, cols, shift, j, part):
+    col = lax.broadcasted_iota(jnp.int32, (1, cols), 1)
+    wanted = jnp.where(
+        col // part % 2 == j, shift + col // (2 * part) * part + col % part, -1
+    )
+    row = lax.broadcasted_iota(jnp.int32, (rows, cols), 0)
+    return jnp.where(row == wanted, 1.0, 0.0).astype(bf)
+
+
 def rope(ref, at, cosine, sine, out, to, head_dim):
     half = head_dim // 2
     former, latter = ref[pl.ds(at, half), :], ref[pl.ds(at + half, half), :]
@@ -531,10 +540,10 @@
             total = jnp.zeros((wrows, pair), f32)
             for j in range(2):
                 loads[2 * i + j].wait()
-                total += jnp.dot(
-                    w_all[2 * i + j, :, pl.ds(start, span)],
-                    select(span, pair, shift, j * wcols, wcols), preferred_element_type=f32,
-                )
+                pick = select(span, pair, shift, j * wcols, wcols)
+                if i:
+                    pick = select_mixed(span, pair, shift, j, trio * head_dim)
+                total += product(w_all[2 * i + j, :, pl.ds(start, span)], pick)
             own4[:, i * pair : (i + 1) * pair] = total.astype(bf)
         for k in range(width // wide):
             own_gain[:, k * wide : (k + 1) * wide] = jnp.dot(
@@ -633,7 +642,9 @@
 
             def turn(n, carry):
                 at = pl.multiple_of(wcols + n * head_dim, 32)
-                rope(raw, pl.multiple_of(skip + at, 32), cosine, sine, qkv, at, head_dim)
+                i, h = n // heads, n % heads
+                first = skip + wcols + (h // trio * 2 + i) * trio * head_dim + h % trio * head_dim
+                rope(raw, pl.multiple_of(first, 32), cosine, sine, qkv, at, head_dim)
                 return carry
 
             lax.fori_loop(0, 2 * heads, turn, 0)
@@ -727,8 +738,8 @@
                 sides_flow(place, dn_own, dn_out, s6),
                 attend(),
             ],
-            (0, 1, 2, 3, 1, 1, 1, 2, 2, 2, 2, 2, 3, 3) + (0,) * (3 * parts) + (4, 5, 6, 0, 0)
-            + (4, 7, 4, 5, 7, 4, 5, 7, 4, 5, 7, 4, 4, 5, 7, 4),
+            (0, 1, 2, 3, 1, 1, 1, 2, 2, 2, 2, 2, 3, 3) + (0,) * (3 * parts)
+            + (4, 4, 4, 0, 6, 5, 7, 4, 7, 7, 7, 5, 4, 7, 4, 5, 7, 5, 4, 4, 7, 6, 5, 4),
         )
         saved = pltpu.make_async_copy(tok_all, tok_out, save.at[1])
         saved.start()
@@ -767,7 +778,7 @@
     )
 
 
-def feed_forward(B, normed_two, d_down, gate_up, down):
+def feed_forward(B, normed_two, d_down, gate_up, down, lefts):
     rows, width = normed_two.shape
     fcols = down.shape[0]
     every = X * A * X * rows
@@ -780,11 +791,12 @@
     pad = fcols // B
     many = 1152
 
-    def kernel(n_in, d_in, gu_in, dn_in, out, f_out, ggu_out, gd_out, *refs):
+    def kernel(n_in, d_in, gu_in, dn_in, *refs):
+        lefts_in, (out, f_out, ggu_out, gd_out), lefts_out, refs = split_refs(refs, 2, 4, 2, 100)
         bufs, (line_recv, line_send, over_x, over_core), sems = split_refs(refs, 11, 4, 100)
         n_all, d_all, gu, dn, part, hid, d_gu, from_core, from_x, landed, g_all = bufs
         (g_down, load, core_sem, x_sem, line_sem, gu_side, gd_side, gu_sem, gd_sem, f_core, f_x,
-         free, f_line) = sems
+         free, core_free, f_line, left_sem) = sems
         place = Place(B)
         a, x, c = place.a, place.x, place.c
         loads = [
@@ -849,6 +861,17 @@
 
         to_x(a).start()
         to_core(x, a).start()
+
+        def left_aside(i, d, k):
+            to = (place.b + k) % B
+            return remote(
+                lefts_in[i].at[d, to], lefts_out[i].at[k - 1, d], left_sem.at[i, k, d, 0],
+                left_sem.at[i, k, d, 1], place.side(to),
+            )
+
+        left_copies = [(i, d, k) for i in range(2) for d in range(A) for k in range(1, B)]
+        for at in left_copies:
+            left_aside(*at).start()
         for copy in loads[1:]:
             copy.wait()
 
@@ -919,9 +942,14 @@
         lax.fori_loop(0, 2 * A, arrive, 0)
         send_sum(nearest(A - 1))
         send_sum(a)
+        for d in range(A):
+            for h in range(parts):
+                merge(x, d, h)
+        pl.semaphore_signal(
+            core_free, inc=1, device_id=place.over_core, device_id_type=MESH
+        )
 
         def ready(d, h):
-            merge(x, d, h)
             sum_x(d, h).wait_recv()
             here = piece(part, (x, d, c), h, parts)
             add_into(here, here, piece(from_x, d, h, parts))
@@ -984,7 +1012,7 @@
 
         def out_core(side, d):
             return remote(
-                d_all.at[side, d, 1 - c], n_all.at[side, d, 0], f_core.at[side, d, 0],
+                d_all.at[side, d, 1 - c], from_core.at[side, d], f_core.at[side, d, 0],
                 f_core.at[side, d, 1], place.over_core,
             )
 
@@ -997,7 +1025,8 @@
         def out_merge(side, d):
             out_core(side, d).wait_recv()
             here = d_all.at[side, d, c]
-            add_into(here, here, n_all.at[side, d, 0])
+            add_into(here, here, from_core.at[side, d])
+
         def out_ready(d, h):
             out_merge(x, d)
             out_x(d).wait_recv()
@@ -1017,6 +1046,12 @@
         lax.fori_loop(0, width // tile, grad_down, 0)
         for k in range(1, B):
             aside_down(k).start()
+        next(chain)
+        lax.fori_loop(0, X * A, forward, 0)
+        pl.semaphore_wait(core_free, 1)
+        for side in (1 - x, x):
+            for i in range(A):
+                out_core(side, far_first(a, i)).start()
         next(chain)
         for k in range(width // many):
             grad_gate_up(k, 0)
@@ -1039,31 +1074,20 @@
             def _():
                 to_line(d, -1).wait_send()
 
-        def tell(device):
+        for device in [place.over_x] + [place.line((a + k) % A) for k in range(1, A)]:
             pl.semaphore_signal(free, inc=1, device_id=device, device_id_type=MESH)
-
-        tell(place.over_core)
-        tell(place.over_x)
-
-        for k in range(1, A):
-            tell(place.line((a + k) % A))
-
-        lax.fori_loop(0, X * A, forward, 0)
-        pl.semaphore_wait(free, A + 1)
-        for side in (1 - x, x):
-            for i in range(A):
-                out_core(side, far_first(a, i)).start()
+        for i in range(A):
+            out_merge(1 - x, far_first(a, i))
+        pl.semaphore_wait(free, A)
+        for i in range(A):
+            out_x(far_first(a, i)).start()
         next(chain)
-        for i in range(A):
-            d = far_first(a, i)
-            out_merge(1 - x, d)
-            out_x(d).start()
-        for _ in chain:
-            pass
         for k in range(1, B):
             aside_down(k).wait_recv()
             add_into(g_down.at[mine], g_down.at[mine], gd_side.at[k - 1])
         outs[0].start()
+        for _ in chain:
+            pass
         next(out_chain)
         for d in range(A):
             for k in range(1, B):
@@ -1074,6 +1098,8 @@
         for _ in out_chain:
             pass
         pltpu.make_async_copy(d_all.at[x, a, c], f_out, load.at[1 + A]).wait()
+        for at in left_copies:
+            left_aside(*at).wait()
         for copy in outs:
             copy.wait()
         for k in range(1, B):
@@ -1093,8 +1119,9 @@
         [
             shape(*block), shape(*block), shape(A, wrows, 2 * fcols),
             shape(pad, width),
-        ],
-        [VMEM, ANY, ANY, ANY],
+        ]
+        + [shape(B - 1, A, *v.shape[2:]) for v in lefts],
+        [VMEM] + [ANY] * 5,
         [
             pltpu.VMEM((X, A, X) + block, bf), pltpu.VMEM((X, A, X) + block, bf),
             pltpu.VMEM(gate_up.shape, bf), pltpu.VMEM(down.shape, bf),
@@ -1107,10 +1134,11 @@
             DMA((A, parts, 2)), DMA((2, A, parts, 2)),
             pltpu.VMEM((B - 1, A, wrows, 2 * fcols), bf), pltpu.VMEM((B - 1, pad, width), bf),
             DMA((B, A, 2)), DMA((B, 2)), DMA((X, A, 2)), DMA((A, 2)), pltpu.SemaphoreType.REGULAR,
-            DMA((2, A, 1, 2)),
+            pltpu.SemaphoreType.REGULAR,
+            DMA((2, A, 1, 2)), DMA((2, B, A, 2)),
         ],
-        [normed_two, d_down, gate_up, down],
-        [ANY] * 4,
+        [normed_two, d_down, gate_up, down, *lefts],
+        [ANY] * 6,
     )
 
 
@@ -1154,50 +1182,41 @@
         to_core(i).wait_send()
 
 
-def grad_scratch(B, rows, width):
+def owners_flow(place, own, out, sems):
+    line, local = sems
+    a = place.a
+    keep = pltpu.make_async_copy(own.at[a], out.at[a], local.at[0])
+    keep.start()
+    copies = []
+    for k in (1, 3, 2):
+        to = (a + k) % A
+        copies.append(
+            remote(own.at[to], out.at[a], line.at[k, 0], line.at[k, 1], place.line(to))
+        )
+        copies[-1].start()
+    yield
+    keep.wait()
+    for copy in copies:
+        copy.wait()
+
+
+def grad_scratch(rows, width):
     block = (rows, width)
     P_ = halves(rows)
     return [
-        pltpu.VMEM((A,) + block, bf),
-        pltpu.VMEM((B - 1, A) + block, bf),
-        pltpu.VMEM((A + 1,) + block, bf),
-        DMA((1,)), DMA((B, A, P_, 2)), DMA((2, A, P_, 2)),
+        pltpu.VMEM((A,) + block, bf), pltpu.VMEM((A + 1,) + block, bf), DMA((2, A, P_, 2)),
         DMA((P_, 2)), DMA((X, P_, 2)), DMA((P_,)),
     ]
 
 
-def grad_flow(place, produce, tile, sent, out, scratch):
-    sums, from_side, landed, stage_sem, side_sem, line_sem, x_sem, core_sem, local = scratch
-    b, B, r, x = place.b, place.B, place.r, place.x
+def grad_flow(place, produce, out, scratch):
+    sums, landed, line_sem, x_sem, core_sem, local = scratch
+    r, x = place.r, place.x
     parts = halves(out.shape[1])
-    wide = out.shape[2]
-
-    def to_side(k, d, h):
-        return remote(
-            piece(sent, (k - 1, d), h, parts), piece(from_side, (k - 1, d), h, parts),
-            side_sem.at[k, d, h, 0], side_sem.at[k, d, h, 1], place.side((b + k) % B),
-        )
-
     for i in range(A):
         d = far_first(place.a, i)
-        for k in range(1, B):
-            tile[:, :wide] = produce(d * B + (b + k) % B)
-            copy = pltpu.make_async_copy(
-                tile.at[:, pl.ds(0, wide)], sent.at[k - 1, d], stage_sem.at[0]
-            )
-            copy.start()
-            if k == 1:
-                sums[d] = produce(d * B + b)
-            copy.wait()
-            for h in range(parts):
-                to_side(k, d, h).start()
-        yield
-
-    def ready(d, h):
-        for k in range(1, B):
-            to_side(k, d, h).wait_recv()
-            here = piece(sums, d, h, parts)
-            add_into(here, here, piece(from_side, (k - 1, d), h, parts))
+        sums[d] = produce(d)
+    yield
 
     def keep(src, h):
         return pltpu.make_async_copy(src, piece(out, r, h, parts), local.at[h])
@@ -1225,7 +1244,7 @@
 
     yield from line_slots(
         place, lambda d: sums.at[d], lambda d, way: landed.at[d + (way > 0)], line_sem, parts,
-        ready, final,
+        lambda d, h: None, final,
     )
     for h in range(parts):
         src = piece(out, r, h, parts)
@@ -1239,35 +1258,12 @@
     yield
     for h in range(parts):
         to_x(piece(out, r, h, parts), h).wait_send()
-    for d in range(A):
-        for h in range(parts):
-            for k in range(1, B):
-                to_side(k, d, h).wait_send()
-    for h in range(parts):
         far(h).wait()
 
 
-def owners_flow(place, own, out, sems):
-    line, local = sems
-    a = place.a
-    keep = pltpu.make_async_copy(own.at[a], out.at[a], local.at[0])
-    keep.start()
-    copies = []
-    for k in (1, 3, 2):
-        to = (a + k) % A
-        copies.append(
-            remote(own.at[to], out.at[a], line.at[k, 0], line.at[k, 1], place.line(to))
-        )
-        copies[-1].start()
-    yield
-    keep.wait()
-    for copy in copies:
-        copy.wait()
-
-
 def attention_backward(
-    B, S, d_n2, after_attn, cotangent, gains, w4, qkv, mixed, tokens, normed_t, tables, ids,
-    g_gate_up, g_down,
+    B, S, d_n2, after_attn, cotangent, gains, w4, qkv, tokens, lefts, tables, ids, g_gate_up,
+    g_down,
 ):
     rows, width = d_n2.shape
     group = 4 * rows
@@ -1278,38 +1274,42 @@
     span = -(-wcols // 128) * 128
     skip = wcols - (span - 128)
     tail = width - span + 128
-    pair = 2 * wcols
+    trio = 3
+    third = 2 * trio * head_dim
+    thirds = heads // trio
     score_scale = 1.0 / math.sqrt(head_dim)
-    widths = (span, span, pair)
-    parts = halves(wrows)
-
-    def window(s):
-        return pl.multiple_of(jnp.minimum(s * wrows // 128 * 128, width - wide), 128)
+    widths = (span, span) + (third,) * thirds
+    count = len(widths)
+    wrows_wide = -(-wrows // 128) * 128
 
     def kernel(*refs):
-        ins, ids_in, outs, mids, own, refs = split_refs(refs, 12, 4, 2, 9, 15, 100)
-        (dn2_in, after_in, cot_in, gain_in, w4_in, qkv_in, mixed_in, tok_in, nt_in, table_in,
-         gu_in, gd_in) = ins
+        ins, lefts_in, ids_in, outs, mids, own, refs = split_refs(
+            refs, 10, 4, 4, 2, count + 3, 20, 100
+        )
+        (dn2_in, after_in, cot_in, gain_in, w4_in, qkv_in, tok_in, table_in, gu_in, gd_in) = ins
         seq_row, seq_col, blk_row, blk_col = ids_in
         gt_out, gain_out = outs
-        all_o, all_v, all_qk, sent_o, sent_v, sent_qk, gu_cols, gu_all, gd_all = mids
-        (w4, qkv_, mix, tok, n_t, bias, factors, d_nat, ex_send, ex_all, d_after, tile,
-         own_gain, gain_all, load) = own
-        f1, f2, g1, g2, g3, u1, u2, u3, (ex_sem, gain_sem) = split_refs(
-            refs, 5, 5, 9, 9, 9, 2, 3, 3, 2
+        shared, (gu_cols, gu_all, gd_all) = mids[:count], mids[count:]
+        (w4, qkv_, mix, mix_far, n_t, n_far, tok, bias, factors, d_t, d_nat, d_far, ex_send,
+         ex_all, ex_far, d_after, own_gain, gain_all, load, side_sem) = own
+        f1, f2, u1, u2, u3, (ex_sem, gain_sem), *grads = split_refs(
+            refs, 5, 5, 2, 3, 3, 2, *(6,) * count
         )
         place = Place(B)
         r, x, c = place.r, place.x, place.c
         loads = [
             pltpu.make_async_copy(src, dst, load.at[i])
             for i, (src, dst) in enumerate(
-                [(w4_in, w4), (mixed_in, mix), (qkv_in, qkv_), (nt_in, n_t), (tok_in, tok)]
+                [
+                    (tok_in, tok), (w4_in, w4), (lefts_in[0].at[:, place.b], mix),
+                    (lefts_in[1], mix_far), (qkv_in, qkv_), (lefts_in[2].at[:, place.b], n_t),
+                    (lefts_in[3], n_far),
+                ]
             )
         ]
         for copy in loads:
             copy.start()
         part1, part2 = f1[0], f2[0]
-        d_t = mix
         gain_one, gain_two = gain_in[0:1], gain_in[1:2]
         own_gain[...] = jnp.zeros_like(own_gain)
         step = 32
@@ -1335,7 +1335,7 @@
                 d_proj[:, at : at + span], select(span, span, k * wcols - at, 0, wcols)
             ).astype(bf)
         ex_all[r] = ex_send[r]
-        greet(place, everyone=(S, 4))
+        greet(place, True, True, True)
         exchange = []
         for k in (2, 3, 1):
             to = (r + k) % 4
@@ -1356,18 +1356,37 @@
             powers = jnp.exp(scores - jnp.max(scores, axis=0, keepdims=True))
             return powers * (1.0 / jnp.sum(powers, axis=0, keepdims=True))
 
+        def aside(src, dst, i):
+            return [
+                remote(
+                    src, dst(k - 1), side_sem.at[i, k, 0], side_sem.at[i, k, 1],
+                    place.side((place.b + k) % B),
+                )
+                for k in range(1, B)
+            ]
+
+        def lanes(i):
+            return pl.ds(0, span) if i == 1 else pl.ds(span + (i - 2) * third, third)
+
+        def aside_of(i):
+            if i == 0:
+                return aside(ex_all, lambda k: ex_far.at[k], 0)
+            return aside(d_nat.at[:, lanes(i)], lambda k: d_far.at[k, :, lanes(i)], i)
+
         def compute():
             allowed = (seq_col[...] == seq_row[...]) & (blk_col[...] <= blk_row[...])
             bias[...] = jnp.where(allowed, 0.0, masked_score).astype(bf)
             for i in range(4):
-                loads[4].wait() if i == 0 else None
+                loads[0].wait() if i == 0 else None
                 value = tok[i].astype(f32)
                 factors[i * rows : (i + 1) * rows, :] = lax.rsqrt(
                     jnp.mean(value * value, axis=1, keepdims=True) + norm_eps
                 )
-            for copy in loads[:4]:
+            for copy in exchange:
                 copy.wait()
-            for copy in exchange:
+            for copy in aside_of(0):
+                copy.start()
+            for copy in loads[1:]:
                 copy.wait()
             d_proj = ex_all[...].reshape(group, span)
             for i in (1 - c, c):
@@ -1392,6 +1411,8 @@
             d_t[:skip, :] = jnp.zeros((skip, group), bf)
             lax.fori_loop(0, heads, values_back, 0)
             lax.fori_loop(0, span // 128, flip, 0)
+            for copy in aside_of(1):
+                copy.start()
             yield
             cosine, sine = table_in[0], table_in[1]
             half = head_dim // 2
@@ -1407,20 +1428,23 @@
                 d_probs = across(qkv_[at_head(0, n), :], d_m)
                 d_s = probs * (d_probs - jnp.sum(d_probs * probs, axis=0, keepdims=True))
                 d_s = d_s.astype(bf)
-                at = pl.multiple_of(span + n * head_dim, 64)
-                turn_back(product(qkv_[at_head(2, n), :], d_s) * score_scale, at)
+                at = span + n // trio * third + n % trio * head_dim
+                turn_back(
+                    product(qkv_[at_head(2, n), :], d_s) * score_scale, pl.multiple_of(at, 64)
+                )
                 turn_back(
                     against(qkv_[at_head(1, n), :], d_s) * score_scale,
-                    pl.multiple_of(at + wcols, 64),
+                    pl.multiple_of(at + third // 2, 64),
                 )
                 return carry
 
-            for k in range(3):
-                lax.fori_loop(heads * k // 3, heads * (k + 1) // 3, scores_back, 0)
-                if k < 2:
-                    yield
-            lax.fori_loop(span // 128, tail // 128, flip, 0)
-            yield
+            for k in range(thirds):
+                lax.fori_loop(trio * k, trio * (k + 1), scores_back, 0)
+                first = (span + third * k) // 128
+                lax.fori_loop(first, first + third // 128, flip, 0)
+                for copy in aside_of(2 + k):
+                    copy.start()
+                yield
 
             def inputs_back(n, carry):
                 at = pl.ds(pl.multiple_of(n * wide, 128), wide)
@@ -1432,47 +1456,62 @@
 
             lax.fori_loop(0, width // wide, inputs_back, 0)
 
-        def row_block(ref, k):
-            if wrows % 16 == 0:
-                return ref[pl.ds(pl.multiple_of(k * wrows, 16), wrows), :]
-            return product(select(wrows, width, 0, k * wrows, wrows), ref[...]).astype(bf)
-
-        def make_o(k):
-            return product(row_block(mix, k), ex_all[...].reshape(group, span)).astype(bf)
-
-        def make_v(k):
-            return product(row_block(n_t, k), d_nat[:, :span]).astype(bf)
-
-        def make_qk(k):
-            return product(row_block(n_t, k), d_nat[:, span:]).astype(bf)
+        def make(i):
+            def produce(d):
+                if i == 0:
+                    own, far, right = mix, mix_far, ex_all[...].reshape(group, span)
+                else:
+                    own, far, right = n_t, n_far, d_nat[:, lanes(i)]
+                total = product(own[d], right)
+                for k in range(B - 1):
+                    if i == 0:
+                        right = ex_far[k].reshape(group, span)
+                    else:
+                        right = d_far[k, :, lanes(i)]
+                    total += product(far[k, d], right)
+                return total.astype(bf)
+
+            return produce
+
+        def grad(i):
+            for copy in aside_of(i):
+                copy.wait_recv()
+            yield from grad_flow(place, make(i), shared[i], grads[i])
+            for copy in aside_of(i):
+                copy.wait_send()
 
         def gains_flow():
-            def copy(k):
-                to = lax.rem(place.s + k // 4, S)
+            def send(i, device):
                 return remote(
-                    own_gain.at[:, pl.ds(window(to), wide)], gain_all.at[k], gain_sem.at[k, 0],
-                    gain_sem.at[k, 1], (to, lax.rem(r + k % 4, 4)),
+                    own_gain, gain_all.at[i], gain_sem.at[i, 0], gain_sem.at[i, 1], device
                 )
 
-            def begin(k, carry):
-                copy(k).start()
-                return carry
-
-            def end(k, total):
-                copy(k).wait()
-                return total + gain_all[k]
-
-            start = window(place.s)
-            lax.fori_loop(1, 4 * S, begin, 0)
-            yield
-            total = lax.fori_loop(1, 4 * S, end, own_gain[:, pl.ds(start, wide)])
-            pick = select(wide, wide, place.s * wrows - start, 0, wrows)
-            value = jnp.zeros_like(total)
-            for _ in range(3):
-                low = total.astype(bf)
-                value += product(low, pick)
-                total = total - low.astype(f32)
-            gain_out[...] = value
+            stages = [
+                [place.over_core], [place.over_x],
+                [place.side((place.b + k) % B) for k in range(1, B)],
+                [place.line((place.a + k) % A) for k in range(1, A)],
+            ]
+            at = 0
+            for stage in stages:
+                copies = [send(at + i, device) for i, device in enumerate(stage)]
+                for copy in copies:
+                    copy.start()
+                yield
+                for copy in copies:
+                    copy.wait()
+                for i in range(len(stage)):
+                    own_gain[...] += gain_all[at + i]
+                at += len(stage)
+            for n in range(width // wide):
+                own = slice(n * wide, (n + 1) * wide)
+                total = own_gain[:, own]
+                pick = select(wide, wrows_wide, place.s * wrows - n * wide, 0, wrows)
+                value = jnp.zeros((8, wrows_wide), f32)
+                for _ in range(3):
+                    low = total.astype(bf)
+                    value += product(low, pick)
+                    total = total - low.astype(f32)
+                gain_out[...] = value if n == 0 else gain_out[...] + value
 
         def input_end():
             def back_one(i, carry):
@@ -1490,12 +1529,9 @@
             lax.fori_loop(0, rows // step, back_one, 0)
             yield
 
-        M, O, V, Q, F1, F2, GU, SU, SD, G, T = range(11)
+        M, F1, F2, GU, SU, SD, G, T, O, V, P, Q, R = range(13)
         flows = [
             compute(),
-            grad_flow(place, make_o, tile, sent_o, all_o, g1),
-            grad_flow(place, make_v, tile, sent_v, all_v, g2),
-            grad_flow(place, make_qk, tile, sent_qk, all_qk, g3),
             fold_flow(place, f1),
             fold_flow(place, f2),
             owners_flow(place, gu_in, gu_cols, u1),
@@ -1503,51 +1539,50 @@
             share_flow(place, gd_in, gd_all, u3),
             gains_flow(),
             input_end(),
-        ]
+        ] + [grad(i) for i in range(count)]
         turns = [
-            GU, M, F1, O, O, O, O, F1, F1, F1, SD, M, GU, SU, V, V, V, V, M, O, M, O, M, Q, Q, Q,
-            Q, O, O, M, F2, G, V, F2, V, SD, SD, O, V, V, V, F2, F2, T, SU, SU, O, V, Q, V, G, Q,
+            GU, M, F1, F1, F1, F1, O, M, O, GU, SU, SD, M, O, V, M, O, V, M, O, V, P, M, F2, G, V,
+            P, Q, F2, G, V, P, Q, R, O, P, G, Q, R, F2, F2, T, G, P, Q, R, O, V, SD, G, Q, R, SD,
+            SU, SU, V, R, O, P, V,
         ]
         run_flows(flows, turns)
 
     block = (rows, width)
-    o_block, q_block = (wrows, span), (wrows, pair)
-    blocks = [(wrows, w) for w in widths]
+    left = (wrows, group)
     return call(
         kernel, "attention_backward", 3,
-        [
-            shape(*block), shape(8, wide, dtype=f32),
-        ]
-        + [shape(4, *v) for v in blocks] + [shape(B - 1, A, *v) for v in blocks]
+        [shape(*block), shape(8, wrows_wide, dtype=f32)]
+        + [shape(4, wrows, w) for w in widths]
         + [shape(*g_gate_up.shape), shape(4, *g_gate_up.shape), shape(4, *g_down.shape)],
-        [VMEM, VMEM] + [ANY] * 9,
+        [VMEM, VMEM] + [ANY] * (count + 3),
         [
             pltpu.VMEM((width, width), bf), pltpu.VMEM((3 * wcols, group), bf),
-            pltpu.VMEM((width, group), bf), pltpu.VMEM((4,) + block, bf),
-            pltpu.VMEM((width, group), bf), pltpu.VMEM((group, group), bf),
-            pltpu.VMEM((group, 1), f32),
-            pltpu.VMEM((group, tail), bf), pltpu.VMEM((4, rows, span), bf),
-            pltpu.VMEM((4, rows, span), bf), pltpu.VMEM(block, f32), pltpu.VMEM((wrows, pair), bf),
-            pltpu.VMEM((8, width), f32), pltpu.VMEM((4 * S, 8, wide), f32), DMA((5,)),
+            pltpu.VMEM((A,) + left, bf), pltpu.VMEM((B - 1, A) + left, bf),
+            pltpu.VMEM((A,) + left, bf), pltpu.VMEM((B - 1, A) + left, bf),
+            pltpu.VMEM((4,) + block, bf), pltpu.VMEM((group, group), bf),
+            pltpu.VMEM((group, 1), f32), pltpu.VMEM((tail, group), bf),
+            pltpu.VMEM((group, tail), bf), pltpu.VMEM((B - 1, group, tail), bf),
+            pltpu.VMEM((4, rows, span), bf), pltpu.VMEM((4, rows, span), bf),
+            pltpu.VMEM((B - 1, 4, rows, span), bf), pltpu.VMEM(block, f32),
+            pltpu.VMEM((8, width), f32), pltpu.VMEM((A + B, 8, width), f32), DMA((7,)),
+            DMA((count, B, 2)),
         ]
         + fold_scratch(wcols, group) + fold_scratch(*block)
-        + grad_scratch(B, wrows, span) + grad_scratch(B, wrows, span)
-        + grad_scratch(B, wrows, pair)
         + [DMA((A, 2)), DMA((1,))] + share_sems() + share_sems()
-        + [DMA((4, 2)), DMA((4 * S, 2))],
+        + [DMA((4, 2)), DMA((A + B, 2))]
+        + [v for w in widths for v in grad_scratch(wrows, w)],
         [
-            d_n2, after_attn, cotangent, gains, w4, qkv, mixed, tokens, normed_t, tables,
-            g_gate_up, g_down, *ids,
+            d_n2, after_attn, cotangent, gains, w4, qkv, tokens, tables, g_gate_up, g_down,
+            *lefts, *ids,
         ],
-        [VMEM] * 4 + [ANY] * 5 + [VMEM] + [ANY] * 2 + [VMEM] * 4,
+        [VMEM] * 4 + [ANY] * 3 + [VMEM] + [ANY] * 6 + [VMEM] * 4,
     )
 
 
-def lay_out(S, ff, out, value, query_key, gate_up, down):
+def lay_out(S, ff, width, out, value, groups, gate_up, down):
     wrows, span = out.shape[1:]
-    pair = query_key.shape[2]
-    wcols = pair // 2
-    width = 4 * wcols
+    wcols = width // 4
+    pair = 2 * wcols
     skip = wcols - (span - 128)
     sub = ff // (S * 4)
     pad = down.shape[1]
@@ -1557,18 +1592,24 @@
     steps = 9 if wrows % 144 == 0 else 1
     rows, cols = wrows // steps, width // steps
 
-    def kernel(o_in, v_in, qk_in, gu_in, d_in, o_out, q_out, k_out, v_out, g_out, u_out, d_out):
-        def beside(ref, at, to):
+    def kernel(o_in, v_in, *refs):
+        g_in, (gu_in, d_in, o_out, q_out, k_out, v_out, g_out, u_out, d_out) = split_refs(
+            refs, len(groups), 9
+        )
+
+        def beside(pieces, to):
             for side in range(2):
                 parts = [
-                    ref[side * 2 + core].astype(f32)[:, at : at + wcols] for core in range(2)
+                    ref[side * 2 + core].astype(f32)[:, at : at + size]
+                    for core in range(2) for ref, at, size in pieces
                 ]
                 to[:, side * pair : (side + 1) * pair] = jnp.concatenate(parts, axis=1)
 
-        beside(o_in, 0, o_out)
-        beside(v_in, skip, v_out)
-        beside(qk_in, 0, q_out)
-        beside(qk_in, wcols, k_out)
+        half = groups[0].shape[2] // 2
+        beside([(o_in, 0, wcols)], o_out)
+        beside([(v_in, skip, wcols)], v_out)
+        beside([(ref, 0, half) for ref in g_in], q_out)
+        beside([(ref, half, half) for ref in g_in], k_out)
         for i, to in enumerate((g_out, u_out)):
             parts = []
             for m in range(4 * S):
@@ -1589,12 +1630,12 @@
         kernel,
         grid=(steps,),
         out_shape=outs + [shape(drows, width, dtype=f32)],
-        in_specs=[by_rows(v) for v in (out, value, query_key, gate_up)]
+        in_specs=[by_rows(v) for v in (out, value, *groups, gate_up)]
         + [pl.BlockSpec((4, pad, cols), lambda i: (0, 0, i))],
         out_specs=[by_rows(v) for v in outs] + [pl.BlockSpec((drows, cols), lambda i: (0, i))],
         name="lay_out",
         compiler_params=pltpu.CompilerParams(vmem_limit_bytes=60 * 2**20),
-    )(out, value, query_key, gate_up, down)
+    )(out, value, *groups, gate_up, down)
 
 
 def product(left_side, right_side):
@@ -1642,15 +1683,16 @@
     ) = attention_forward(
         B, [w_out, w_value, w_query, w_key], [w_gate, w_up], w_down, gains, tokens, cotangent, ids
     )
-    d_n2, ffn_out, g_gate_up, g_down = feed_forward(
-        B, normed_two, d_down, gate_up.reshape(width, -1), down_w.reshape(-1, width)
+    lefts = [v.reshape(A, B, wrows, -1) for v in (mixed_all, normed_t)]
+    d_n2, ffn_out, g_gate_up, g_down, mixed_far, normed_far = feed_forward(
+        B, normed_two, d_down, gate_up.reshape(width, -1), down_w.reshape(-1, width), lefts
     )
-    grad_tokens, gain_sums, *parts = attention_backward(
-        B, S, d_n2, after_attn, cotangent, gains, w4.reshape(width, width), qkv,
-        mixed_all.reshape(width, -1), tokens_group, normed_t, tables, ids, g_gate_up, g_down,
+    grad_tokens, gain_sums, g_out, g_value, *parts = attention_backward(
+        B, S, d_n2, after_attn, cotangent, gains, w4.reshape(width, width), qkv, tokens_group,
+        [lefts[0], mixed_far, lefts[1], normed_far], tables, ids, g_gate_up, g_down,
     )
     g_out, g_query, g_key, g_value, g_gate, g_up, g_down = lay_out(
-        S, ff, *parts[:3], *parts[7:]
+        S, ff, width, g_out, g_value, parts[:-3], *parts[-2:]
     )
     result = after_attn + branch_scale * ffn_out.astype(f32)
     return (

time: 618 us -> 583 us (0.943)
  Pallas kernels: 601 us -> 569 us
    pallas_call x3, Pallas kernels: 584 us -> 551 us  [call(): pl.pallas_call(kernel, out_shape=outs, in_specs=in_specs, out_specs=out_s...]
where the time goes in v5:
time: 583 us; the launch traced here: 579 us
  Pallas kernels  569 us (98%)
  local copies, waits for them, and re-layouts  6.64 us (1%)
    pallas_call x3, Pallas kernels, call(): pl.pallas_call(kernel, out_shape=outs, in_specs=in_specs, out_specs=out_s...  551 us
    pallas_call x1, Pallas kernels, lay_out(): pl.pallas_call(kernel, grid=(steps,), out_shape=outs + [shape(drows, widt...  17.7 us

profile of v5, /device:TPU:9, one launch (start us, length us, event | category | flops | bytes accessed | tf_op | source)
XLA Modules:
  0.0 579.1 jit_solution(15122556894491447210)
XLA Ops:
  0.6 0.7 stack.9
  1.3 0.7 stack.10
  2.0 0.6 fusion.2.refs_7_
  2.6 1.5 copy.25.refs_13_.refs_17_
  4.1 1.5 copy.24.refs_11_.refs_15_
  5.7 199.4 %attention_forward.1 = (bf16[4,2,288,2304]{3,2,1,0:T(8,128)(2,1)}, f32[8,2304]{1,0:T(8,128)}, bf16[4,128,2304]{2,1,0:T(8,128)(2,1)}, bf16[2,4,2,128,2304]{4,3,2,...) custom-call(bf16[288,2304]{1,0:T(8,128)(2,1)} %refs_0_.1, ...), custom_call_target="tpu_custom_call" | custom-call | tf_op jit(solution)/shard_map/attention_forward/pallas_call | solution.py:453
  205.1 178.6 %feed_forward.1 = (bf16[128,2304]{1,0:T(8,128)(2,1)}, bf16[128,2304]{1,0:T(8,128)(2,1)}, bf16[4,288,768]{2,1,0:T(8,128)(2,1)}, bf16[192,2304]{1,0:T(8,128)(2,1)}...) custom-call(bf16[128,2304]{1,0:T(8,128)(2,1)} %get-tuple-element.46.n_in, ...), custom_call_target="tpu_custom_call" | custom-call | tf_op jit(solution)/shard_map/feed_forward/pallas_call | solution.py:453
  383.7 0.0 copy-start.1
  383.7 173.1 %attention_backward.1 = (bf16[128,2304]{1,0:T(8,128)(2,1)}, f32[8,384]{1,0:T(8,128)}, bf16[4,288,640]{2,1,0:T(8,128)(2,1)}, bf16[4,288,640]{2,1,0:T(8,128)(2,1)}...) custom-call(bf16[128,2304]{1,0:T(8,128)(2,1)} %get-tuple-element.53., ...), custom_call_target="tpu_custom_call" | custom-call | tf_op jit(solution)/shard_map/attention_backward/pallas_call | solution.py:453
  556.8 0.0 copy-done.1
  556.8 2.2 add_convert_fusion
  559.1 1.4 slice_reduce_fusion
  560.4 0.0 copy-start
  560.4 17.7 %lay_out.1 = (f32[288,2304]{1,0:T(8,128)}, f32[288,2304]{1,0:T(8,128)}, f32[288,2304]{1,0:T(8,128)}, f32[288,2304]{1,0:T(8,128)}, f32[288,5760]{1,0:T(8,128)}, /*index=5*/f32[288,5760]{1,0:T(8,128)}, f32[720,2304]{1,0:T(8,128)}) custom-call(bf16[4,288,640]{2,1,0:T(8,128)(2,1)} %get-tuple-element.65.o_in, bf16[4,288,640]{2,1,0:T(8,128)(2,1)} %get-tuple-element.66.v_in, ...), custom_call_target="tpu_custom_call" | custom-call | tf_op jit(solution)/shard_map/lay_out/pallas_call | solution.py:1629
  578.1 0.0 copy-done
  578.1 0.8 copy.29
Async XLA Ops:
  383.7 173.1 %copy-start.1 = (bf16[128,2304]{1,0:T(8,128)(2,1)S(1)}, bf16[128,2304]{1,0:T(8,128)(2,1)}, u32[]{:S(2)}) copy-start(bf16[128,2304]{1,0:T(8,128)(2,1)} %get-tuple-element.52) | copy-start | bytes 1769476
  560.4 17.7 %copy-start = (bf16[128,2304]{1,0:T(8,128)(2,1)S(1)}, bf16[128,2304]{1,0:T(8,128)(2,1)}, u32[]{:S(2)}) copy-start(bf16[128,2304]{1,0:T(8,128)(2,1)} %get-tuple-element.93) | copy-start | bytes 1769476

commit v6 on v5

--- a/solution.py
+++ b/solution.py
@@ -491,6 +491,16 @@
     return jnp.where(row == wanted, 1.0, 0.0).astype(bf)
 
 
+def masks(seq_row, blk_row):
+    def columns(ref):
+        row = ref[...].astype(f32)
+        return row, jnp.broadcast_to(row, (8, row.shape[1])).T[:, :1]
+
+    seq, seq_t = columns(seq_row)
+    blk, blk_t = columns(blk_row)
+    return seq_t < seq, (seq_t == seq) & (blk_t <= blk)
+
+
 def rope(ref, at, cosine, sine, out, to, head_dim):
     half = head_dim // 2
     former, latter = ref[pl.ds(at, half), :], ref[pl.ds(at + half, half), :]
@@ -517,8 +527,8 @@
     score_scale = 1.0 / math.sqrt(head_dim)
 
     def kernel(*refs):
-        w_in, g_in, ins, outs, scratch, refs = split_refs(refs, 4, 2, 8, 12, 18, 100)
-        wd_in, gain_in, tok_in, cot_in, seq_row, seq_col, blk_row, blk_col = ins
+        w_in, g_in, ins, outs, scratch, refs = split_refs(refs, 4, 2, 6, 12, 18, 100)
+        wd_in, gain_in, tok_in, cot_in, seq_row, blk_row = ins
         (w4_out, gain_out, tok_out, d_out, gu_out, dn_out, qkv_out, mixed_out, after_out,
          n2_out, table_out, normed_t) = outs
         (w_all, g_all, wd_all, own4, gu_own, dn_own, own_gain, gain_all, tok_all, d_own, w4_all,
@@ -587,15 +597,14 @@
 
             lax.fori_loop(0, width // tile, down, 0)
             d_own[...] = (branch_scale * cot_in[...].astype(f32)).astype(bf)
-            less = jnp.where(seq_col[...] < seq_row[...], 1.0, 0.0)
-            earlier = jnp.sum(less, axis=0, keepdims=True)
+            less, allowed = masks(seq_row, blk_row)
+            earlier = jnp.sum(jnp.where(less, 1.0, 0.0), axis=0, keepdims=True)
             at = lax.broadcasted_iota(jnp.int32, (1, group), 1).astype(f32) - earlier
             half = head_dim // 2
             index = lax.broadcasted_iota(jnp.int32, (half, group), 0).astype(f32)
             angle = at * jnp.exp(index * (-2.0 * math.log(rope_base) / head_dim))
             table_out[0] = jnp.cos(angle)
             table_out[1] = jnp.sin(angle)
-            allowed = (seq_col[...] == seq_row[...]) & (blk_col[...] <= blk_row[...])
             bias[...] = jnp.where(allowed, 0.0, masked_score)
             yield
             total = jnp.zeros((8, width), f32)
@@ -738,8 +747,8 @@
                 sides_flow(place, dn_own, dn_out, s6),
                 attend(),
             ],
-            (0, 1, 2, 3, 1, 1, 1, 2, 2, 2, 2, 2, 3, 3) + (0,) * (3 * parts)
-            + (4, 4, 4, 0, 6, 5, 7, 4, 7, 7, 7, 5, 4, 7, 4, 5, 7, 5, 4, 4, 7, 6, 5, 4),
+            (0, 1, 2, 3, 1, 1, 1, 2, 2, 2, 2, 2, 3, 3) + (0,) * (2 * parts) + (4,)
+            + (0,) * parts + (4, 4, 0, 6, 5, 7, 4, 7, 7, 7, 5, 4, 7, 4, 5, 7, 5, 4, 4, 7, 6, 5, 4),
         )
         saved = pltpu.make_async_copy(tok_all, tok_out, save.at[1])
         saved.start()
@@ -774,7 +783,7 @@
             DMA((3,)),
         ],
         [*weights, *gates, w_down, gains, tokens, cotangent, *ids],
-        [ANY] * 7 + [VMEM, ANY] + [VMEM] * 5,
+        [ANY] * 7 + [VMEM, ANY] + [VMEM] * 3,
     )
 
 
@@ -1278,16 +1287,16 @@
     third = 2 * trio * head_dim
     thirds = heads // trio
     score_scale = 1.0 / math.sqrt(head_dim)
-    widths = (span, span) + (third,) * thirds
+    widths = (span - 128, span) + (third,) * thirds
     count = len(widths)
     wrows_wide = -(-wrows // 128) * 128
 
     def kernel(*refs):
         ins, lefts_in, ids_in, outs, mids, own, refs = split_refs(
-            refs, 10, 4, 4, 2, count + 3, 20, 100
+            refs, 10, 4, 2, 2, count + 3, 20, 100
         )
         (dn2_in, after_in, cot_in, gain_in, w4_in, qkv_in, tok_in, table_in, gu_in, gd_in) = ins
-        seq_row, seq_col, blk_row, blk_col = ids_in
+        seq_row, blk_row = ids_in
         gt_out, gain_out = outs
         shared, (gu_cols, gu_all, gd_all) = mids[:count], mids[count:]
         (w4, qkv_, mix, mix_far, n_t, n_far, tok, bias, factors, d_t, d_nat, d_far, ex_send,
@@ -1374,7 +1383,7 @@
             return aside(d_nat.at[:, lanes(i)], lambda k: d_far.at[k, :, lanes(i)], i)
 
         def compute():
-            allowed = (seq_col[...] == seq_row[...]) & (blk_col[...] <= blk_row[...])
+            _, allowed = masks(seq_row, blk_row)
             bias[...] = jnp.where(allowed, 0.0, masked_score).astype(bf)
             for i in range(4):
                 loads[0].wait() if i == 0 else None
@@ -1409,7 +1418,10 @@
                 return carry
 
             d_t[:skip, :] = jnp.zeros((skip, group), bf)
-            lax.fori_loop(0, heads, values_back, 0)
+            for k in range(thirds):
+                lax.fori_loop(trio * k, trio * (k + 1), values_back, 0)
+                if k + 1 < thirds:
+                    yield
             lax.fori_loop(0, span // 128, flip, 0)
             for copy in aside_of(1):
                 copy.start()
@@ -1459,16 +1471,23 @@
         def make(i):
             def produce(d):
                 if i == 0:
-                    own, far, right = mix, mix_far, ex_all[...].reshape(group, span)
+                    own, far, right = mix, mix_far, ex_all[:, :, : span - 128]
+                    right = right.reshape(group, span - 128)
                 else:
                     own, far, right = n_t, n_far, d_nat[:, lanes(i)]
                 total = product(own[d], right)
                 for k in range(B - 1):
                     if i == 0:
-                        right = ex_far[k].reshape(group, span)
+                        right = ex_far[k, :, :, : span - 128].reshape(group, span - 128)
                     else:
                         right = d_far[k, :, lanes(i)]
                     total += product(far[k, d], right)
+                if i == 1:
+                    last = product(mix[d], ex_all[:, :, span - 128 :].reshape(group, 128))
+                    for k in range(B - 1):
+                        right = ex_far[k, :, :, span - 128 :].reshape(group, 128)
+                        last += product(mix_far[k, d], right)
+                    total = jnp.concatenate([total[:, :128] + last, total[:, 128:]], axis=1)
                 return total.astype(bf)
 
             return produce
@@ -1541,9 +1560,9 @@
             input_end(),
         ] + [grad(i) for i in range(count)]
         turns = [
-            GU, M, F1, F1, F1, F1, O, M, O, GU, SU, SD, M, O, V, M, O, V, M, O, V, P, M, F2, G, V,
-            P, Q, F2, G, V, P, Q, R, O, P, G, Q, R, F2, F2, T, G, P, Q, R, O, V, SD, G, Q, R, SD,
-            SU, SU, V, R, O, P, V,
+            GU, M, F1, F1, F1, F1, SD, O, O, M, M, M, GU, SU, M, O, V, M, O, V, M, O, V, P, M, SD,
+            F2, V, P, Q, F2, V, P, Q, R, O, SU, P, Q, R, F2, F2, T, P, Q, R, O, V, Q, R, G, SD, SU,
+            V, R, O, P, V, G, R, G, R, G, R, G,
         ]
         run_flows(flows, turns)
 
@@ -1575,12 +1594,13 @@
             d_n2, after_attn, cotangent, gains, w4, qkv, tokens, tables, g_gate_up, g_down,
             *lefts, *ids,
         ],
-        [VMEM] * 4 + [ANY] * 3 + [VMEM] + [ANY] * 6 + [VMEM] * 4,
+        [VMEM] * 4 + [ANY] * 3 + [VMEM] + [ANY] * 6 + [VMEM] * 2,
     )
 
 
-def lay_out(S, ff, width, out, value, groups, gate_up, down):
-    wrows, span = out.shape[1:]
+def lay_out(S, ff, width, out, value, groups, gate_up, down, after_attn, ffn_out):
+    wrows, span = value.shape[1:]
+    tokens = after_attn.shape[0]
     wcols = width // 4
     pair = 2 * wcols
     skip = wcols - (span - 128)
@@ -1589,13 +1609,14 @@
     fcols = gate_up.shape[3] // 2
     B = fcols // pad
     drows = ff // S
-    steps = 9 if wrows % 144 == 0 else 1
+    steps = 3 if wrows % (3 * 16) == 0 else 1
     rows, cols = wrows // steps, width // steps
 
     def kernel(o_in, v_in, *refs):
-        g_in, (gu_in, d_in, o_out, q_out, k_out, v_out, g_out, u_out, d_out) = split_refs(
-            refs, len(groups), 9
-        )
+        g_in, ins, outs = split_refs(refs, len(groups), 4, 8)
+        gu_in, d_in, after_in, f_in = ins
+        o_out, q_out, k_out, v_out, g_out, u_out, d_out, r_out = outs
+        r_out[...] = (after_in[...] + branch_scale * f_in[...].astype(f32)).astype(bf)
 
         def beside(pieces, to):
             for side in range(2):
@@ -1606,7 +1627,7 @@
                 to[:, side * pair : (side + 1) * pair] = jnp.concatenate(parts, axis=1)
 
         half = groups[0].shape[2] // 2
-        beside([(o_in, 0, wcols)], o_out)
+        beside([(o_in, 0, wcols - skip), (v_in, 0, skip)], o_out)
         beside([(v_in, skip, wcols)], v_out)
         beside([(ref, 0, half) for ref in g_in], q_out)
         beside([(ref, half, half) for ref in g_in], k_out)
@@ -1629,13 +1650,15 @@
     return pl.pallas_call(
         kernel,
         grid=(steps,),
-        out_shape=outs + [shape(drows, width, dtype=f32)],
+        out_shape=outs + [shape(drows, width, dtype=f32), shape(tokens, width)],
         in_specs=[by_rows(v) for v in (out, value, *groups, gate_up)]
-        + [pl.BlockSpec((4, pad, cols), lambda i: (0, 0, i))],
-        out_specs=[by_rows(v) for v in outs] + [pl.BlockSpec((drows, cols), lambda i: (0, i))],
+        + [pl.BlockSpec((4, pad, cols), lambda i: (0, 0, i))]
+        + [pl.BlockSpec((tokens, cols), lambda i: (0, i))] * 2,
+        out_specs=[by_rows(v) for v in outs]
+        + [pl.BlockSpec((n, cols), lambda i: (0, i)) for n in (drows, tokens)],
         name="lay_out",
         compiler_params=pltpu.CompilerParams(vmem_limit_bytes=60 * 2**20),
-    )(out, value, *groups, gate_up, down)
+    )(out, value, *groups, gate_up, down, after_attn, ffn_out)
 
 
 def product(left_side, right_side):
@@ -1675,7 +1698,7 @@
     rows, width = tokens.shape
     ff = w_gate.shape[1]
     wrows = width // S
-    ids = (seq_ids[None, :], seq_ids[:, None], block_ids[None, :], block_ids[:, None])
+    ids = (seq_ids[None, :], block_ids[None, :])
     gains = jnp.pad(jnp.stack([attn_gain, ffn_gain]), ((0, 6), (0, 0)))
     (
         w4, gains, tokens_group, d_down, gate_up, down_w, qkv, mixed_all, after_attn, normed_two,
@@ -1691,12 +1714,11 @@
         B, S, d_n2, after_attn, cotangent, gains, w4.reshape(width, width), qkv, tokens_group,
         [lefts[0], mixed_far, lefts[1], normed_far], tables, ids, g_gate_up, g_down,
     )
-    g_out, g_query, g_key, g_value, g_gate, g_up, g_down = lay_out(
-        S, ff, width, g_out, g_value, parts[:-3], *parts[-2:]
+    g_out, g_query, g_key, g_value, g_gate, g_up, g_down, result = lay_out(
+        S, ff, width, g_out, g_value, parts[:-3], *parts[-2:], after_attn, ffn_out
     )
-    result = after_attn + branch_scale * ffn_out.astype(f32)
     return (
-        result.astype(bf), grad_tokens, gain_sums[0, :wrows], g_query, g_key, g_value, g_out,
+        result, grad_tokens, gain_sums[0, :wrows], g_query, g_key, g_value, g_out,
         gain_sums[1, :wrows], g_gate, g_up, g_down,
     )
 

time: 583 us -> 561 us (0.962)
  Pallas kernels: 569 us -> 552 us
    pallas_call x3, Pallas kernels: 551 us -> 536 us  [call(): pl.pallas_call(kernel, out_shape=outs, in_specs=in_specs, out_specs=out_s...]
where the time goes in v6:
time: 561 us; the launch traced here: 557 us
  Pallas kernels  552 us (98%)
    pallas_call x3, Pallas kernels, call(): pl.pallas_call(kernel, out_shape=outs, in_specs=in_specs, out_specs=out_s...  536 us
    pallas_call x1, Pallas kernels, lay_out(): pl.pallas_call(kernel, grid=(steps,), out_shape=outs + [shape(drows, widt...  15.9 us

profile of v6, /device:TPU:9, one launch (start us, length us, event | category | flops | bytes accessed | tf_op | source)
XLA Modules:
  0.0 556.6 jit_solution(7761866724945861085)
XLA Ops:
  0.6 0.7 stack.9
  1.3 0.7 stack.10
  2.0 0.6 fusion.2.refs_7_
  2.6 199.2 %attention_forward.1 = (bf16[4,2,288,2304]{3,2,1,0:T(8,128)(2,1)}, f32[8,2304]{1,0:T(8,128)}, bf16[4,128,2304]{2,1,0:T(8,128)(2,1)}, bf16[2,4,2,128,2304]{4,3,2,...) custom-call(bf16[288,2304]{1,0:T(8,128)(2,1)} %refs_0_.1, ...), custom_call_target="tpu_custom_call" | custom-call | tf_op jit(solution)/shard_map/attention_forward/pallas_call | solution.py:453
  201.8 178.5 %feed_forward.1 = (bf16[128,2304]{1,0:T(8,128)(2,1)}, bf16[128,2304]{1,0:T(8,128)(2,1)}, bf16[4,288,768]{2,1,0:T(8,128)(2,1)}, bf16[192,2304]{1,0:T(8,128)(2,1)}...) custom-call(bf16[128,2304]{1,0:T(8,128)(2,1)} %get-tuple-element.46.n_in, ...), custom_call_target="tpu_custom_call" | custom-call | tf_op jit(solution)/shard_map/feed_forward/pallas_call | solution.py:453
  380.4 158.0 %attention_backward.1 = (bf16[128,2304]{1,0:T(8,128)(2,1)}, f32[8,384]{1,0:T(8,128)}, bf16[4,288,512]{2,1,0:T(8,128)(2,1)}, bf16[4,288,640]{2,1,0:T(8,128)(2,1)}...) custom-call(bf16[128,2304]{1,0:T(8,128)(2,1)} %get-tuple-element.52., ...), custom_call_target="tpu_custom_call" | custom-call | tf_op jit(solution)/shard_map/attention_backward/pallas_call | solution.py:453
  538.4 1.4 slice_reduce_fusion
  539.7 0.0 copy-start
  539.7 15.9 %lay_out.1 = (f32[288,2304]{1,0:T(8,128)}, f32[288,2304]{1,0:T(8,128)}, f32[288,2304]{1,0:T(8,128)}, f32[288,2304]{1,0:T(8,128)}, f32[288,5760]{1,0:T(8,128)}, /...) custom-call(bf16[4,288,512]{2,1,0:T(8,128)(2,1)} %get-tuple-element.63.o_in, ...), custom_call_target="tpu_custom_call" | custom-call | tf_op jit(solution)/shard_map/lay_out/pallas_call | solution.py:1650
  555.6 0.0 copy-done
  555.6 0.8 copy.25
Async XLA Ops:
  539.7 15.9 %copy-start = (bf16[128,2304]{1,0:T(8,128)(2,1)S(1)}, bf16[128,2304]{1,0:T(8,128)(2,1)}, u32[]{:S(2)}) copy-start(bf16[128,2304]{1,0:T(8,128)(2,1)} %get-tuple-element.95) | copy-start | bytes 1769476

commit v7 on v6

--- a/solution.py
+++ b/solution.py
@@ -47,36 +47,18 @@
         return (self.s, self.rc)
 
 
-def greet(place, a_peers=True, b_peers=False, r_peers=True, everyone=None):
+def greet(place, a_peers=True, b_peers=False, r_peers=True):
     barrier = pltpu.get_barrier_semaphore()
-
-    def signal(device):
+    devices = []
+    if a_peers:
+        devices += [place.line((place.a + k) % A) for k in range(1, A)]
+    if b_peers:
+        devices += [place.side((place.b + k) % place.B) for k in range(1, place.B)]
+    if r_peers:
+        devices += [(place.s, (place.r + k) % 4) for k in range(1, 4)]
+    for device in devices:
         pl.semaphore_signal(barrier, inc=1, device_id=device, device_id_type=MESH)
-
-    if everyone is not None:
-        S, R = everyone
-
-        def one(k, carry):
-            signal((lax.rem(place.s + k // R, S), lax.rem(place.r + k % R, R)))
-            return carry
-
-        lax.fori_loop(1, S * R, one, 0)
-        pl.semaphore_wait(barrier, S * R - 1)
-        return
-    count = 0
-    if a_peers:
-        for k in range(1, A):
-            signal(place.line((place.a + k) % A))
-            count += 1
-    if b_peers:
-        for k in range(1, place.B):
-            signal(place.side((place.b + k) % place.B))
-            count += 1
-    if r_peers:
-        for k in range(1, 4):
-            signal((place.s, (place.r + k) % 4))
-            count += 1
-    pl.semaphore_wait(barrier, count)
+    return lambda: pl.semaphore_wait(barrier, len(devices))
 
 
 def remote(src, dst, send, recv, device):
@@ -527,15 +509,16 @@
     score_scale = 1.0 / math.sqrt(head_dim)
 
     def kernel(*refs):
-        w_in, g_in, ins, outs, scratch, refs = split_refs(refs, 4, 2, 6, 12, 18, 100)
+        w_in, g_in, ins, outs, scratch, refs = split_refs(refs, 4, 2, 6, 12, 19, 100)
         wd_in, gain_in, tok_in, cot_in, seq_row, blk_row = ins
         (w4_out, gain_out, tok_out, d_out, gu_out, dn_out, qkv_out, mixed_out, after_out,
-         n2_out, table_out, normed_t) = outs
+         n2_out, table_out, nt_out) = outs
         (w_all, g_all, wd_all, own4, gu_own, dn_own, own_gain, gain_all, tok_all, d_own, w4_all,
-         normed, raw, bias, mixed, proj, proj_all, load) = scratch
+         normed, normed_t, raw, bias, mixed, proj, proj_all, load) = scratch
         s1, s2, s3, s4, s5, s6, s7 = split_refs(refs, 4, 4, 3, 6, 3, 2, 100)
         qkv, mix_x, mix_core, ex_sem, save = s7
         place = Place(B)
+        met = greet(place, True, True, True)
         r, x, c = place.r, place.x, place.c
         loads = [pltpu.make_async_copy(w, w_all.at[i], load.at[i]) for i, w in enumerate(w_in)]
         loads += [
@@ -560,7 +543,7 @@
                 gain_in[...], select(wrows, wide, 0, place.s * wrows - k * wide, wrows),
                 preferred_element_type=f32,
             )
-        greet(place, True, True, True)
+        met()
 
         def prepare():
             for i in range(2):
@@ -619,6 +602,15 @@
                 at = slice(i * rows, (i + 1) * rows)
                 normed[at, :] = value.astype(bf)
                 normed_t[:, at] = value.T.astype(bf)
+            early = [
+                pltpu.make_async_copy(normed_t, nt_out, load.at[1]),
+                pltpu.make_async_copy(tok_all, tok_out, load.at[2]),
+            ]
+            for copy in early:
+                copy.start()
+            yield
+            for copy in early:
+                copy.wait()
 
         def share_piece(k):
             at = pl.ds(k * trio * head_dim, trio * head_dim)
@@ -750,9 +742,6 @@
             (0, 1, 2, 3, 1, 1, 1, 2, 2, 2, 2, 2, 3, 3) + (0,) * (2 * parts) + (4,)
             + (0,) * parts + (4, 4, 0, 6, 5, 7, 4, 7, 7, 7, 5, 4, 7, 4, 5, 7, 5, 4, 4, 7, 6, 5, 4),
         )
-        saved = pltpu.make_async_copy(tok_all, tok_out, save.at[1])
-        saved.start()
-        saved.wait()
         pltpu.make_async_copy(w4_all, w4_out, save.at[2]).wait()
 
     block = (rows, width)
@@ -764,7 +753,7 @@
             shape(3 * wcols, group), shape(4, wcols, group), shape(*block, dtype=f32),
             shape(*block), shape(2, head_dim // 2, group, dtype=f32), shape(width, group),
         ],
-        [ANY, VMEM, ANY, ANY, ANY, ANY, ANY, ANY, VMEM, VMEM, VMEM, VMEM],
+        [ANY, VMEM, ANY, ANY, ANY, ANY, ANY, ANY, VMEM, VMEM, VMEM, ANY],
         [
             pltpu.VMEM((4, wrows, width), bf), pltpu.VMEM((2, wrows, ff), bf),
             pltpu.VMEM(w_down.shape, bf), pltpu.VMEM((wrows, 4 * wcols), bf),
@@ -772,6 +761,7 @@
             pltpu.VMEM((8, width), f32), pltpu.VMEM((A, B, 8, width), f32),
             pltpu.VMEM((4,) + block, bf), pltpu.VMEM(block, bf),
             pltpu.VMEM((A, B, wrows, 4 * wcols), bf), pltpu.VMEM((group, width), bf),
+            pltpu.VMEM((width, group), bf),
             pltpu.VMEM((width - span + 128, group), f32), pltpu.VMEM((group, group), f32),
             pltpu.VMEM((4, wcols, group), bf), pltpu.VMEM((4, rows, span), bf),
             pltpu.VMEM((4, rows, span), bf), DMA((7,)),
@@ -799,13 +789,14 @@
     wrows = gate_up.shape[0] // (A * B)
     pad = fcols // B
     many = 1152
+    most = rows * 3 // 4
 
     def kernel(n_in, d_in, gu_in, dn_in, *refs):
         lefts_in, (out, f_out, ggu_out, gd_out), lefts_out, refs = split_refs(refs, 2, 4, 2, 100)
         bufs, (line_recv, line_send, over_x, over_core), sems = split_refs(refs, 11, 4, 100)
         n_all, d_all, gu, dn, part, hid, d_gu, from_core, from_x, landed, g_all = bufs
         (g_down, load, core_sem, x_sem, line_sem, gu_side, gd_side, gu_sem, gd_sem, f_core, f_x,
-         free, core_free, f_line, left_sem) = sems
+         free, core_free, f_line, left_sem, rest_send, rest_recv) = sems
         place = Place(B)
         a, x, c = place.a, place.x, place.c
         loads = [
@@ -816,7 +807,7 @@
         ]
         for copy in loads:
             copy.start()
-        greet(place, True, True, True)
+        greet(place, True, True, True)()
 
         def to_line(block, way):
             src = n_all.at[x, block, c]
@@ -825,9 +816,18 @@
                 place.line(a + way),
             )
 
-        def to_x(block):
+        def to_x(block, some=True):
             src = n_all.at[x, block, c]
+            if some:
+                src = src.at[pl.ds(0, most)]
             return remote(src, src, over_x.at[block, 0], over_x.at[block, 1], place.over_x)
+
+        def rest_to_line(block, way):
+            src = n_all.at[1 - x, block, c, pl.ds(most, rows - most)]
+            return remote(
+                src, src, rest_send.at[block, (1 - way) // 2], rest_recv.at[block],
+                place.line(a + way),
+            )
 
         def to_core(side, block):
             src = n_all.at[side, block, c]
@@ -868,7 +868,7 @@
         def _():
             to_line(a, -1).start()
 
-        to_x(a).start()
+        to_x(a, False).start()
         to_core(x, a).start()
 
         def left_aside(i, d, k):
@@ -932,7 +932,25 @@
 
             @pl.when(jnp.logical_not(near))
             def _():
-                to_x(block).wait_recv()
+                @pl.when(block == a)
+                def _():
+                    to_x(block, False).wait_recv()
+                    for way in (1, -1):
+                        @pl.when((a + way >= 0) & (a + way < A))
+                        def _():
+                            rest_to_line(block, way).start()
+
+                @pl.when(block != a)
+                def _():
+                    way = jnp.where(block < a, 1, -1)
+                    rest_to_line(block, way).wait_recv()
+
+                    @pl.when((a + way >= 0) & (a + way < A))
+                    def _():
+                        rest_to_line(block, way).start()
+
+                    to_x(block).wait_recv()
+
                 to_core(1 - x, block).start()
 
             to_core(side, block).wait_recv()
@@ -1069,7 +1087,14 @@
                     aside(d, j).start()
             next(chain)
         for d in range(A):
-            to_x(d).wait_send()
+            @pl.when(d == a)
+            def _():
+                to_x(d, False).wait_send()
+
+            @pl.when(d != a)
+            def _():
+                to_x(d).wait_send()
+
             for side in range(X):
                 to_core(side, d).wait_send()
                 for h in range(parts):
@@ -1078,10 +1103,12 @@
             @pl.when((a < A - 1) & (d <= a))
             def _():
                 to_line(d, 1).wait_send()
+                rest_to_line(d, 1).wait_send()
 
             @pl.when((a > 0) & (d >= a))
             def _():
                 to_line(d, -1).wait_send()
+                rest_to_line(d, -1).wait_send()
 
         for device in [place.over_x] + [place.line((a + k) % A) for k in range(1, A)]:
             pl.semaphore_signal(free, inc=1, device_id=device, device_id_type=MESH)
@@ -1144,7 +1171,7 @@
             pltpu.VMEM((B - 1, A, wrows, 2 * fcols), bf), pltpu.VMEM((B - 1, pad, width), bf),
             DMA((B, A, 2)), DMA((B, 2)), DMA((X, A, 2)), DMA((A, 2)), pltpu.SemaphoreType.REGULAR,
             pltpu.SemaphoreType.REGULAR,
-            DMA((2, A, 1, 2)), DMA((2, B, A, 2)),
+            DMA((2, A, 1, 2)), DMA((2, B, A, 2)), DMA((A, 2)), DMA((A,)),
         ],
         [normed_two, d_down, gate_up, down, *lefts],
         [ANY] * 6,
@@ -1305,6 +1332,7 @@
             refs, 5, 5, 2, 3, 3, 2, *(6,) * count
         )
         place = Place(B)
+        met = greet(place, True, True, True)
         r, x, c = place.r, place.x, place.c
         loads = [
             pltpu.make_async_copy(src, dst, load.at[i])
@@ -1344,7 +1372,7 @@
                 d_proj[:, at : at + span], select(span, span, k * wcols - at, 0, wcols)
             ).astype(bf)
         ex_all[r] = ex_send[r]
-        greet(place, True, True, True)
+        met()
         exchange = []
         for k in (2, 3, 1):
             to = (r + k) % 4

time: 561 us -> 557 us (level)
  Pallas kernels: 552 us -> 546 us
where the time goes in v7:
time: 557 us; the launch traced here: 551 us
  Pallas kernels  546 us (98%)
    pallas_call x3, Pallas kernels, call(): pl.pallas_call(kernel, out_shape=outs, in_specs=in_specs, out_specs=out_s...  530 us
    pallas_call x1, Pallas kernels, lay_out(): pl.pallas_call(kernel, grid=(steps,), out_shape=outs + [shape(drows, widt...  15.9 us

profile of v7, /device:TPU:9, one launch (start us, length us, event | category | flops | bytes accessed | tf_op | source)
XLA Modules:
  0.0 551.3 jit_solution(5466023603256148889)
XLA Ops:
  0.6 0.7 stack.9
  1.3 0.7 stack.10
  2.0 0.6 fusion.2.refs_7_
  2.6 196.8 %attention_forward.1 = (bf16[4,2,288,2304]{3,2,1,0:T(8,128)(2,1)}, f32[8,2304]{1,0:T(8,128)}, bf16[4,128,2304]{2,1,0:T(8,128)(2,1)}, bf16[2,4,2,128,2304]{4,3,2,...) custom-call(bf16[288,2304]{1,0:T(8,128)(2,1)} %refs_0_.1, ...), custom_call_target="tpu_custom_call" | custom-call | tf_op jit(solution)/shard_map/attention_forward/pallas_call | solution.py:435
  199.4 177.2 %feed_forward.1 = (bf16[128,2304]{1,0:T(8,128)(2,1)}, bf16[128,2304]{1,0:T(8,128)(2,1)}, bf16[4,288,768]{2,1,0:T(8,128)(2,1)}, bf16[192,2304]{1,0:T(8,128)(2,1)}...) custom-call(bf16[128,2304]{1,0:T(8,128)(2,1)} %get-tuple-element.46.n_in, ...), custom_call_target="tpu_custom_call" | custom-call | tf_op jit(solution)/shard_map/feed_forward/pallas_call | solution.py:435
  376.6 156.4 %attention_backward.1 = (bf16[128,2304]{1,0:T(8,128)(2,1)}, f32[8,384]{1,0:T(8,128)}, bf16[4,288,512]{2,1,0:T(8,128)(2,1)}, bf16[4,288,640]{2,1,0:T(8,128)(2,1)}...) custom-call(bf16[128,2304]{1,0:T(8,128)(2,1)} %get-tuple-element.52., ...), custom_call_target="tpu_custom_call" | custom-call | tf_op jit(solution)/shard_map/attention_backward/pallas_call | solution.py:435
  533.0 1.4 slice_reduce_fusion
  534.4 0.0 copy-start
  534.4 15.9 %lay_out.1 = (f32[288,2304]{1,0:T(8,128)}, f32[288,2304]{1,0:T(8,128)}, f32[288,2304]{1,0:T(8,128)}, f32[288,2304]{1,0:T(8,128)}, f32[288,5760]{1,0:T(8,128)}, /...) custom-call(bf16[4,288,512]{2,1,0:T(8,128)(2,1)} %get-tuple-element.63.o_in, ...), custom_call_target="tpu_custom_call" | custom-call | tf_op jit(solution)/shard_map/lay_out/pallas_call | solution.py:1678
  550.3 0.0 copy-done
  550.3 0.8 copy.25
Async XLA Ops:
  534.4 15.9 %copy-start = (bf16[128,2304]{1,0:T(8,128)(2,1)S(1)}, bf16[128,2304]{1,0:T(8,128)(2,1)}, u32[]{:S(2)}) copy-start(bf16[128,2304]{1,0:T(8,128)(2,1)} %get-tuple-element.95) | copy-start | bytes 1769476

commit v8 on v7

--- a/solution.py
+++ b/solution.py
@@ -1637,7 +1637,7 @@
     fcols = gate_up.shape[3] // 2
     B = fcols // pad
     drows = ff // S
-    steps = 3 if wrows % (3 * 16) == 0 else 1
+    steps = 2 if wrows % (2 * 16) == 0 else 1
     rows, cols = wrows // steps, width // steps
 
     def kernel(o_in, v_in, *refs):

time: 557 us -> 557 us (level)
  no operation moved by 1% of the time
where the time goes in v8:
time: 557 us; the launch traced here: 552 us
  Pallas kernels  547 us (98%)
    pallas_call x3, Pallas kernels, call(): pl.pallas_call(kernel, out_shape=outs, in_specs=in_specs, out_specs=out_s...  531 us
    pallas_call x1, Pallas kernels, lay_out(): pl.pallas_call(kernel, grid=(steps,), out_shape=outs + [shape(drows, widt...  15.4 us

profile of v8, /device:TPU:9, one launch (start us, length us, event | category | flops | bytes accessed | tf_op | source)
XLA Modules:
  0.0 552.0 jit_solution(12205622489887444198)
XLA Ops:
  0.6 0.7 stack.9
  1.3 0.7 stack.10
  2.0 0.6 fusion.2.refs_7_
  2.6 197.1 %attention_forward.1 = (bf16[4,2,288,2304]{3,2,1,0:T(8,128)(2,1)}, f32[8,2304]{1,0:T(8,128)}, bf16[4,128,2304]{2,1,0:T(8,128)(2,1)}, bf16[2,4,2,128,2304]{4,3,2,...) custom-call(bf16[288,2304]{1,0:T(8,128)(2,1)} %refs_0_.1, ...), custom_call_target="tpu_custom_call" | custom-call | tf_op jit(solution)/shard_map/attention_forward/pallas_call | solution.py:435
  199.7 177.0 %feed_forward.1 = (bf16[128,2304]{1,0:T(8,128)(2,1)}, bf16[128,2304]{1,0:T(8,128)(2,1)}, bf16[4,288,768]{2,1,0:T(8,128)(2,1)}, bf16[192,2304]{1,0:T(8,128)(2,1)}...) custom-call(bf16[128,2304]{1,0:T(8,128)(2,1)} %get-tuple-element.46.n_in, ...), custom_call_target="tpu_custom_call" | custom-call | tf_op jit(solution)/shard_map/feed_forward/pallas_call | solution.py:435
  376.7 157.2 %attention_backward.1 = (bf16[128,2304]{1,0:T(8,128)(2,1)}, f32[8,384]{1,0:T(8,128)}, bf16[4,288,512]{2,1,0:T(8,128)(2,1)}, bf16[4,288,640]{2,1,0:T(8,128)(2,1)}...) custom-call(bf16[128,2304]{1,0:T(8,128)(2,1)} %get-tuple-element.52., ...), custom_call_target="tpu_custom_call" | custom-call | tf_op jit(solution)/shard_map/attention_backward/pallas_call | solution.py:435
  534.0 1.4 slice_reduce_fusion
  535.4 0.0 copy-start
  535.4 15.4 %lay_out.1 = (f32[288,2304]{1,0:T(8,128)}, f32[288,2304]{1,0:T(8,128)}, f32[288,2304]{1,0:T(8,128)}, f32[288,2304]{1,0:T(8,128)}, f32[288,5760]{1,0:T(8,128)}, /...) custom-call(bf16[4,288,512]{2,1,0:T(8,128)(2,1)} %get-tuple-element.63.o_in, ...), custom_call_target="tpu_custom_call" | custom-call | tf_op jit(solution)/shard_map/lay_out/pallas_call | solution.py:1678
  550.7 0.0 copy-done
  550.8 0.8 copy.25
Async XLA Ops:
  535.4 15.4 %copy-start = (bf16[128,2304]{1,0:T(8,128)(2,1)S(1)}, bf16[128,2304]{1,0:T(8,128)(2,1)}, u32[]{:S(2)}) copy-start(bf16[128,2304]{1,0:T(8,128)(2,1)} %get-tuple-element.95) | copy-start | bytes 1769476
